TPU v7x, 32 devices: a whole 2x2x4 slice. The times are simulated.
32 devices in a mesh: groups: 2 (over y), gx: 8 (over z, x), gy: 2 (over core).
Axes of the slice: x: 2, y: 2, z: 4, core: 2. Of those that a mesh axis runs over, the one named last changes fastest.
Arguments:
- x_in: bfloat16 [256, 4672], P(('groups', 'gx'), 'gy'), parts along dimension 0, may hold values from -6 to 6
- lengths: int32 [256], P(('groups', 'gy')), parts along dimension 0, may hold values from 32 to 128, as said below
- self_gain: float32 [4672], P('gy'), may hold values from 0.1 to 1.9
- cross_gain: float32 [4672], P('gy'), may hold values from 0.1 to 1.9
- ffn_gain: float32 [4672], P('gy'), may hold values from 0.1 to 1.9
- final_gain: float32 [4672], P('gy'), may hold values from 0.1 to 1.9
- self_query: bfloat16 [4672, 4096], P('gy', 'gx'), may hold values from -0.01171875 to 0.01171875
- self_kv: bfloat16 [4672, 64, 128], P('gy', 'gx'), may hold values from -0.09375 to 0.09375
- self_out: bfloat16 [4096, 4672], P('gx', 'gy'), may hold values from -0.09375 to 0.09375
- cross_query: bfloat16 [4672, 4096], P('gy', 'gx'), may hold values from -0.01171875 to 0.01171875
- cross_out: bfloat16 [4096, 4672], P('gx', 'gy'), may hold values from -0.09375 to 0.09375
- ffn_gate: bfloat16 [4672, 12352], P('gy', 'gx'), may hold values from -0.09375 to 0.09375
- ffn_up: bfloat16 [4672, 12352], P('gy', 'gx'), may hold values from -0.09375 to 0.09375
- ffn_down: bfloat16 [12352, 4672], P('gx', 'gy'), may hold values from -0.0546875 to 0.0546875
- self_keys: bfloat16 [64, 256, 64, 128], P('gx', ('groups', 'gy')), parts along dimension 1, may hold values from -1500 to 1500
- self_values: bfloat16 [64, 256, 64, 128], P('gx', ('groups', 'gy')), parts along dimension 1, may hold values from -6 to 6
- cross_keys: bfloat16 [64, 256, 64, 128], P('gx', ('groups', 'gy')), parts along dimension 1, may hold values from -1500 to 1500
- cross_values: bfloat16 [64, 256, 64, 128], P('gx', ('groups', 'gy')), parts along dimension 1, may hold values from -6 to 6
Outputs:
- decoded: bfloat16 [256, 4672], P(('groups', 'gx'), 'gy'), parts along dimension 0
There are 2 independent parts, one for each index of `groups`. A program takes and returns all parts, laid end to end along the dimension named above; an argument that names none is the same for every part. Nothing has to cross between parts.
Inputs may be any that keep to these rules, and one draw needn't show every extreme that they name: lengths[b] counts the filled slots of row b's self-attention cache, slots 0 to lengths[b] - 1; in every draw some row fills all 128 slots.
All inputs are finite; a program needn't handle non-finite values.
Results may differ from a plain program's by a relative error of at most 0.02.
The roundings to bfloat16 on the way count: a program that leaves them out, or rounds other values in their place, can miss the bound.
Values may be sent and summed in bfloat16 or wider, within the bound.
No kernel may reach another device: no remote copies, remote signals or barrier semaphores. Data moves between devices by JAX's collectives and lax.ppermute only.
A program may use at most 192 MiB of HBM per device.

v0:
```python
import jax
import jax.numpy as jnp
from jax import lax
from jax.sharding import PartitionSpec as P

D = 4672
DK = 64


def self_attend(query, new_key, new_value, cache_keys, cache_values, lengths):
    scores = jnp.einsum("bhd,hbds->hbs", query, cache_keys, preferred_element_type=jnp.float32)
    own_score = jnp.einsum("bhd,bhd->hb", query, new_key, preferred_element_type=jnp.float32)
    slots = lax.broadcasted_iota(jnp.int32, (1, scores.shape[1], scores.shape[2]), 2)
    valid_slots = slots < lengths[None, :, None]
    scores = jnp.where(valid_slots, scores, -1e30)
    top_score = jnp.maximum(jnp.max(scores, axis=2), own_score)
    expo = jnp.where(valid_slots, jnp.exp(scores - top_score[:, :, None]), 0.0)
    own_expo = jnp.exp(own_score - top_score)
    totals = jnp.sum(expo, axis=2) + own_expo
    attn_probs = (expo / totals[:, :, None]).astype(jnp.bfloat16)
    own_prob = (own_expo / totals).astype(jnp.bfloat16)
    mixed = jnp.einsum(
        "hbs,hbds->bhd", attn_probs, cache_values, preferred_element_type=jnp.float32
    )
    mixed = mixed + own_prob.T.astype(jnp.float32)[:, :, None] * new_value.astype(jnp.float32)
    return mixed.astype(jnp.bfloat16).reshape(query.shape[0], query.shape[1] * query.shape[2])


def cross_attend(query, cache_keys, cache_values):
    scores = jnp.einsum("bhd,hbds->hbs", query, cache_keys, preferred_element_type=jnp.float32)
    top_score = jnp.max(scores, axis=2)
    expo = jnp.exp(scores - top_score[:, :, None])
    totals = jnp.sum(expo, axis=2)
    attn_probs = (expo / totals[:, :, None]).astype(jnp.bfloat16)
    mixed = jnp.einsum(
        "hbs,hbds->bhd", attn_probs, cache_values, preferred_element_type=jnp.float32
    )
    return mixed.astype(jnp.bfloat16).reshape(query.shape[0], query.shape[1] * query.shape[2])


def normalize(stream, gain):
    stream_f = stream.astype(jnp.float32)
    squares = lax.psum(jnp.sum(stream_f * stream_f, axis=1), "gy")
    inverse = lax.rsqrt(squares / D + 1e-06)
    return (stream_f * inverse[:, None] * gain[None, :]).astype(jnp.bfloat16)


def widen(stream):
    return lax.all_gather(stream, "gx", axis=0, tiled=True)


def accumulate(stream, left, weight):
    summed = lax.psum_scatter(
        jnp.dot(left, weight, preferred_element_type=jnp.float32),
        "gx",
        scatter_dimension=0,
        tiled=True,
    )
    return (stream.astype(jnp.float32) + summed).astype(jnp.bfloat16)


def project_heads(stream, heads_local, weight):
    gathered = lax.all_gather(heads_local, "gy", axis=0, tiled=True)
    return accumulate(stream, gathered, weight)


def per_device(
    x_in,
    lengths,
    self_gain,
    cross_gain,
    ffn_gain,
    final_gain,
    self_query,
    self_kv,
    self_out,
    cross_query,
    cross_out,
    ffn_gate,
    ffn_up,
    ffn_down,
    self_keys,
    self_values,
    cross_keys,
    cross_values,
):
    width_local = x_in.shape[1]
    heads_here = self_query.shape[1] // DK
    rows_here = self_keys.shape[1]
    stream = x_in
    normed = normalize(widen(stream), self_gain)
    query_part = jnp.dot(normed, self_query, preferred_element_type=jnp.float32)
    pair_part = jnp.dot(
        normed,
        self_kv.reshape(width_local, heads_here * 2 * DK),
        preferred_element_type=jnp.float32,
    )
    query_rows, pair_rows = (
        lax.psum_scatter(query_part, "gy", scatter_dimension=0, tiled=True),
        lax.psum_scatter(pair_part, "gy", scatter_dimension=0, tiled=True),
    )
    query = query_rows.astype(jnp.bfloat16).reshape(rows_here, heads_here, DK)
    new_pair = pair_rows.astype(jnp.bfloat16).reshape(rows_here, heads_here, 2 * DK)
    heads_local = self_attend(
        query, new_pair[:, :, :DK], new_pair[:, :, DK:], self_keys, self_values, lengths
    )
    stream = project_heads(stream, heads_local, self_out)
    normed = normalize(widen(stream), cross_gain)
    query_part = jnp.dot(normed, cross_query, preferred_element_type=jnp.float32)
    query_rows = lax.psum_scatter(query_part, "gy", scatter_dimension=0, tiled=True)
    query = query_rows.astype(jnp.bfloat16).reshape(rows_here, heads_here, DK)
    heads_local = cross_attend(query, cross_keys, cross_values)
    stream = project_heads(stream, heads_local, cross_out)
    normed = normalize(widen(stream), ffn_gain)
    gate_sum, up_sum = (
        lax.psum(
            jnp.dot(normed, ffn_gate, preferred_element_type=jnp.float32).astype(jnp.bfloat16), "gy"
        ).astype(jnp.float32),
        lax.psum(
            jnp.dot(normed, ffn_up, preferred_element_type=jnp.float32).astype(jnp.bfloat16), "gy"
        ).astype(jnp.float32),
    )
    hidden = (jax.nn.gelu(gate_sum, approximate=True) * up_sum).astype(jnp.bfloat16)
    stream = accumulate(stream, hidden, ffn_down)
    return normalize(stream, final_gain)


def solution(mesh):
    return jax.shard_map(
        per_device,
        mesh=mesh,
        in_specs=(
            P(("groups", "gx"), "gy"),
            P(("groups", "gy")),
            P("gy"),
            P("gy"),
            P("gy"),
            P("gy"),
            P("gy", "gx"),
            P("gy", "gx", None),
            P("gx", "gy"),
            P("gy", "gx"),
            P("gx", "gy"),
            P("gy", "gx"),
            P("gy", "gx"),
            P("gx", "gy"),
            P("gx", ("groups", "gy"), None, None),
            P("gx", ("groups", "gy"), None, None),
            P("gx", ("groups", "gy"), None, None),
            P("gx", ("groups", "gy"), None, None),
        ),
        out_specs=P(("groups", "gx"), "gy"),
        check_vma=False,
    )
```

profile of v0, /device:TPU:0, one launch (start us, length us, event | category | flops | bytes accessed | tf_op | source)
XLA Modules:
  0.0 425.3 jit_solution(14525222655755831522)
XLA Ops:
  6.5 33.6 %all_gather.15 = bf16[128,2336]{1,0:T(8,128)(2,1)S(1)} all-gather(bf16[16,2336]{1,0:T(8,128)(2,1)} %param.18), channel_id=1, replica_groups=mesh['groups'=2,'gx'=8,'gy'=2] {'gx'}, dimensions={0}, use_global_device_ids=true | all-gather | bytes 672768 | tf_op jit(solution)/shard_map/all_gather | solution.py:49
  40.2 0.2 fusion.9
  40.4 2.5 psum.42
  42.8 3.0 fusion.51
  45.9 4.1 fusion.6
  50.1 4.6 %reduce-scatter.7.cloned.1.call-done = f32[64,512]{1,0:T(8,128)} async-done(((f32[128,512]{1,0:T(8,128)}), f32[64,512]{1,0:T(8,128)}) %reduce-scatter.7.cloned.1.call-update) | async-done | bytes 131088 | tf_op jit(solution)/shard_map/reduce_scatter | solution.py:99
  54.8 0.9 convert_element_type.91
  55.8 0.1 reshape.49
  56.0 5.6 %fusion.45 = f32[8,64,1,128]{3,2,1,0:T(1,128)S(1)} fusion(bf16[8,64,64,128]{3,2,1,0:T(8,128)(2,1)} %param.32, bf16[64,8,64,1]{2,1,0,3:T(8,128)(2,1)S(1)} %reshape.55), kind=kOutput, calls=%fused_computation.56 | convolution fusion | flops 8388608 | bytes 8716288 | tf_op jit(solution)/shard_map/bhd,hbds->hbs/dot_general | solution.py:11
  61.6 0.2 select_reduce_fusion
  61.8 4.5 %reduce-scatter.9.cloned.1.call-done = f32[64,1024]{1,0:T(8,128)} async-done(((f32[128,1024]{1,0:T(8,128)}), f32[64,1024]{1,0:T(8,128)}) %reduce-scatter.9.cloned.1.call-update) | async-done | bytes 262160 | tf_op jit(solution)/shard_map/reduce_scatter | solution.py:100
  66.2 1.0 convert_bitcast_fusion
  67.2 0.1 fusion.40
  67.4 0.3 fusion.47
  67.8 0.2 fusion.56
  68.1 7.8 %fusion.4 = f32[64,8,1,64]{3,2,1,0:T(1,128)S(1)} fusion(bf16[8,64,64,128]{3,2,1,0:T(8,128)(2,1)} %param.33, bf16[8,64,128,1]{2,1,0,3:T(8,128)(2,1)S(1)} %fusion.56), kind=kOutput, calls=%fused_computation.4 | convolution fusion | flops 8388608 | bytes 8650752 | tf_op jit(solution)/shard_map/hbs,hbds->bhd/dot_general | solution.py:22
  75.8 0.2 add_convert_fusion
  76.0 0.1 reshape.52
  76.2 1.9 all_gather.16
  78.1 2.0 fusion.65
  80.1 66.0 %reduce-scatter.11.cloned.1.call-done = f32[16,2336]{1,0:T(8,128)} async-done(((f32[128,2336]{1,0:T(8,128)}), f32[16,2336]{1,0:T(8,128)}) %reduce-scatter.11.cloned.1.call-update) | async-done | bytes 149520 | tf_op jit(solution)/shard_map/reduce_scatter | solution.py:53
  146.2 0.9 add_convert_fusion.3
  147.1 31.8 %all_gather.17 = bf16[128,2336]{1,0:T(8,128)(2,1)S(1)} all-gather(bf16[16,2336]{1,0:T(8,128)(2,1)S(1)} %add_convert_fusion.3), channel_id=1, replica_groups=mesh['groups'=2,'gx'=8,'gy'=2] {'gx'}, dimensions={0}, use_global_device_ids=true | all-gather | bytes 672768 | tf_op jit(solution)/shard_map/all_gather | solution.py:49
  178.9 0.2 fusion.12
  179.1 2.5 psum.43
  181.6 2.9 fusion.30
  184.5 0.2 reduce-scatter.15.cloned.1.call-start
  184.7 6.5 %reduce-scatter.13.cloned.1.call-done = f32[64,512]{1,0:T(8,128)} async-done(((f32[128,512]{1,0:T(8,128)}), f32[64,512]{1,0:T(8,128)}) %reduce-scatter.13.cloned.1.call-update) | async-done | bytes 131088 | tf_op jit(solution)/shard_map/reduce_scatter | solution.py:110
  191.2 0.9 convert_element_type.102
  192.3 5.6 %fusion.42 = f32[8,64,1,128]{3,2,1,0:T(1,128)S(1)} fusion(bf16[8,64,64,128]{3,2,1,0:T(8,128)(2,1)} %param.34, bf16[64,8,64,1]{2,1,0,3:T(8,128)(2,1)S(1)} %reshape.61), kind=kOutput, calls=%fused_computation.53 | convolution fusion | flops 8388608 | bytes 8716288 | tf_op jit(solution)/shard_map/bhd,hbds->hbs/dot_general | solution.py:30
  197.9 0.2 fusion.22
  198.2 7.9 %fusion.2 = f32[64,8,1,64]{3,2,1,0:T(1,128)S(1)} fusion(bf16[8,64,64,128]{3,2,1,0:T(8,128)(2,1)} %param.35, bf16[8,64,128,1]{2,1,0,3:T(8,128)(2,1)S(1)} %fusion.22), kind=kOutput, calls=%fused_computation.2 | convolution fusion | flops 8388608 | bytes 8650752 | tf_op jit(solution)/shard_map/hbs,hbds->bhd/dot_general | solution.py:35
  206.2 0.1 reshape.54
  206.3 1.9 all_gather.18
  208.2 2.0 fusion.66
  210.3 65.9 %reduce-scatter.15.cloned.1.call-done = f32[16,2336]{1,0:T(8,128)} async-done(((f32[128,2336]{1,0:T(8,128)}), f32[16,2336]{1,0:T(8,128)}) %reduce-scatter.15.cloned.1.call-update) | async-done | bytes 149520 | tf_op jit(solution)/shard_map/reduce_scatter | solution.py:53
  276.2 0.9 add_convert_fusion.2
  277.1 31.8 %all_gather.19 = bf16[128,2336]{1,0:T(8,128)(2,1)S(1)} all-gather(bf16[16,2336]{1,0:T(8,128)(2,1)S(1)} %add_convert_fusion.2), channel_id=1, replica_groups=mesh['groups'=2,'gx'=8,'gy'=2] {'gx'}, dimensions={0}, use_global_device_ids=true | all-gather | bytes 672768 | tf_op jit(solution)/shard_map/all_gather | solution.py:49
  308.9 0.2 fusion.15
  309.1 2.5 psum.44
  311.6 5.5 %convolution_convert_fusion = bf16[128,1544]{0,1:T(8,128)(2,1)} fusion(bf16[2336,1544]{0,1:T(8,128)(2,1)} %param.30, bf16[128,2336]{1,0:T(8,128)(2,1)S(1)} %all_gather.19, f32[2336]{0:T(1024)S(1)} %copy-done.4, f32[128]{0:T(128)S(1)} %add_rsqrt_fusion.1), kind=kOutput, calls=%fused_computation.9 | convolution fusion | flops 924730368 | bytes 8216704 | tf_op jit(solution)/shard_map/dot_general | solution.py:120
  317.1 5.5 %convolution_convert_fusion.1 = bf16[128,1544]{0,1:T(8,128)(2,1)} fusion(bf16[2336,1544]{0,1:T(8,128)(2,1)} %param.29, bf16[128,2336]{1,0:T(8,128)(2,1)S(1)} %all_gather.19, f32[2336]{0:T(1024)S(1)} %copy-done.4, f32[128]{0:T(128)S(1)} %add_rsqrt_fusion.1), kind=kOutput, calls=%fused_computation.10 | convolution fusion | flops 924730368 | bytes 8216704 | tf_op jit(solution)/shard_map/dot_general | solution.py:117
  322.6 18.3 %all-reduce.3.cloned.1.call-done = (bf16[128,1544]{0,1:T(8,128)(2,1)}, bf16[128,1544]{0,1:T(8,128)(2,1)}) async-done(((bf16[128,1544]{0,1:T(8,128)(2,1)}, bf16[128,1544]{0,1:T(8,128)(2,1)}), (bf16[128,1544]{0,1:T(8,128)(2,1)}, bf16[128,1544]{0,1:T(8,128)(2,1)})) %all-reduce.3.cloned.1.call-update) | async-done | bytes 790544 | tf_op jit(solution)/shard_map/psum | solution.py:116
  341.0 6.2 %fusion.34 = f32[128,2336]{1,0:T(8,128)} fusion(bf16[1544,2336]{1,0:T(8,128)(2,1)} %param.31, bf16[128,1544]{0,1:T(8,128)(2,1)} %get-tuple-element.5, bf16[128,1544]{0,1:T(8,128)(2,1)} %get-tuple-element.6), kind=kOutput, calls=%fused_computation.45 | convolution fusion | flops 925708288 | bytes 9200128 | tf_op jit(solution)/shard_map/dot_general | solution.py:54
  347.1 66.1 %reduce-scatter.17.cloned.1.call-done = f32[16,2336]{1,0:T(8,128)} async-done(((f32[128,2336]{1,0:T(8,128)}), f32[16,2336]{1,0:T(8,128)}) %reduce-scatter.17.cloned.1.call-update) | async-done | bytes 149520 | tf_op jit(solution)/shard_map/reduce_scatter | solution.py:53
  413.3 1.0 fusion.53
  414.3 2.5 psum.47
  416.8 1.6 fusion.55
  (45 shorter events, 1.0 us)
Async XLA Ops:
  6.5 71.6 %copy-start = (bf16[512,2336]{0,1:T(8,128)(2,1)S(1)}, bf16[512,2336]{0,1:T(8,128)(2,1)}, u32[]{:S(2)}) copy-start(bf16[512,2336]{0,1:T(8,128)(2,1)} %param.26) | copy-start | bytes 7176196
  6.5 39.4 %copy-start.7 = (f32[2336]{0:T(1024)S(1)}, f32[2336]{0:T(1024)}, u32[]{:S(2)}) copy-start(f32[2336]{0:T(1024)} %param.20) | copy-start | bytes 28036
  6.5 48.2 %reduce-scatter.7.cloned.1.call-start = ((), (), s32[]{:S(2)}) async-start(), calls=%async_computation.6 | async-start | bytes 393216 | tf_op jit(solution)/shard_map/reduce_scatter | solution.py:99
  45.8 20.4 %reduce-scatter.9.cloned.1.call-start = ((), (), s32[]{:S(2)}) async-start(), calls=%async_computation.7 | async-start | bytes 786432 | tf_op jit(solution)/shard_map/reduce_scatter | solution.py:100
  45.9 4.2 copy-start.6
  50.0 96.1 %reduce-scatter.11.cloned.1.call-start = ((), (), s32[]{:S(2)}) async-start(), calls=%async_computation.8 | async-start | bytes 1400832 | tf_op jit(solution)/shard_map/reduce_scatter | solution.py:53
  78.1 68.1 %copy-start.3 = (bf16[16,2336]{1,0:T(8,128)(2,1)S(1)}, bf16[16,2336]{1,0:T(8,128)(2,1)}, u32[]{:S(2)}) copy-start(bf16[16,2336]{1,0:T(8,128)(2,1)} %param.18) | copy-start | bytes 224260
  78.1 103.5 %copy-start.8 = (f32[2336]{0:T(1024)S(1)}, f32[2336]{0:T(1024)}, u32[]{:S(2)}) copy-start(f32[2336]{0:T(1024)} %param.21) | copy-start | bytes 28036
  80.1 111.1 %reduce-scatter.13.cloned.1.call-start = ((), (), s32[]{:S(2)}) async-start(), calls=%async_computation.9 | async-start | bytes 393216 | tf_op jit(solution)/shard_map/reduce_scatter | solution.py:110
  184.5 91.7 %reduce-scatter.15.cloned.1.call-start = ((), (), s32[]{:S(2)}) async-start(), calls=%async_computation.10 | async-start | bytes 1400832 | tf_op jit(solution)/shard_map/reduce_scatter | solution.py:53
  198.2 10.0 %copy-start.2 = (bf16[512,2336]{0,1:T(8,128)(2,1)S(1)}, bf16[512,2336]{0,1:T(8,128)(2,1)}, u32[]{:S(2)}) copy-start(bf16[512,2336]{0,1:T(8,128)(2,1)} %param.28) | copy-start | bytes 7176196
  208.2 103.4 %copy-start.4 = (f32[2336]{0:T(1024)S(1)}, f32[2336]{0:T(1024)}, u32[]{:S(2)}) copy-start(f32[2336]{0:T(1024)} %param.22) | copy-start | bytes 28036
  210.2 130.7 %all-reduce.3.cloned.1.call-start = ((), (), s32[]{:S(2)}) async-start(), calls=%async_computation.12 | async-start | bytes 1581056 | tf_op jit(solution)/shard_map/psum | solution.py:116
  322.6 90.7 %reduce-scatter.17.cloned.1.call-start = ((), (), s32[]{:S(2)}) async-start(), calls=%async_computation.11 | async-start | bytes 1400832 | tf_op jit(solution)/shard_map/reduce_scatter | solution.py:53
  341.0 75.8 %copy-start.5 = (f32[2336]{0:T(1024)S(1)}, f32[2336]{0:T(1024)}, u32[]{:S(2)}) copy-start(f32[2336]{0:T(1024)} %param.23) | copy-start | bytes 28036
  341.0 77.5 %copy-start.1 = (bf16[512,2336]{0,1:T(8,128)(2,1)S(1)}, bf16[512,2336]{0,1:T(8,128)(2,1)}, u32[]{:S(2)}) copy-start(bf16[512,2336]{0,1:T(8,128)(2,1)} %param.26) | copy-start | bytes 7176196
Sparse Core Ops, SparseCore 0:
  46.0 8.7 reduce-scatter.6
  57.1 9.0 reduce-scatter.8
  80.2 65.8 reduce-scatter.10
  184.6 6.5 reduce-scatter.12
  210.4 65.7 reduce-scatter.14
  322.7 18.1 all-reduce.2
  347.3 65.9 reduce-scatter.16
where the time goes:
time: 426 us; the launch traced here: 425 us
  waiting for transfers between devices  232 us (54%)
  blocking collectives  111 us (26%)
  matrix products  58.1 us (14%)
  between operations  13.6 us (3%)
  other arithmetic  9.37 us (2%)
    reduce_scatter x3, waiting for transfers between devices, accumulate(): lax.psum_scatter(jnp.dot(left, weight, preferred_element_type=jnp.float32...  198 us
    all_gather x3, blocking collectives, widen(): return lax.all_gather(stream, 'gx', axis=0, tiled=True)  97.2 us
    psum x1, waiting for transfers between devices, per_device(): lax.psum(jnp.dot(normed, ffn_gate, preferred_element_type=jnp.float32).as...  18.3 us
    reduce_scatter x2, waiting for transfers between devices, per_device(): lax.psum_scatter(query_part, 'gy', scatter_dimension=0, tiled=True)  11.1 us
    dot_general x3, matrix products, accumulate(): jnp.dot(left, weight, preferred_element_type=jnp.float32)  10.1 us
    psum x4, blocking collectives, normalize(): squares = lax.psum(jnp.sum(stream_f * stream_f, axis=1), 'gy')  9.85 us
  transfers between devices with their start and end apart: 7, of which 7 were waited for; matrix products, arithmetic and copies ran while one was open for 3% of the time, Pallas kernels for 0%

commit v1 on v0

v1 whole, which is shorter than its diff:
```python
import jax
import jax.numpy as jnp
from jax import lax
from jax.sharding import PartitionSpec as P

D = 4672
DK = 64
F32 = jnp.float32
BF16 = jnp.bfloat16


def swap(value, axis, mask, size):
    return lax.ppermute(value, axis, [(i, i ^ mask) for i in range(size)])


class Line:
    def __init__(self, size):
        self.size = size
        self.direct = size == 8
        self.index = lax.axis_index("gx")

    def gather(self, block):
        if not self.direct:
            return lax.all_gather(block, "gx", axis=0, tiled=True)
        blocks = {0: block}
        for mask in (4, 6, 2):
            blocks[mask] = swap(block, "gx", mask, self.size)
        blocks[1] = swap(block, "gx", 1, self.size)
        for mask in (4, 2, 6):
            blocks[mask ^ 1] = swap(blocks[mask], "gx", 1, self.size)
        return jnp.concatenate([blocks[p] for p in range(self.size)], axis=0)

    def scatter_sum(self, partial):
        if not self.direct:
            return lax.psum_scatter(partial, "gx", scatter_dimension=0, tiled=True)
        rows = partial.shape[0] // self.size
        blocks = [partial[p * rows : (p + 1) * rows] for p in range(self.size)]
        pairs = {}
        for p in (6, 4, 2, 0):
            pairs[p] = blocks[p] + swap(blocks[p ^ 1].astype(BF16), "gx", 1, self.size).astype(F32)
        total = pairs[0]
        for mask in (6, 4, 2):
            total = total + swap(pairs[mask].astype(BF16), "gx", mask, self.size).astype(F32)
        return total

    def halves(self, value):
        gy = lax.axis_index("gy")
        half = value.shape[0] // 2
        first = gy ^ (self.index // 4) if self.direct else gy
        mine = jnp.where(first == 0, value[:half], value[half:])
        other = jnp.where(first == 0, value[half:], value[:half])
        return mine, other

    def join(self, mine, other):
        gy = lax.axis_index("gy")
        first = gy ^ (self.index // 4) if self.direct else gy
        low = jnp.where(first == 0, mine, other)
        high = jnp.where(first == 0, other, mine)
        return jnp.concatenate([low, high], axis=0)

    def reorder(self, half):
        if not self.direct:
            return half
        blocks = half.reshape(4, half.shape[0] // 4, half.shape[1])
        low = self.index & 3
        blocks = jnp.where(low & 1 == 0, blocks, blocks[jnp.array([1, 0, 3, 2])])
        blocks = jnp.where(low & 2 == 0, blocks, blocks[jnp.array([2, 3, 0, 1])])
        return blocks.reshape(half.shape)


def self_attend(query, new_key, new_value, cache_keys, cache_values, lengths):
    scores = jnp.einsum("bhd,hbds->hbs", query, cache_keys, preferred_element_type=jnp.float32)
    own_score = jnp.einsum("bhd,bhd->hb", query, new_key, preferred_element_type=jnp.float32)
    slots = lax.broadcasted_iota(jnp.int32, (1, scores.shape[1], scores.shape[2]), 2)
    valid_slots = slots < lengths[None, :, None]
    scores = jnp.where(valid_slots, scores, -1e30)
    top_score = jnp.maximum(jnp.max(scores, axis=2), own_score)
    expo = jnp.where(valid_slots, jnp.exp(scores - top_score[:, :, None]), 0.0)
    own_expo = jnp.exp(own_score - top_score)
    totals = jnp.sum(expo, axis=2) + own_expo
    attn_probs = (expo / totals[:, :, None]).astype(jnp.bfloat16)
    own_prob = (own_expo / totals).astype(jnp.bfloat16)
    mixed = jnp.einsum(
        "hbs,hbds->bhd", attn_probs, cache_values, preferred_element_type=jnp.float32
    )
    mixed = mixed + own_prob.T.astype(jnp.float32)[:, :, None] * new_value.astype(jnp.float32)
    return mixed.astype(jnp.bfloat16).reshape(query.shape[0], query.shape[1] * query.shape[2])


def cross_attend(query, cache_keys, cache_values):
    scores = jnp.einsum("bhd,hbds->hbs", query, cache_keys, preferred_element_type=jnp.float32)
    top_score = jnp.max(scores, axis=2)
    expo = jnp.exp(scores - top_score[:, :, None])
    totals = jnp.sum(expo, axis=2)
    attn_probs = (expo / totals[:, :, None]).astype(jnp.bfloat16)
    mixed = jnp.einsum(
        "hbs,hbds->bhd", attn_probs, cache_values, preferred_element_type=jnp.float32
    )
    return mixed.astype(jnp.bfloat16).reshape(query.shape[0], query.shape[1] * query.shape[2])


def normalize(stream, gain):
    stream_f = stream.astype(F32)
    squares = jnp.sum(stream_f * stream_f, axis=1, keepdims=True)
    squares = squares + swap(squares, "gy", 1, 2)
    inverse = lax.rsqrt(squares / D + 1e-06)
    return (stream_f * inverse * gain[None, :]).astype(BF16)


def dot(left, right):
    return jnp.dot(left, right, preferred_element_type=F32)


def per_device(
    size,
    x_in,
    lengths,
    self_gain,
    cross_gain,
    ffn_gain,
    final_gain,
    self_query,
    self_kv,
    self_out,
    cross_query,
    cross_out,
    ffn_gate,
    ffn_up,
    ffn_down,
    self_keys,
    self_values,
    cross_keys,
    cross_values,
):
    line = Line(size)
    width_local = x_in.shape[1]
    heads_here = self_query.shape[1] // DK
    rows_here = self_keys.shape[1]

    def half_sum(partial):
        mine, other = line.halves(partial)
        return mine + swap(other, "gy", 1, 2)

    def update(stream, partial):
        return (stream.astype(F32) + line.scatter_sum(partial)).astype(BF16)

    def project_heads(stream, heads, weight):
        heads = line.reorder(heads)
        return update(stream, dot(line.join(heads, swap(heads, "gy", 1, 2)), weight))

    stream = x_in
    normed = line.gather(normalize(stream, self_gain))
    query_part = dot(normed, self_query)
    pair_part = dot(normed, self_kv.reshape(width_local, heads_here * 2 * DK))
    query = line.reorder(half_sum(query_part)).astype(BF16).reshape(rows_here, heads_here, DK)
    new_pair = line.reorder(half_sum(pair_part)).astype(BF16).reshape(rows_here, heads_here, 2 * DK)
    heads = self_attend(
        query, new_pair[:, :, :DK], new_pair[:, :, DK:], self_keys, self_values, lengths
    )
    stream = project_heads(stream, heads, self_out)

    normed = line.gather(normalize(stream, cross_gain))
    query = line.reorder(half_sum(dot(normed, cross_query)))
    query = query.astype(BF16).reshape(rows_here, heads_here, DK)
    stream = project_heads(stream, cross_attend(query, cross_keys, cross_values), cross_out)

    normed = line.gather(normalize(stream, ffn_gain))
    gate = dot(normed, ffn_gate)
    gate = gate + swap(gate.astype(BF16), "gy", 1, 2).astype(F32)
    up = dot(normed, ffn_up)
    up = up + swap(up.astype(BF16), "gy", 1, 2).astype(F32)
    hidden = (jax.nn.gelu(gate, approximate=True) * up).astype(BF16)
    stream = update(stream, dot(hidden, ffn_down))
    return normalize(stream, final_gain)


def solution(mesh):
    size = mesh.shape["gx"]

    def device(*args):
        return per_device(size, *args)

    return jax.shard_map(
        device,
        mesh=mesh,
        in_specs=(
            P(("groups", "gx"), "gy"),
            P(("groups", "gy")),
            P("gy"),
            P("gy"),
            P("gy"),
            P("gy"),
            P("gy", "gx"),
            P("gy", "gx", None),
            P("gx", "gy"),
            P("gy", "gx"),
            P("gx", "gy"),
            P("gy", "gx"),
            P("gy", "gx"),
            P("gx", "gy"),
            P("gx", ("groups", "gy"), None, None),
            P("gx", ("groups", "gy"), None, None),
            P("gx", ("groups", "gy"), None, None),
            P("gx", ("groups", "gy"), None, None),
        ),
        out_specs=P(("groups", "gx"), "gy"),
        check_vma=False,
    )
```

time: 426 us -> 199 us (0.47)
  waiting for transfers between devices: 232 us -> 40.9 us
  blocking collectives: 111 us -> 0 us
  starting transfers between devices: 0.43 us -> 54 us
  local copies, waits for them, and re-layouts: 0.88 us -> 43.9 us
  between operations: 13.6 us -> 0.71 us
  matrix products: 58.1 us -> 49.4 us
    reduce_scatter x6 -> x0, waiting for transfers between devices: 214 us -> none  [the longest x3 198 us: accumulate(): lax.psum_scatter(jnp.dot(left, weight, preferred_element_type=jnp.float32...]
    all_gather x5 -> x0, blocking collectives: 101 us -> none  [the longest x3 97.2 us: widen(): return lax.all_gather(stream, 'gx', axis=0, tiled=True)]
    ppermute x0 -> x53, starting transfers between devices: none -> 54 us  [swap(): return lax.ppermute(value, axis, [(i, i ^ mask) for i in range(size)])]
    ppermute x0 -> x53, waiting for transfers between devices: none -> 40.9 us  [swap(): return lax.ppermute(value, axis, [(i, i ^ mask) for i in range(size)])]
    slice x0 -> x18, local copies, waits for them, and re-layouts: none -> 23.3 us  [scatter_sum(): blocks = [partial[p * rows:(p + 1) * rows] for p in range(self.size)]]
    psum x1 -> x0, waiting for transfers between devices: 18.3 us -> none  [per_device(): lax.psum(jnp.dot(normed, ffn_gate, preferred_element_type=jnp.float32).as...]
    unnamed x19 -> x57, local copies, waits for them, and re-layouts: 0.06 us -> 14 us
    psum x4 -> x0, blocking collectives: 9.85 us -> none  [normalize(): squares = lax.psum(jnp.sum(stream_f * stream_f, axis=1), 'gy')]
  transfers between devices with their start and end apart: 7 -> 53, of which waited for: 7 -> 23; matrix products, arithmetic and copies ran while one was open for 3% -> 18% of each run, Pallas kernels for 0% -> 0%
where the time goes in v1:
time: 199 us; the launch traced here: 198 us
  starting transfers between devices  54 us (27%)
  matrix products  49.4 us (25%)
  local copies, waits for them, and re-layouts  43.9 us (22%)
  waiting for transfers between devices  40.9 us (21%)
  other arithmetic  9.3 us (5%)
    ppermute x53, starting transfers between devices, swap(): return lax.ppermute(value, axis, [(i, i ^ mask) for i in range(size)])  54 us
    ppermute x53, waiting for transfers between devices, swap(): return lax.ppermute(value, axis, [(i, i ^ mask) for i in range(size)])  40.9 us
    slice x18, local copies, waits for them, and re-layouts, scatter_sum(): blocks = [partial[p * rows:(p + 1) * rows] for p in range(self.size)]  23.3 us
    dot_general x8, matrix products, dot(): return jnp.dot(left, right, preferred_element_type=F32)  22.5 us
    unnamed x57, local copies, waits for them, and re-layouts  14 us
    dot_general x1, matrix products, cross_attend(): jnp.einsum('hbs,hbds->bhd', attn_probs, cache_values, preferred_element_t...  7.78 us
    dot_general x1, matrix products, self_attend(): jnp.einsum('hbs,hbds->bhd', attn_probs, cache_values, preferred_element_t...  7.78 us
    dot_general x1, matrix products, self_attend(): jnp.einsum('bhd,hbds->hbs', query, cache_keys, preferred_element_type=jnp...  5.65 us
  transfers between devices with their start and end apart: 53, of which 23 were waited for; matrix products, arithmetic and copies ran while one was open for 18% of the time, Pallas kernels for 0%

profile of v1, /device:TPU:0, one launch (start us, length us, event | category | flops | bytes accessed | tf_op | source)
XLA Modules:
  0.0 198.1 jit_solution(134874917627729166)
XLA Ops:
  4.1 4.7 %collective-permute-start.6 = (bf16[16,2336]{1,0:T(8,128)(2,1)S(1)}, bf16[16,2336]{1,0:T(8,128)(2,1)S(1)}, u32[]{:S(2)}, u32[]{:S(2)}) collective-permute-start(bf16[16,2336]{1,0:T(8,128)(2,1)S(1)} %get-tuple-element.16), channel_id=1, source_target_pairs={{0,12},{2,14},{4,8},{6,10},{8,4},{10,6},{12,0},{14,2},{1,13},{3,15... | collective-permute-start | bytes 224264 | tf_op jit(solution)/shard_map/ppermute | solution.py:13
  9.5 1.6 collective-permute-start.1
  12.1 1.6 collective-permute-start.7
  13.8 2.2 %collective-permute-done.4 = bf16[16,2336]{1,0:T(8,128)(2,1)S(1)} collective-permute-done((bf16[16,2336]{1,0:T(8,128)(2,1)S(1)}, bf16[16,2336]{1,0:T(8,128)(2,1)S(1)}, u32[]{:S(2)}, u32[]{:S(2)}) %collective-permute-start.4) | collective-permute-done | bytes 74784 | tf_op jit(solution)/shard_map/ppermute | solution.py:13
  16.0 1.5 collective-permute-start.5
  18.0 3.9 %collective-permute-done.3 = bf16[16,2336]{1,0:T(8,128)(2,1)S(1)} collective-permute-done((bf16[16,2336]{1,0:T(8,128)(2,1)S(1)}, bf16[16,2336]{1,0:T(8,128)(2,1)S(1)}, u32[]{:S(2)}, u32[]{:S(2)}) %collective-permute-start.3) | collective-permute-done | bytes 74784 | tf_op jit(solution)/shard_map/ppermute | solution.py:13
  22.1 2.2 %fusion.91 = f32[128,512]{1,0:T(8,128)S(1)} fusion(bf16[128,2336]{1,0:T(8,128)(2,1)S(1)} %constant_dynamic-update-slice_fusion, bf16[2336,512]{1,0:T(8,128)(2,1)} %param.34), kind=kOutput, calls=%fused_computation.180 | convolution fusion | flops 306184192 | bytes 3252224 | tf_op jit(solution)/shard_map/dot_general | solution.py:111
  24.2 3.2 %fusion.6 = f32[128,1024]{1,0:T(8,128)S(1)} fusion(bf16[128,2336]{1,0:T(8,128)(2,1)S(1)} %constant_dynamic-update-slice_fusion, bf16[292,8,8,128]{3,2,1,0:T(8,128)(2,1)} %bitcast.134), kind=kOutput, calls=%fused_computation.16 | convolution fusion | flops 612368384 | bytes 5906432 | tf_op jit(solution)/shard_map/dot_general | solution.py:111
  30.2 5.6 %fusion.35 = f32[8,64,1,128]{3,2,1,0:T(1,128)S(1)} fusion(bf16[8,64,64,128]{3,2,1,0:T(8,128)(2,1)} %param.42, bf16[64,8,64,1]{2,1,0,3:T(8,128)(2,1)S(1)} %reshape.152), kind=kOutput, calls=%fused_computation.48 | convolution fusion | flops 8388608 | bytes 8716288 | tf_op jit(solution)/shard_map/bhd,hbds->hbs/dot_general | solution.py:72
  39.3 7.8 %fusion.4 = f32[64,8,1,64]{3,2,1,0:T(1,128)S(1)} fusion(bf16[8,64,64,128]{3,2,1,0:T(8,128)(2,1)} %param.43, bf16[8,64,128,1]{2,1,0,3:T(8,128)(2,1)S(1)} %fusion.63), kind=kOutput, calls=%fused_computation.14 | convolution fusion | flops 8388608 | bytes 8650752 | tf_op jit(solution)/shard_map/hbs,hbds->bhd/dot_general | solution.py:83
  50.0 1.9 fusion.86
  51.9 1.5 fusion.85
  53.4 1.4 copy.192
  60.2 2.8 %fusion.82 = (f32[16,2336]{0,1:T(8,128)S(1)}, f32[16,2336]{0,1:T(8,128)}, f32[16,2336]{0,1:T(8,128)}, f32[16,2336]{0,1:T(8,128)}) fusion(f32[128,2336]{0,1:T(8,128)S(1)} %copy-done.2), kind=kLoop, calls=%fused_computation.171 | loop fusion | bytes 1196032 | tf_op jit(solution)/shard_map/slice | solution.py:37
  63.0 1.7 copy.234
  64.7 1.7 copy.233
  67.8 2.0 %collective-permute-start.13 = (bf16[16,2336]{1,0:T(8,128)(2,1)S(1)}, bf16[16,2336]{1,0:T(8,128)(2,1)S(1)}, u32[]{:S(2)}, u32[]{:S(2)}) collective-permute-start(bf16[16,2336]{1,0:T(8,128)(2,1)S(1)} %add_convert_fusion.9), channel_id=1, source_target_pairs={{0,12},{2,14},{4,8},{6,10},{8,4},{10,6},{12,0},{14,2},{1,13},{3,15... | collective-permute-start | bytes 224264 | tf_op jit(solution)/shard_map/ppermute | solution.py:13
  70.9 4.4 %collective-permute-done.15 = bf16[16,2336]{1,0:T(8,128)(2,1)S(1)} collective-permute-done((bf16[16,2336]{1,0:T(8,128)(2,1)S(1)}, bf16[16,2336]{1,0:T(8,128)(2,1)S(1)}, u32[]{:S(2)}, u32[]{:S(2)}) %collective-permute-start.15) | collective-permute-done | bytes 74784 | tf_op jit(solution)/shard_map/ppermute | solution.py:13
  77.1 2.0 %collective-permute-start.24 = (bf16[16,2336]{1,0:T(8,128)(2,1)S(1)}, bf16[16,2336]{1,0:T(8,128)(2,1)S(1)}, u32[]{:S(2)}, u32[]{:S(2)}) collective-permute-start(bf16[16,2336]{1,0:T(8,128)(2,1)S(1)} %get-tuple-element.12), channel_id=1, source_target_pairs={{0,12},{2,14},{4,8},{6,10},{8,4},{10,6},{12,0},{14,2},{1,13},{3,15... | collective-permute-start | bytes 224264 | tf_op jit(solution)/shard_map/ppermute | solution.py:13
  79.6 2.0 collective-permute-start.20
  82.8 1.5 collective-permute-done.24
  85.5 1.6 collective-permute-done.22
  89.1 3.9 %collective-permute-done.21 = bf16[16,2336]{1,0:T(8,128)(2,1)S(1)} collective-permute-done((bf16[16,2336]{1,0:T(8,128)(2,1)S(1)}, bf16[16,2336]{1,0:T(8,128)(2,1)S(1)}, u32[]{:S(2)}, u32[]{:S(2)}) %collective-permute-start.21) | collective-permute-done | bytes 74784 | tf_op jit(solution)/shard_map/ppermute | solution.py:13
  93.2 2.2 %fusion.92 = f32[128,512]{1,0:T(8,128)S(1)} fusion(bf16[128,2336]{1,0:T(8,128)(2,1)S(1)} %constant_dynamic-update-slice_fusion.8, bf16[2336,512]{1,0:T(8,128)(2,1)} %param.37), kind=kOutput, calls=%fused_computation.181 | convolution fusion | flops 306184192 | bytes 3252224 | tf_op jit(solution)/shard_map/dot_general | solution.py:111
  98.1 5.6 %fusion.32 = f32[8,64,1,128]{3,2,1,0:T(1,128)S(1)} fusion(bf16[8,64,64,128]{3,2,1,0:T(8,128)(2,1)} %param.44, bf16[64,8,64,1]{2,1,0,3:T(8,128)(2,1)S(1)} %reshape.158), kind=kOutput, calls=%fused_computation.45 | convolution fusion | flops 8388608 | bytes 8716288 | tf_op jit(solution)/shard_map/bhd,hbds->hbs/dot_general | solution.py:91
  104.0 7.8 %fusion.2 = f32[64,8,1,64]{3,2,1,0:T(1,128)S(1)} fusion(bf16[8,64,64,128]{3,2,1,0:T(8,128)(2,1)} %param.45, bf16[8,64,128,1]{2,1,0,3:T(8,128)(2,1)S(1)} %fusion.13), kind=kOutput, calls=%fused_computation.12 | convolution fusion | flops 8388608 | bytes 8650752 | tf_op jit(solution)/shard_map/hbs,hbds->bhd/dot_general | solution.py:96
  114.7 2.5 %fusion.87 = (bf16[128,2336]{0,1:T(8,128)(2,1)S(1)}, f32[128,2336]{0,1:T(8,128)S(1)}) fusion(bf16[512,2336]{0,1:T(8,128)(2,1)} %param.38, bf16[64,512]{1,0:T(8,128)(2,1)S(1)} %get-tuple-element.42, bf16[64,512]{1,0:T(8,128)(2,1)S(1)} %get-tuple-element.41), kind=kOutput, calls=%fused_computation.176 | convolution fusion | flops 306745344 | bytes 4317184 | tf_op jit(solution)/shard_map/dot_general | solution.py:111
  117.1 1.8 fusion.84
  126.6 2.8 %fusion.81 = (f32[16,2336]{0,1:T(8,128)S(1)}, f32[16,2336]{0,1:T(8,128)}, f32[16,2336]{0,1:T(8,128)}, f32[16,2336]{0,1:T(8,128)}) fusion(f32[128,2336]{0,1:T(8,128)S(1)} %get-tuple-element.48), kind=kLoop, calls=%fused_computation.170 | loop fusion | bytes 1196032 | tf_op jit(solution)/shard_map/slice | solution.py:37
  129.4 1.7 copy.238
  131.1 1.6 copy.237
  133.6 2.0 %collective-permute-start.30 = (bf16[16,2336]{1,0:T(8,128)(2,1)S(1)}, bf16[16,2336]{1,0:T(8,128)(2,1)S(1)}, u32[]{:S(2)}, u32[]{:S(2)}) collective-permute-start(bf16[16,2336]{1,0:T(8,128)(2,1)S(1)} %add_convert_fusion.6), channel_id=1, source_target_pairs={{0,12},{2,14},{4,8},{6,10},{8,4},{10,6},{12,0},{14,2},{1,13},{3,15... | collective-permute-start | bytes 224264 | tf_op jit(solution)/shard_map/ppermute | solution.py:13
  137.3 3.7 %collective-permute-done.32 = bf16[16,2336]{1,0:T(8,128)(2,1)S(1)} collective-permute-done((bf16[16,2336]{1,0:T(8,128)(2,1)S(1)}, bf16[16,2336]{1,0:T(8,128)(2,1)S(1)}, u32[]{:S(2)}, u32[]{:S(2)}) %collective-permute-start.32) | collective-permute-done | bytes 74784 | tf_op jit(solution)/shard_map/ppermute | solution.py:13
  142.9 2.0 %collective-permute-start.41 = (bf16[16,2336]{1,0:T(8,128)(2,1)S(1)}, bf16[16,2336]{1,0:T(8,128)(2,1)S(1)}, u32[]{:S(2)}, u32[]{:S(2)}) collective-permute-start(bf16[16,2336]{1,0:T(8,128)(2,1)S(1)} %get-tuple-element.8), channel_id=1, source_target_pairs={{0,12},{2,14},{4,8},{6,10},{8,4},{10,6},{12,0},{14,2},{1,13},{3,15... | collective-permute-start | bytes 224264 | tf_op jit(solution)/shard_map/ppermute | solution.py:13
  145.3 2.0 %collective-permute-start.37 = (bf16[16,2336]{1,0:T(8,128)(2,1)S(1)}, bf16[16,2336]{1,0:T(8,128)(2,1)S(1)}, u32[]{:S(2)}, u32[]{:S(2)}) collective-permute-start(bf16[16,2336]{1,0:T(8,128)(2,1)S(1)} %get-tuple-element.8), channel_id=1, source_target_pairs={{0,4},{2,6},{4,0},{6,2},{8,12},{10,14},{12,8},{14,10},{1,5},{3,7},... | collective-permute-start | bytes 224264 | tf_op jit(solution)/shard_map/ppermute | solution.py:13
  148.5 1.5 collective-permute-done.41
  151.2 1.6 collective-permute-done.39
  154.9 4.0 %collective-permute-done.38 = bf16[16,2336]{1,0:T(8,128)(2,1)S(1)} collective-permute-done((bf16[16,2336]{1,0:T(8,128)(2,1)S(1)}, bf16[16,2336]{1,0:T(8,128)(2,1)S(1)}, u32[]{:S(2)}, u32[]{:S(2)}) %collective-permute-start.38) | collective-permute-done | bytes 74784 | tf_op jit(solution)/shard_map/ppermute | solution.py:13
  158.9 4.9 %fusion.89 = (bf16[128,1544]{0,1:T(8,128)(2,1)S(1)}, f32[128,1544]{0,1:T(8,128)S(1)}) fusion(bf16[128,2336]{1,0:T(8,128)(2,1)S(1)} %constant_dynamic-update-slice_fusion.16, bf16[2336,1544]{0,1:T(8,128)(2,1)} %param.39), kind=kOutput, calls=%fused_computation.178 | convolution fusion | flops 923534336 | bytes 8997376 | tf_op jit(solution)/shard_map/dot_general | solution.py:111
  164.0 2.3 %fusion.88 = (bf16[128,1544]{0,1:T(8,128)(2,1)S(1)}, f32[128,1544]{0,1:T(8,128)S(1)}) fusion(bf16[128,2336]{1,0:T(8,128)(2,1)S(1)} %constant_dynamic-update-slice_fusion.16, bf16[2336,1544]{0,1:T(8,128)(2,1)S(1)} %bitcast.113), kind=kOutput, calls=%fused_computation.177 | convolution fusion | flops 923534336 | bytes 8997376 | tf_op jit(solution)/shard_map/dot_general | solution.py:111
  168.2 3.4 %fusion.90 = (bf16[128,2336]{0,1:T(8,128)(2,1)S(1)}, f32[128,2336]{0,1:T(8,128)S(1)}) fusion(bf16[1544,2336]{1,0:T(8,128)(2,1)S(1)} %bitcast.115, f32[128,1544]{0,1:T(8,128)S(1)} %get-tuple-element.50, bf16[128,1544]{0,1:T(8,128)(2,1)S(1)} %collective-permute-done.44, f32[128,1544]{0,1:T(8,128)S(1)} %get-tuple-element.52, ...), kind=kOutput, calls=%fused_computation.179 | convolution fusion | flops 926402560 | bytes 11379200 | tf_op jit(solution)/shard_map/dot_general | solution.py:111
  171.6 1.8 fusion.83
  181.1 2.8 %fusion.80 = (f32[16,2336]{0,1:T(8,128)}, f32[16,2336]{0,1:T(8,128)S(1)}, f32[16,2336]{0,1:T(8,128)}, f32[16,2336]{0,1:T(8,128)}) fusion(f32[128,2336]{0,1:T(8,128)S(1)} %get-tuple-element.54), kind=kLoop, calls=%fused_computation.169 | loop fusion | bytes 1196032 | tf_op jit(solution)/shard_map/slice | solution.py:37
  184.2 1.8 copy.241
  186.0 1.7 copy.243
  188.1 2.0 %collective-permute-start.47 = (bf16[16,2336]{1,0:T(8,128)(2,1)S(1)}, bf16[16,2336]{1,0:T(8,128)(2,1)S(1)}, u32[]{:S(2)}, u32[]{:S(2)}) collective-permute-start(bf16[16,2336]{1,0:T(8,128)(2,1)S(1)} %add_convert_fusion.3), channel_id=1, source_target_pairs={{0,12},{2,14},{4,8},{6,10},{8,4},{10,6},{12,0},{14,2},{1,13},{3,15... | collective-permute-start | bytes 224264 | tf_op jit(solution)/shard_map/ppermute | solution.py:13
  191.4 1.6 copy.240
  193.1 2.6 %collective-permute-done.49 = bf16[16,2336]{1,0:T(8,128)(2,1)S(1)} collective-permute-done((bf16[16,2336]{1,0:T(8,128)(2,1)S(1)}, bf16[16,2336]{1,0:T(8,128)(2,1)S(1)}, u32[]{:S(2)}, u32[]{:S(2)}) %collective-permute-start.49) | collective-permute-done | bytes 74784 | tf_op jit(solution)/shard_map/ppermute | solution.py:13
  (221 shorter events, 67.2 us)
Async XLA Ops:
  1.2 1.9 collective-permute-start
  4.1 8.0 %collective-permute-start.6 = (bf16[16,2336]{1,0:T(8,128)(2,1)S(1)}, bf16[16,2336]{1,0:T(8,128)(2,1)S(1)}, u32[]{:S(2)}, u32[]{:S(2)}) collective-permute-start(bf16[16,2336]{1,0:T(8,128)(2,1)S(1)} %get-tuple-element.16), channel_id=1, source_target_pairs={{0,12},{2,14},{4,8},{6,10},{8,4},{10,6},{12,0},{14,2},{1,13},{3,15... | collective-permute-start | bytes 224264 | tf_op jit(solution)/shard_map/ppermute | solution.py:13
  8.8 7.1 %collective-permute-start.4 = (bf16[16,2336]{1,0:T(8,128)(2,1)S(1)}, bf16[16,2336]{1,0:T(8,128)(2,1)S(1)}, u32[]{:S(2)}, u32[]{:S(2)}) collective-permute-start(bf16[16,2336]{1,0:T(8,128)(2,1)S(1)} %get-tuple-element.16), channel_id=1, source_target_pairs={{0,8},{2,10},{4,12},{6,14},{8,0},{10,2},{12,4},{14,6},{1,9},{3,11}... | collective-permute-start | bytes 224264 | tf_op jit(solution)/shard_map/ppermute | solution.py:13
  8.8 8.6 %collective-permute-start.2 = (bf16[16,2336]{1,0:T(8,128)(2,1)S(1)}, bf16[16,2336]{1,0:T(8,128)(2,1)S(1)}, u32[]{:S(2)}, u32[]{:S(2)}) collective-permute-start(bf16[16,2336]{1,0:T(8,128)(2,1)S(1)} %get-tuple-element.16), channel_id=1, source_target_pairs={{0,4},{2,6},{4,0},{6,2},{8,12},{10,14},{12,8},{14,10},{1,5},{3,7},... | collective-permute-start | bytes 224264 | tf_op jit(solution)/shard_map/ppermute | solution.py:13
  9.5 8.5 %collective-permute-start.1 = (bf16[16,2336]{1,0:T(8,128)(2,1)S(1)}, bf16[16,2336]{1,0:T(8,128)(2,1)S(1)}, u32[]{:S(2)}, u32[]{:S(2)}) collective-permute-start(bf16[16,2336]{1,0:T(8,128)(2,1)S(1)} %get-tuple-element.16), channel_id=1, source_target_pairs={{0,2},{2,0},{4,6},{6,4},{8,10},{10,8},{12,14},{14,12},{1,3},{3,1},... | collective-permute-start | bytes 224264 | tf_op jit(solution)/shard_map/ppermute | solution.py:13
  12.1 9.9 %collective-permute-start.7 = (bf16[16,2336]{1,0:T(8,128)(2,1)S(1)}, bf16[16,2336]{1,0:T(8,128)(2,1)S(1)}, u32[]{:S(2)}, u32[]{:S(2)}) collective-permute-start(bf16[16,2336]{1,0:T(8,128)(2,1)S(1)} %collective-permute-done.6), channel_id=1, source_target_pairs={{0,2},{2,0},{4,6},{6,4},{8,10},{10,8},{12,14},{14,12},{1,3},{3,1},... | collective-permute-start | bytes 224264 | tf_op jit(solution)/shard_map/ppermute | solution.py:13
  16.0 6.0 %collective-permute-start.5 = (bf16[16,2336]{1,0:T(8,128)(2,1)S(1)}, bf16[16,2336]{1,0:T(8,128)(2,1)S(1)}, u32[]{:S(2)}, u32[]{:S(2)}) collective-permute-start(bf16[16,2336]{1,0:T(8,128)(2,1)S(1)} %collective-permute-done.4), channel_id=1, source_target_pairs={{0,2},{2,0},{4,6},{6,4},{8,10},{10,8},{12,14},{14,12},{1,3},{3,1},... | collective-permute-start | bytes 224264 | tf_op jit(solution)/shard_map/ppermute | solution.py:13
  17.5 4.5 %collective-permute-start.3 = (bf16[16,2336]{1,0:T(8,128)(2,1)S(1)}, bf16[16,2336]{1,0:T(8,128)(2,1)S(1)}, u32[]{:S(2)}, u32[]{:S(2)}) collective-permute-start(bf16[16,2336]{1,0:T(8,128)(2,1)S(1)} %collective-permute-done.2), channel_id=1, source_target_pairs={{0,2},{2,0},{4,6},{6,4},{8,10},{10,8},{12,14},{14,12},{1,3},{3,1},... | collective-permute-start | bytes 224264 | tf_op jit(solution)/shard_map/ppermute | solution.py:13
  27.5 1.4 collective-permute-start.8
  28.3 7.9 %collective-permute-start.9 = (f32[64,1024]{1,0:T(8,128)}, f32[64,1024]{1,0:T(8,128)}, u32[]{:S(2)}, u32[]{:S(2)}) collective-permute-start(f32[64,1024]{1,0:T(8,128)} %slice_select_fusion), channel_id=1, source_target_pairs={{0,1},{1,0},{2,3},{3,2},{4,5},{5,4},{6,7},{7,6},{8,9},{9,8},{10,11... | collective-permute-start | bytes 786440 | tf_op jit(solution)/shard_map/ppermute | solution.py:13
  56.1 11.7 %collective-permute-start.12 = (bf16[16,2336]{1,0:T(8,128)(2,1)S(1)}, bf16[16,2336]{1,0:T(8,128)(2,1)S(1)}, u32[]{:S(2)}, u32[]{:S(2)}) collective-permute-start(bf16[16,2336]{1,0:T(8,128)(2,1)S(1)} %copy.194), channel_id=1, source_target_pairs={{0,2},{2,0},{4,6},{6,4},{8,10},{10,8},{12,14},{14,12},{1,3},{3,1},... | collective-permute-start | bytes 224264 | tf_op jit(solution)/shard_map/ppermute | solution.py:13
  57.3 9.5 %collective-permute-start.14 = (bf16[16,2336]{1,0:T(8,128)(2,1)}, bf16[16,2336]{1,0:T(8,128)(2,1)S(1)}, u32[]{:S(2)}, u32[]{:S(2)}) collective-permute-start(bf16[16,2336]{1,0:T(8,128)(2,1)} %copy.196), channel_id=1, source_target_pairs={{0,2},{2,0},{4,6},{6,4},{8,10},{10,8},{12,14},{14,12},{1,3},{3,1},... | collective-permute-start | bytes 224264 | tf_op jit(solution)/shard_map/ppermute | solution.py:13
  58.2 11.7 %collective-permute-start.16 = (bf16[16,2336]{1,0:T(8,128)(2,1)S(1)}, bf16[16,2336]{1,0:T(8,128)(2,1)S(1)}, u32[]{:S(2)}, u32[]{:S(2)}) collective-permute-start(bf16[16,2336]{1,0:T(8,128)(2,1)S(1)} %copy.198), channel_id=1, source_target_pairs={{0,2},{2,0},{4,6},{6,4},{8,10},{10,8},{12,14},{14,12},{1,3},{3,1},... | collective-permute-start | bytes 224264 | tf_op jit(solution)/shard_map/ppermute | solution.py:13
  59.3 11.6 %collective-permute-start.11 = (bf16[16,2336]{1,0:T(8,128)(2,1)S(1)}, bf16[16,2336]{1,0:T(8,128)(2,1)S(1)}, u32[]{:S(2)}, u32[]{:S(2)}) collective-permute-start(bf16[16,2336]{1,0:T(8,128)(2,1)S(1)} %copy.192), channel_id=1, source_target_pairs={{0,2},{2,0},{4,6},{6,4},{8,10},{10,8},{12,14},{14,12},{1,3},{3,1},... | collective-permute-start | bytes 224264 | tf_op jit(solution)/shard_map/ppermute | solution.py:13
  66.8 8.4 %collective-permute-start.15 = (bf16[16,2336]{1,0:T(8,128)(2,1)S(1)}, bf16[16,2336]{1,0:T(8,128)(2,1)S(1)}, u32[]{:S(2)}, u32[]{:S(2)}) collective-permute-start(bf16[16,2336]{1,0:T(8,128)(2,1)S(1)} %add_convert_fusion.8), channel_id=1, source_target_pairs={{0,8},{2,10},{4,12},{6,14},{8,0},{10,2},{12,4},{14,6},{1,9},{3,11}... | collective-permute-start | bytes 224264 | tf_op jit(solution)/shard_map/ppermute | solution.py:13
  67.8 7.4 %collective-permute-start.13 = (bf16[16,2336]{1,0:T(8,128)(2,1)S(1)}, bf16[16,2336]{1,0:T(8,128)(2,1)S(1)}, u32[]{:S(2)}, u32[]{:S(2)}) collective-permute-start(bf16[16,2336]{1,0:T(8,128)(2,1)S(1)} %add_convert_fusion.9), channel_id=1, source_target_pairs={{0,12},{2,14},{4,8},{6,10},{8,4},{10,6},{12,0},{14,2},{1,13},{3,15... | collective-permute-start | bytes 224264 | tf_op jit(solution)/shard_map/ppermute | solution.py:13
  69.9 5.8 %collective-permute-start.17 = (bf16[16,2336]{1,0:T(8,128)(2,1)S(1)}, bf16[16,2336]{1,0:T(8,128)(2,1)S(1)}, u32[]{:S(2)}, u32[]{:S(2)}) collective-permute-start(bf16[16,2336]{1,0:T(8,128)(2,1)S(1)} %add_convert_fusion.7), channel_id=1, source_target_pairs={{0,4},{2,6},{4,0},{6,2},{8,12},{10,14},{12,8},{14,10},{1,5},{3,7},... | collective-permute-start | bytes 224264 | tf_op jit(solution)/shard_map/ppermute | solution.py:13
  77.1 7.2 %collective-permute-start.24 = (bf16[16,2336]{1,0:T(8,128)(2,1)S(1)}, bf16[16,2336]{1,0:T(8,128)(2,1)S(1)}, u32[]{:S(2)}, u32[]{:S(2)}) collective-permute-start(bf16[16,2336]{1,0:T(8,128)(2,1)S(1)} %get-tuple-element.12), channel_id=1, source_target_pairs={{0,12},{2,14},{4,8},{6,10},{8,4},{10,6},{12,0},{14,2},{1,13},{3,15... | collective-permute-start | bytes 224264 | tf_op jit(solution)/shard_map/ppermute | solution.py:13
  79.1 7.9 %collective-permute-start.22 = (bf16[16,2336]{1,0:T(8,128)(2,1)S(1)}, bf16[16,2336]{1,0:T(8,128)(2,1)S(1)}, u32[]{:S(2)}, u32[]{:S(2)}) collective-permute-start(bf16[16,2336]{1,0:T(8,128)(2,1)S(1)} %get-tuple-element.12), channel_id=1, source_target_pairs={{0,8},{2,10},{4,12},{6,14},{8,0},{10,2},{12,4},{14,6},{1,9},{3,11}... | collective-permute-start | bytes 224264 | tf_op jit(solution)/shard_map/ppermute | solution.py:13
  79.6 8.6 %collective-permute-start.20 = (bf16[16,2336]{1,0:T(8,128)(2,1)S(1)}, bf16[16,2336]{1,0:T(8,128)(2,1)S(1)}, u32[]{:S(2)}, u32[]{:S(2)}) collective-permute-start(bf16[16,2336]{1,0:T(8,128)(2,1)S(1)} %get-tuple-element.12), channel_id=1, source_target_pairs={{0,4},{2,6},{4,0},{6,2},{8,12},{10,14},{12,8},{14,10},{1,5},{3,7},... | collective-permute-start | bytes 224264 | tf_op jit(solution)/shard_map/ppermute | solution.py:13
  81.6 7.5 %collective-permute-start.19 = (bf16[16,2336]{1,0:T(8,128)(2,1)S(1)}, bf16[16,2336]{1,0:T(8,128)(2,1)S(1)}, u32[]{:S(2)}, u32[]{:S(2)}) collective-permute-start(bf16[16,2336]{1,0:T(8,128)(2,1)S(1)} %get-tuple-element.12), channel_id=1, source_target_pairs={{0,2},{2,0},{4,6},{6,4},{8,10},{10,8},{12,14},{14,12},{1,3},{3,1},... | collective-permute-start | bytes 224264 | tf_op jit(solution)/shard_map/ppermute | solution.py:13
  84.3 8.9 %collective-permute-start.25 = (bf16[16,2336]{1,0:T(8,128)(2,1)S(1)}, bf16[16,2336]{1,0:T(8,128)(2,1)S(1)}, u32[]{:S(2)}, u32[]{:S(2)}) collective-permute-start(bf16[16,2336]{1,0:T(8,128)(2,1)S(1)} %collective-permute-done.24), channel_id=1, source_target_pairs={{0,2},{2,0},{4,6},{6,4},{8,10},{10,8},{12,14},{14,12},{1,3},{3,1},... | collective-permute-start | bytes 224264 | tf_op jit(solution)/shard_map/ppermute | solution.py:13
  87.1 6.0 %collective-permute-start.23 = (bf16[16,2336]{1,0:T(8,128)(2,1)S(1)}, bf16[16,2336]{1,0:T(8,128)(2,1)S(1)}, u32[]{:S(2)}, u32[]{:S(2)}) collective-permute-start(bf16[16,2336]{1,0:T(8,128)(2,1)S(1)} %collective-permute-done.22), channel_id=1, source_target_pairs={{0,2},{2,0},{4,6},{6,4},{8,10},{10,8},{12,14},{14,12},{1,3},{3,1},... | collective-permute-start | bytes 224264 | tf_op jit(solution)/shard_map/ppermute | solution.py:13
  88.2 4.9 %collective-permute-start.21 = (bf16[16,2336]{1,0:T(8,128)(2,1)S(1)}, bf16[16,2336]{1,0:T(8,128)(2,1)S(1)}, u32[]{:S(2)}, u32[]{:S(2)}) collective-permute-start(bf16[16,2336]{1,0:T(8,128)(2,1)S(1)} %collective-permute-done.20), channel_id=1, source_target_pairs={{0,2},{2,0},{4,6},{6,4},{8,10},{10,8},{12,14},{14,12},{1,3},{3,1},... | collective-permute-start | bytes 224264 | tf_op jit(solution)/shard_map/ppermute | solution.py:13
  95.4 1.4 collective-permute-start.26
  122.5 11.0 %collective-permute-start.29 = (bf16[16,2336]{1,0:T(8,128)(2,1)S(1)}, bf16[16,2336]{1,0:T(8,128)(2,1)S(1)}, u32[]{:S(2)}, u32[]{:S(2)}) collective-permute-start(bf16[16,2336]{1,0:T(8,128)(2,1)S(1)} %copy.202), channel_id=1, source_target_pairs={{0,2},{2,0},{4,6},{6,4},{8,10},{10,8},{12,14},{14,12},{1,3},{3,1},... | collective-permute-start | bytes 224264 | tf_op jit(solution)/shard_map/ppermute | solution.py:13
  123.7 9.5 %collective-permute-start.31 = (bf16[16,2336]{1,0:T(8,128)(2,1)}, bf16[16,2336]{1,0:T(8,128)(2,1)S(1)}, u32[]{:S(2)}, u32[]{:S(2)}) collective-permute-start(bf16[16,2336]{1,0:T(8,128)(2,1)} %copy.204), channel_id=1, source_target_pairs={{0,2},{2,0},{4,6},{6,4},{8,10},{10,8},{12,14},{14,12},{1,3},{3,1},... | collective-permute-start | bytes 224264 | tf_op jit(solution)/shard_map/ppermute | solution.py:13
  124.6 11.0 %collective-permute-start.33 = (bf16[16,2336]{1,0:T(8,128)(2,1)S(1)}, bf16[16,2336]{1,0:T(8,128)(2,1)S(1)}, u32[]{:S(2)}, u32[]{:S(2)}) collective-permute-start(bf16[16,2336]{1,0:T(8,128)(2,1)S(1)} %copy.206), channel_id=1, source_target_pairs={{0,2},{2,0},{4,6},{6,4},{8,10},{10,8},{12,14},{14,12},{1,3},{3,1},... | collective-permute-start | bytes 224264 | tf_op jit(solution)/shard_map/ppermute | solution.py:13
  125.7 11.6 %collective-permute-start.28 = (bf16[16,2336]{1,0:T(8,128)(2,1)S(1)}, bf16[16,2336]{1,0:T(8,128)(2,1)S(1)}, u32[]{:S(2)}, u32[]{:S(2)}) collective-permute-start(bf16[16,2336]{1,0:T(8,128)(2,1)S(1)} %copy.200), channel_id=1, source_target_pairs={{0,2},{2,0},{4,6},{6,4},{8,10},{10,8},{12,14},{14,12},{1,3},{3,1},... | collective-permute-start | bytes 224264 | tf_op jit(solution)/shard_map/ppermute | solution.py:13
  133.2 7.8 %collective-permute-start.32 = (bf16[16,2336]{1,0:T(8,128)(2,1)S(1)}, bf16[16,2336]{1,0:T(8,128)(2,1)S(1)}, u32[]{:S(2)}, u32[]{:S(2)}) collective-permute-start(bf16[16,2336]{1,0:T(8,128)(2,1)S(1)} %add_convert_fusion.5), channel_id=1, source_target_pairs={{0,8},{2,10},{4,12},{6,14},{8,0},{10,2},{12,4},{14,6},{1,9},{3,11}... | collective-permute-start | bytes 224264 | tf_op jit(solution)/shard_map/ppermute | solution.py:13
  133.6 7.4 %collective-permute-start.30 = (bf16[16,2336]{1,0:T(8,128)(2,1)S(1)}, bf16[16,2336]{1,0:T(8,128)(2,1)S(1)}, u32[]{:S(2)}, u32[]{:S(2)}) collective-permute-start(bf16[16,2336]{1,0:T(8,128)(2,1)S(1)} %add_convert_fusion.6), channel_id=1, source_target_pairs={{0,12},{2,14},{4,8},{6,10},{8,4},{10,6},{12,0},{14,2},{1,13},{3,15... | collective-permute-start | bytes 224264 | tf_op jit(solution)/shard_map/ppermute | solution.py:13
  135.6 5.8 %collective-permute-start.34 = (bf16[16,2336]{1,0:T(8,128)(2,1)S(1)}, bf16[16,2336]{1,0:T(8,128)(2,1)S(1)}, u32[]{:S(2)}, u32[]{:S(2)}) collective-permute-start(bf16[16,2336]{1,0:T(8,128)(2,1)S(1)} %add_convert_fusion.4), channel_id=1, source_target_pairs={{0,4},{2,6},{4,0},{6,2},{8,12},{10,14},{12,8},{14,10},{1,5},{3,7},... | collective-permute-start | bytes 224264 | tf_op jit(solution)/shard_map/ppermute | solution.py:13
  142.9 7.2 %collective-permute-start.41 = (bf16[16,2336]{1,0:T(8,128)(2,1)S(1)}, bf16[16,2336]{1,0:T(8,128)(2,1)S(1)}, u32[]{:S(2)}, u32[]{:S(2)}) collective-permute-start(bf16[16,2336]{1,0:T(8,128)(2,1)S(1)} %get-tuple-element.8), channel_id=1, source_target_pairs={{0,12},{2,14},{4,8},{6,10},{8,4},{10,6},{12,0},{14,2},{1,13},{3,15... | collective-permute-start | bytes 224264 | tf_op jit(solution)/shard_map/ppermute | solution.py:13
  144.9 7.9 %collective-permute-start.39 = (bf16[16,2336]{1,0:T(8,128)(2,1)S(1)}, bf16[16,2336]{1,0:T(8,128)(2,1)S(1)}, u32[]{:S(2)}, u32[]{:S(2)}) collective-permute-start(bf16[16,2336]{1,0:T(8,128)(2,1)S(1)} %get-tuple-element.8), channel_id=1, source_target_pairs={{0,8},{2,10},{4,12},{6,14},{8,0},{10,2},{12,4},{14,6},{1,9},{3,11}... | collective-permute-start | bytes 224264 | tf_op jit(solution)/shard_map/ppermute | solution.py:13
  145.3 8.6 %collective-permute-start.37 = (bf16[16,2336]{1,0:T(8,128)(2,1)S(1)}, bf16[16,2336]{1,0:T(8,128)(2,1)S(1)}, u32[]{:S(2)}, u32[]{:S(2)}) collective-permute-start(bf16[16,2336]{1,0:T(8,128)(2,1)S(1)} %get-tuple-element.8), channel_id=1, source_target_pairs={{0,4},{2,6},{4,0},{6,2},{8,12},{10,14},{12,8},{14,10},{1,5},{3,7},... | collective-permute-start | bytes 224264 | tf_op jit(solution)/shard_map/ppermute | solution.py:13
  147.3 7.5 %collective-permute-start.36 = (bf16[16,2336]{1,0:T(8,128)(2,1)S(1)}, bf16[16,2336]{1,0:T(8,128)(2,1)S(1)}, u32[]{:S(2)}, u32[]{:S(2)}) collective-permute-start(bf16[16,2336]{1,0:T(8,128)(2,1)S(1)} %get-tuple-element.8), channel_id=1, source_target_pairs={{0,2},{2,0},{4,6},{6,4},{8,10},{10,8},{12,14},{14,12},{1,3},{3,1},... | collective-permute-start | bytes 224264 | tf_op jit(solution)/shard_map/ppermute | solution.py:13
  150.0 8.8 %collective-permute-start.42 = (bf16[16,2336]{1,0:T(8,128)(2,1)S(1)}, bf16[16,2336]{1,0:T(8,128)(2,1)S(1)}, u32[]{:S(2)}, u32[]{:S(2)}) collective-permute-start(bf16[16,2336]{1,0:T(8,128)(2,1)S(1)} %collective-permute-done.41), channel_id=1, source_target_pairs={{0,2},{2,0},{4,6},{6,4},{8,10},{10,8},{12,14},{14,12},{1,3},{3,1},... | collective-permute-start | bytes 224264 | tf_op jit(solution)/shard_map/ppermute | solution.py:13
  152.8 6.0 %collective-permute-start.40 = (bf16[16,2336]{1,0:T(8,128)(2,1)S(1)}, bf16[16,2336]{1,0:T(8,128)(2,1)S(1)}, u32[]{:S(2)}, u32[]{:S(2)}) collective-permute-start(bf16[16,2336]{1,0:T(8,128)(2,1)S(1)} %collective-permute-done.39), channel_id=1, source_target_pairs={{0,2},{2,0},{4,6},{6,4},{8,10},{10,8},{12,14},{14,12},{1,3},{3,1},... | collective-permute-start | bytes 224264 | tf_op jit(solution)/shard_map/ppermute | solution.py:13
  154.0 4.9 %collective-permute-start.38 = (bf16[16,2336]{1,0:T(8,128)(2,1)S(1)}, bf16[16,2336]{1,0:T(8,128)(2,1)S(1)}, u32[]{:S(2)}, u32[]{:S(2)}) collective-permute-start(bf16[16,2336]{1,0:T(8,128)(2,1)S(1)} %collective-permute-done.37), channel_id=1, source_target_pairs={{0,2},{2,0},{4,6},{6,4},{8,10},{10,8},{12,14},{14,12},{1,3},{3,1},... | collective-permute-start | bytes 224264 | tf_op jit(solution)/shard_map/ppermute | solution.py:13
  163.9 3.0 %collective-permute-start.43 = (bf16[128,1544]{0,1:T(8,128)(2,1)S(1)}, bf16[128,1544]{0,1:T(8,128)(2,1)S(1)}, u32[]{:S(2)}, u32[]{:S(2)}) collective-permute-start(bf16[128,1544]{0,1:T(8,128)(2,1)S(1)} %get-tuple-element.51), channel_id=1, source_target_pairs={{0,1},{1,0},{2,3},{3,2},{4,5},{5,4},{6,7},{7,6},{8,9},{9,8},{10,11... | collective-permute-start | bytes 1185800 | tf_op jit(solution)/shard_map/ppermute | solution.py:13
  166.3 1.9 collective-permute-start.44
  177.0 11.1 %collective-permute-start.46 = (bf16[16,2336]{1,0:T(8,128)(2,1)}, bf16[16,2336]{1,0:T(8,128)(2,1)S(1)}, u32[]{:S(2)}, u32[]{:S(2)}) collective-permute-start(bf16[16,2336]{1,0:T(8,128)(2,1)} %copy.210), channel_id=1, source_target_pairs={{0,2},{2,0},{4,6},{6,4},{8,10},{10,8},{12,14},{14,12},{1,3},{3,1},... | collective-permute-start | bytes 224264 | tf_op jit(solution)/shard_map/ppermute | solution.py:13
  178.1 9.5 %collective-permute-start.48 = (bf16[16,2336]{1,0:T(8,128)(2,1)S(1)}, bf16[16,2336]{1,0:T(8,128)(2,1)S(1)}, u32[]{:S(2)}, u32[]{:S(2)}) collective-permute-start(bf16[16,2336]{1,0:T(8,128)(2,1)S(1)} %copy.212), channel_id=1, source_target_pairs={{0,2},{2,0},{4,6},{6,4},{8,10},{10,8},{12,14},{14,12},{1,3},{3,1},... | collective-permute-start | bytes 224264 | tf_op jit(solution)/shard_map/ppermute | solution.py:13
  179.0 11.1 %collective-permute-start.50 = (bf16[16,2336]{1,0:T(8,128)(2,1)S(1)}, bf16[16,2336]{1,0:T(8,128)(2,1)S(1)}, u32[]{:S(2)}, u32[]{:S(2)}) collective-permute-start(bf16[16,2336]{1,0:T(8,128)(2,1)S(1)} %copy.214), channel_id=1, source_target_pairs={{0,2},{2,0},{4,6},{6,4},{8,10},{10,8},{12,14},{14,12},{1,3},{3,1},... | collective-permute-start | bytes 224264 | tf_op jit(solution)/shard_map/ppermute | solution.py:13
  180.2 12.9 %collective-permute-start.45 = (bf16[16,2336]{1,0:T(8,128)(2,1)S(1)}, bf16[16,2336]{1,0:T(8,128)(2,1)S(1)}, u32[]{:S(2)}, u32[]{:S(2)}) collective-permute-start(bf16[16,2336]{1,0:T(8,128)(2,1)S(1)} %copy.208), channel_id=1, source_target_pairs={{0,2},{2,0},{4,6},{6,4},{8,10},{10,8},{12,14},{14,12},{1,3},{3,1},... | collective-permute-start | bytes 224264 | tf_op jit(solution)/shard_map/ppermute | solution.py:13
  187.7 8.0 %collective-permute-start.49 = (bf16[16,2336]{1,0:T(8,128)(2,1)S(1)}, bf16[16,2336]{1,0:T(8,128)(2,1)S(1)}, u32[]{:S(2)}, u32[]{:S(2)}) collective-permute-start(bf16[16,2336]{1,0:T(8,128)(2,1)S(1)} %add_convert_fusion.2), channel_id=1, source_target_pairs={{0,8},{2,10},{4,12},{6,14},{8,0},{10,2},{12,4},{14,6},{1,9},{3,11}... | collective-permute-start | bytes 224264 | tf_op jit(solution)/shard_map/ppermute | solution.py:13
  188.1 7.6 %collective-permute-start.47 = (bf16[16,2336]{1,0:T(8,128)(2,1)S(1)}, bf16[16,2336]{1,0:T(8,128)(2,1)S(1)}, u32[]{:S(2)}, u32[]{:S(2)}) collective-permute-start(bf16[16,2336]{1,0:T(8,128)(2,1)S(1)} %add_convert_fusion.3), channel_id=1, source_target_pairs={{0,12},{2,14},{4,8},{6,10},{8,4},{10,6},{12,0},{14,2},{1,13},{3,15... | collective-permute-start | bytes 224264 | tf_op jit(solution)/shard_map/ppermute | solution.py:13
  190.1 5.9 %collective-permute-start.51 = (bf16[16,2336]{1,0:T(8,128)(2,1)S(1)}, bf16[16,2336]{1,0:T(8,128)(2,1)S(1)}, u32[]{:S(2)}, u32[]{:S(2)}) collective-permute-start(bf16[16,2336]{1,0:T(8,128)(2,1)S(1)} %add_convert_fusion.1), channel_id=1, source_target_pairs={{0,4},{2,6},{4,0},{6,2},{8,12},{10,14},{12,8},{14,10},{1,5},{3,7},... | collective-permute-start | bytes 224264 | tf_op jit(solution)/shard_map/ppermute | solution.py:13
  (18 other events, 163.1 us)

commit v2 on v0

v2 whole, which is shorter than its diff:
```python
import jax
import jax.numpy as jnp
from jax import lax
from jax.experimental import pallas as pl
from jax.experimental.pallas import tpu as pltpu
from jax.sharding import PartitionSpec as P

D = 4672
DK = 64
F32 = jnp.float32
BF16 = jnp.bfloat16
VMEM = pl.BlockSpec(memory_space=pltpu.VMEM)
SMEM = pl.BlockSpec(memory_space=pltpu.SMEM)
ANY = pl.BlockSpec(memory_space=pl.ANY)
NT = (((1,), (1,)), ((), ()))


def swap(value, axis, mask, size):
    return lax.ppermute(value, axis, [(i, i ^ mask) for i in range(size)])


def dot(left, right):
    return jnp.dot(left, right, preferred_element_type=F32)


def pieces(total, step):
    starts = list(range(0, total, step))
    if total - starts[-1] < step // 8 and len(starts) > 1:
        starts.pop()
    return [(s, e - s) for s, e in zip(starts, starts[1:] + [total])]


def normalize(stream, gain):
    stream_f = stream.astype(F32)
    squares = jnp.sum(stream_f * stream_f, axis=1, keepdims=True)
    squares = squares + swap(squares, "gy", 1, 2)
    inverse = lax.rsqrt(squares / D + 1e-06)
    return (stream_f * inverse * gain[None, :]).astype(BF16)


def gather_blocks(block):
    blocks = {0: block}
    for mask in (4, 6, 2):
        blocks[mask] = swap(block, "gx", mask, 8)
    blocks[1] = swap(block, "gx", 1, 8)
    for mask in (4, 2, 6):
        blocks[mask ^ 1] = swap(blocks[mask], "gx", 1, 8)
    return [blocks[p] for p in range(8)]


def scatter_sum(kept, sent):
    pairs = {}
    for k in (3, 2, 1, 0):
        pairs[k] = kept[k] + swap(sent[k], "gx", 1, 8).astype(F32)
    total = pairs[0]
    for k in (3, 2, 1):
        total = total + swap(pairs[k].astype(BF16), "gx", 2 * k, 8).astype(F32)
    return total


def store_blocks(result, kept, sent, start, length):
    rows = kept[0].shape[0]
    for k in range(4):
        low = 2 * k * rows
        kept[k][:, start : start + length] = result[low : low + rows]
        sent[k][:, start : start + length] = result[low + rows : low + 2 * rows].astype(BF16)


def block_shapes(rows, width):
    return [jax.ShapeDtypeStruct((rows, width), F32)] * 4 + [
        jax.ShapeDtypeStruct((rows, width), BF16)
    ] * 4


def heads_out_kernel(cuts, first, mine, other, weight, *rest):
    kept, sent, (held, sems) = rest[:4], rest[4:8], rest[8:]
    copies = [
        pltpu.make_async_copy(weight.at[pl.ds(s, n)], held.at[pl.ds(s, n)], sems.at[i])
        for i, (s, n) in enumerate(cuts)
    ]
    for copy in copies:
        copy.start()
    swapped = first[0] == 1
    a, b = mine[...], other[...]
    left = jnp.concatenate([jnp.where(swapped, b, a), jnp.where(swapped, a, b)], axis=0)
    for copy, (s, n) in zip(copies, cuts):
        copy.wait()
        result = lax.dot_general(left, held[pl.ds(s, n), :], NT, preferred_element_type=F32)
        store_blocks(result, kept, sent, s, n)


def heads_out(first, mine, other, weight_t):
    width, depth = weight_t.shape
    cuts = pieces(width, 512)
    outs = pl.pallas_call(
        lambda *refs: heads_out_kernel(cuts, *refs),
        out_shape=block_shapes(mine.shape[0] // 4, width),
        in_specs=[SMEM, VMEM, VMEM, ANY],
        out_specs=[VMEM] * 8,
        scratch_shapes=[
            pltpu.VMEM((width, depth), BF16),
            pltpu.SemaphoreType.DMA((len(cuts),)),
        ],
        compiler_params=pltpu.CompilerParams(vmem_limit_bytes=16 << 20),
        name="heads_out",
    )(first, mine, other, weight_t)
    return outs[:4], outs[4:]


def arranged(first, blocks):
    swapped = first[0] == 1
    low = jnp.concatenate([b[...] for b in blocks[:4]], axis=0)
    high = jnp.concatenate([b[...] for b in blocks[4:]], axis=0)
    return jnp.concatenate([jnp.where(swapped, high, low), jnp.where(swapped, low, high)], axis=0)


def query_kernel(cuts, first, *rest):
    blocks, (weight, mine, other, left, held, sems) = rest[:8], rest[8:]
    copies = [
        pltpu.make_async_copy(weight.at[pl.ds(s, n)], held.at[pl.ds(s, n)], sems.at[i])
        for i, (s, n) in enumerate(cuts)
    ]
    for copy in copies:
        copy.start()
    left[...] = arranged(first, blocks)
    total = None
    for copy, (s, n) in zip(copies, cuts):
        copy.wait()
        part = dot(left[:, s : s + n], held[pl.ds(s, n), :])
        total = part if total is None else total + part
    half = mine.shape[0]
    mine[...] = total[:half]
    other[...] = total[half:]


def query_halves(first, blocks, weight):
    depth, width = weight.shape
    half = 4 * blocks[0].shape[0]
    cuts = pieces(depth, 640)
    return pl.pallas_call(
        lambda *refs: query_kernel(cuts, *refs),
        out_shape=[jax.ShapeDtypeStruct((half, width), F32)] * 2,
        in_specs=[SMEM] + [VMEM] * 8 + [ANY],
        out_specs=[VMEM] * 2,
        scratch_shapes=[
            pltpu.VMEM((2 * half, depth), BF16),
            pltpu.VMEM((depth, width), BF16),
            pltpu.SemaphoreType.DMA((len(cuts),)),
        ],
        compiler_params=pltpu.CompilerParams(vmem_limit_bytes=16 << 20),
        name="query",
    )(first, *blocks, weight)


def gate_up_kernel(cuts, *rest):
    blocks, (gate_w, up_w, gate, up, gate_s, up_s, left, gate_h, up_h, sems) = rest[:8], rest[8:]
    copies = []
    for i, (s, n) in enumerate(cuts):
        for j, (source, held) in enumerate(((gate_w, gate_h), (up_w, up_h))):
            copies.append(
                pltpu.make_async_copy(
                    source.at[pl.ds(s, n)], held.at[pl.ds(s, n)], sems.at[2 * i + j]
                )
            )
    for copy in copies:
        copy.start()
    left[...] = jnp.concatenate([b[...] for b in blocks], axis=0)
    for i, (s, n) in enumerate(cuts):
        for j, (held, full, short) in enumerate(((gate_h, gate, gate_s), (up_h, up, up_s))):
            copies[2 * i + j].wait()
            result = lax.dot_general(
                left[...], held[pl.ds(s, n), :], NT, preferred_element_type=F32
            )
            full[:, s : s + n] = result
            short[:, s : s + n] = result.astype(BF16)


def gate_up(blocks, gate_t, up_t):
    units, depth = gate_t.shape
    rows = 8 * blocks[0].shape[0]
    cuts = pieces(units, 512)
    return pl.pallas_call(
        lambda *refs: gate_up_kernel(cuts, *refs),
        out_shape=[jax.ShapeDtypeStruct((rows, units), F32)] * 2
        + [jax.ShapeDtypeStruct((rows, units), BF16)] * 2,
        in_specs=[VMEM] * 8 + [ANY] * 2,
        out_specs=[VMEM] * 4,
        scratch_shapes=[
            pltpu.VMEM((rows, depth), BF16),
            pltpu.VMEM((units, depth), BF16),
            pltpu.VMEM((units, depth), BF16),
            pltpu.SemaphoreType.DMA((2 * len(cuts),)),
        ],
        compiler_params=pltpu.CompilerParams(vmem_limit_bytes=32 << 20),
        name="gate_up",
    )(*blocks, gate_t, up_t)


def down_kernel(cuts, gate, up, gate_r, up_r, weight, *rest):
    kept, sent, (held, sems) = rest[:4], rest[4:8], rest[8:]
    copies = [
        pltpu.make_async_copy(weight.at[:, pl.ds(s, n)], held.at[:, pl.ds(s, n)], sems.at[i])
        for i, (s, n) in enumerate(cuts)
    ]
    for copy in copies:
        copy.start()
    g = gate[...] + gate_r[...].astype(F32)
    u = up[...] + up_r[...].astype(F32)
    left = (jax.nn.gelu(g, approximate=True) * u).astype(BF16)
    for copy, (s, n) in zip(copies, cuts):
        copy.wait()
        store_blocks(dot(left, held[:, pl.ds(s, n)]), kept, sent, s, n)


def down(gate, up, gate_r, up_r, weight):
    units, width = weight.shape
    cuts = pieces(width, 512)
    outs = pl.pallas_call(
        lambda *refs: down_kernel(cuts, *refs),
        out_shape=block_shapes(gate.shape[0] // 8, width),
        in_specs=[VMEM] * 4 + [ANY],
        out_specs=[VMEM] * 8,
        scratch_shapes=[
            pltpu.VMEM((units, width), BF16),
            pltpu.SemaphoreType.DMA((len(cuts),)),
        ],
        compiler_params=pltpu.CompilerParams(vmem_limit_bytes=32 << 20),
        name="down",
    )(gate, up, gate_r, up_r, weight)
    return outs[:4], outs[4:]


def attend_kernel(own, block, *refs):
    if own:
        low, lengths, query_a, query_b, pair_a, pair_b, keys, values, out = refs[:9]
    else:
        low, query_a, query_b, keys, values, out = refs[:6]
    held_k, held_v, sems = refs[-3:]
    heads, rows, width, slots = held_k.shape
    pairs = heads // 2

    def copies(i):
        both = pl.ds(2 * i, 2)
        return (
            pltpu.make_async_copy(keys.at[both], held_k.at[both], sems.at[0, i]),
            pltpu.make_async_copy(values.at[both], held_v.at[both], sems.at[1, i]),
        )

    for i in range(pairs):
        for copy in copies(i):
            copy.start()
    spread = block * width
    row = lax.broadcasted_iota(jnp.int32, (block, spread), 0)
    lane = lax.broadcasted_iota(jnp.int32, (block, spread), 1)
    diagonal = lane // width == row
    places = [pl.multiple_of((b ^ low[0]) * block, block) for b in range(rows // block)]
    if own:
        lens = jnp.concatenate([lengths[pl.ds(p, block), :] for p in places], axis=0)
        valid = lax.broadcasted_iota(jnp.int32, (rows, slots), 1) < lens

    def step(i, carry):
        cols = pl.ds(pl.multiple_of(i * 2 * width, 2 * width), 2 * width)
        both = (query_a[:, cols] + query_b[:, cols]).astype(BF16)
        for copy in copies(i):
            copy.wait()
        mixes = []
        for e in range(2):
            h = 2 * i + e
            query = both[:, e * width : (e + 1) * width]
            scores = []
            for b, place in enumerate(places):
                some = query[b * block : (b + 1) * block]
                wide = jnp.concatenate([some] * block, axis=1)
                wide = jnp.where(diagonal, wide, jnp.zeros_like(wide))
                key = held_k[h, pl.ds(place, block)].reshape(spread, slots)
                scores.append(dot(wide, key))
            scores = jnp.concatenate(scores, axis=0)
            if own:
                hcols = pl.ds(pl.multiple_of(h * 2 * width, 2 * width), 2 * width)
                new = (pair_a[:, hcols] + pair_b[:, hcols]).astype(BF16).astype(F32)
                own_score = jnp.sum(query.astype(F32) * new[:, :width], axis=1, keepdims=True)
                scores = jnp.where(valid, scores, -1e30)
                top = jnp.maximum(jnp.max(scores, axis=1, keepdims=True), own_score)
                expo = jnp.where(valid, jnp.exp(scores - top), 0.0)
                own_expo = jnp.exp(own_score - top)
                total = jnp.sum(expo, axis=1, keepdims=True) + own_expo
                own_prob = (own_expo / total).astype(BF16).astype(F32)
            else:
                top = jnp.max(scores, axis=1, keepdims=True)
                expo = jnp.exp(scores - top)
                total = jnp.sum(expo, axis=1, keepdims=True)
            probs = (expo / total).astype(BF16)
            mixed = []
            for b, place in enumerate(places):
                value = held_v[h, pl.ds(place, block)].reshape(spread, slots)
                wide = lax.dot_general(
                    probs[b * block : (b + 1) * block], value, NT, preferred_element_type=F32
                )
                wide = jnp.where(diagonal, wide, 0.0)
                tiles = [wide[:, j * 2 * width : (j + 1) * 2 * width] for j in range(block // 2)]
                while len(tiles) > 1:
                    tiles = [a + c for a, c in zip(tiles[::2], tiles[1::2])]
                mixed.append(tiles[0][:, :width] + tiles[0][:, width:])
            mixed = jnp.concatenate(mixed, axis=0)
            if own:
                mixed = mixed + own_prob * new[:, width:]
            mixes.append(mixed)
        out[:, cols] = jnp.concatenate(mixes, axis=1).astype(BF16)
        return carry

    lax.fori_loop(0, pairs, step, 0)


def attend(low, lengths, query, pair, keys, values):
    own = pair is not None
    operands = [low]
    if own:
        operands += [lengths]
    operands += list(query)
    if own:
        operands += list(pair)
    heads, rows, width, slots = keys.shape
    return pl.pallas_call(
        lambda *refs: attend_kernel(own, rows // 4, *refs),
        out_shape=jax.ShapeDtypeStruct((rows, heads * width), BF16),
        in_specs=[SMEM] + [VMEM] * (len(operands) - 1) + [ANY, ANY],
        out_specs=VMEM,
        scratch_shapes=[
            pltpu.VMEM(keys.shape, BF16),
            pltpu.VMEM(values.shape, BF16),
            pltpu.SemaphoreType.DMA((2, heads // 2)),
        ],
        compiler_params=pltpu.CompilerParams(vmem_limit_bytes=32 << 20),
        name="self_attend" if own else "cross_attend",
    )(*operands, keys, values)


def per_device_eight(
    x_in,
    lengths,
    self_gain,
    cross_gain,
    ffn_gain,
    final_gain,
    self_query,
    self_kv,
    self_out,
    cross_query,
    cross_out,
    ffn_gate,
    ffn_up,
    ffn_down,
    self_keys,
    self_values,
    cross_keys,
    cross_values,
):
    index = lax.axis_index("gx")
    first = (lax.axis_index("gy") ^ (index // 4)).astype(jnp.int32).reshape(1)
    low = (index & 3).astype(jnp.int32).reshape(1)
    half = self_keys.shape[1]
    lengths = jnp.broadcast_to(lengths[:, None], (half, self_keys.shape[3]))

    def other_core(value):
        return swap(value, "gy", 1, 2)

    def update(stream, outs):
        return (stream.astype(F32) + scatter_sum(*outs)).astype(BF16)

    def project_heads(stream, heads, weight):
        return update(stream, heads_out(first, heads, other_core(heads), weight.T))

    stream = x_in
    blocks = gather_blocks(normalize(stream, self_gain))
    lower, upper = jnp.concatenate(blocks[:4], axis=0), jnp.concatenate(blocks[4:], axis=0)
    swapped = first[0] == 1
    normed = jnp.concatenate(
        [jnp.where(swapped, upper, lower), jnp.where(swapped, lower, upper)], axis=0
    )
    query_part = dot(normed, self_query)
    pair_part = dot(normed, self_kv.reshape(self_kv.shape[0], -1))
    query = query_part[:half], other_core(query_part[half:])
    pair = pair_part[:half], other_core(pair_part[half:])
    heads = attend(low, lengths, query, pair, self_keys, self_values)
    stream = project_heads(stream, heads, self_out)

    blocks = gather_blocks(normalize(stream, cross_gain))
    mine, other = query_halves(first, blocks, cross_query)
    heads = attend(low, None, (mine, other_core(other)), None, cross_keys, cross_values)
    stream = project_heads(stream, heads, cross_out)

    blocks = gather_blocks(normalize(stream, ffn_gain))
    gate, up, gate_s, up_s = gate_up(blocks, ffn_gate.T, ffn_up.T)
    stream = update(stream, down(gate, up, other_core(gate_s), other_core(up_s), ffn_down))
    return normalize(stream, final_gain)


def softmax_mix(scores, own_score, cache_values, own_value):
    top = jnp.max(scores, axis=2)
    if own_score is not None:
        top = jnp.maximum(top, own_score)
    expo = jnp.exp(scores - top[:, :, None])
    totals = jnp.sum(expo, axis=2)
    if own_score is not None:
        own_expo = jnp.exp(own_score - top)
        totals = totals + own_expo
    probs = (expo / totals[:, :, None]).astype(BF16)
    mixed = jnp.einsum("hbs,hbds->bhd", probs, cache_values, preferred_element_type=F32)
    if own_score is not None:
        own_prob = (own_expo / totals).astype(BF16).T.astype(F32)
        mixed = mixed + own_prob[:, :, None] * own_value.astype(F32)
    return mixed.astype(BF16).reshape(mixed.shape[0], -1)


def per_device_any(
    x_in,
    lengths,
    self_gain,
    cross_gain,
    ffn_gain,
    final_gain,
    self_query,
    self_kv,
    self_out,
    cross_query,
    cross_out,
    ffn_gate,
    ffn_up,
    ffn_down,
    self_keys,
    self_values,
    cross_keys,
    cross_values,
):
    heads_here = self_query.shape[1] // DK
    rows_here = self_keys.shape[1]

    def half_sum(partial):
        total = lax.psum_scatter(partial, "gy", scatter_dimension=0, tiled=True).astype(BF16)
        return total.reshape(rows_here, heads_here, -1)

    def gather(stream, gain):
        return lax.all_gather(normalize(stream, gain), "gx", axis=0, tiled=True)

    def update(stream, left, weight):
        summed = lax.psum_scatter(dot(left, weight), "gx", scatter_dimension=0, tiled=True)
        return (stream.astype(F32) + summed).astype(BF16)

    def both_halves(heads):
        return lax.all_gather(heads, "gy", axis=0, tiled=True)

    def score(query, keys):
        return jnp.einsum("bhd,hbds->hbs", query, keys, preferred_element_type=F32)

    stream = x_in
    normed = gather(stream, self_gain)
    query = half_sum(dot(normed, self_query))
    pair = half_sum(dot(normed, self_kv.reshape(self_kv.shape[0], -1)))
    scores = score(query, self_keys)
    slots = lax.broadcasted_iota(jnp.int32, (1,) + scores.shape[1:], 2)
    scores = jnp.where(slots < lengths[None, :, None], scores, -jnp.inf)
    own_score = jnp.einsum("bhd,bhd->hb", query, pair[:, :, :DK], preferred_element_type=F32)
    heads = softmax_mix(scores, own_score, self_values, pair[:, :, DK:])
    stream = update(stream, both_halves(heads), self_out)

    query = half_sum(dot(gather(stream, cross_gain), cross_query))
    heads = softmax_mix(score(query, cross_keys), None, cross_values, None)
    stream = update(stream, both_halves(heads), cross_out)

    normed = gather(stream, ffn_gain)
    gate, up = dot(normed, ffn_gate), dot(normed, ffn_up)
    gate = gate + swap(gate.astype(BF16), "gy", 1, 2).astype(F32)
    up = up + swap(up.astype(BF16), "gy", 1, 2).astype(F32)
    hidden = (jax.nn.gelu(gate, approximate=True) * up).astype(BF16)
    return normalize(update(stream, hidden, ffn_down), final_gain)


def solution(mesh):
    eight = mesh.shape["gx"] == 8 and mesh.shape["gy"] == 2
    return jax.shard_map(
        per_device_eight if eight else per_device_any,
        mesh=mesh,
        in_specs=(
            P(("groups", "gx"), "gy"),
            P(("groups", "gy")),
            P("gy"),
            P("gy"),
            P("gy"),
            P("gy"),
            P("gy", "gx"),
            P("gy", "gx", None),
            P("gx", "gy"),
            P("gy", "gx"),
            P("gx", "gy"),
            P("gy", "gx"),
            P("gy", "gx"),
            P("gx", "gy"),
            P("gx", ("groups", "gy"), None, None),
            P("gx", ("groups", "gy"), None, None),
            P("gx", ("groups", "gy"), None, None),
            P("gx", ("groups", "gy"), None, None),
        ),
        out_specs=P(("groups", "gx"), "gy"),
        check_vma=False,
    )
```

time: 426 us -> 166 us (0.39)
  waiting for transfers between devices: 232 us -> 51.3 us
  blocking collectives: 111 us -> 0 us
  matrix products: 58.1 us -> 1.35 us
  starting transfers between devices: 0.43 us -> 56 us
  Pallas kernels: 0 us -> 32.3 us
  local copies, waits for them, and re-layouts: 0.88 us -> 20.3 us
  between operations: 13.6 us -> 0.35 us
  other arithmetic: 9.37 us -> 3.91 us
    reduce_scatter x6 -> x0, waiting for transfers between devices: 214 us -> none  [the longest x3 198 us: accumulate(): lax.psum_scatter(jnp.dot(left, weight, preferred_element_type=jnp.float32...]
    all_gather x5 -> x0, blocking collectives: 101 us -> none  [the longest x3 97.2 us: widen(): return lax.all_gather(stream, 'gx', axis=0, tiled=True)]
    dot_general x12 -> x2, matrix products: 58.1 us -> 1.35 us  [dot(): return jnp.dot(left, right, preferred_element_type=F32)]
    ppermute x0 -> x53, starting transfers between devices: none -> 56 us  [swap(): return lax.ppermute(value, axis, [(i, i ^ mask) for i in range(size)])]
    ppermute x0 -> x53, waiting for transfers between devices: none -> 51.3 us  [swap(): return lax.ppermute(value, axis, [(i, i ^ mask) for i in range(size)])]
    pallas_call x0 -> x7, Pallas kernels: none -> 32.3 us  [the longest x2 15.2 us: attend(): pl.pallas_call(lambda *refs: attend_kernel(own, rows // 4, *refs), out_sh...]
    unnamed x19 -> x41, local copies, waits for them, and re-layouts: 0.06 us -> 20.2 us
    psum x1 -> x0, waiting for transfers between devices: 18.3 us -> none  [per_device(): lax.psum(jnp.dot(normed, ffn_gate, preferred_element_type=jnp.float32).as...]
  transfers between devices with their start and end apart: 7 -> 53, of which waited for: 7 -> 38; matrix products, arithmetic and copies ran while one was open for 3% -> 0% of each run, Pallas kernels for 0% -> 0%
where the time goes in v2:
time: 166 us
  starting transfers between devices  56 us (34%)
  waiting for transfers between devices  51.3 us (31%)
  Pallas kernels  32.3 us (19%)
  local copies, waits for them, and re-layouts  20.3 us (12%)
  other arithmetic  3.91 us (2%)
    ppermute x53, starting transfers between devices, swap(): return lax.ppermute(value, axis, [(i, i ^ mask) for i in range(size)])  56 us
    ppermute x53, waiting for transfers between devices, swap(): return lax.ppermute(value, axis, [(i, i ^ mask) for i in range(size)])  51.3 us
    unnamed x41, local copies, waits for them, and re-layouts  20.2 us
    pallas_call x2, Pallas kernels, attend(): pl.pallas_call(lambda *refs: attend_kernel(own, rows // 4, *refs), out_sh...  15.2 us
    pallas_call x1, Pallas kernels, gate_up(): pl.pallas_call(lambda *refs: gate_up_kernel(cuts, *refs), out_shape=[jax....  8.39 us
    pallas_call x1, Pallas kernels, down(): pl.pallas_call(lambda *refs: down_kernel(cuts, *refs), out_shape=block_sh...  3.57 us
    pallas_call x2, Pallas kernels, heads_out(): pl.pallas_call(lambda *refs: heads_out_kernel(cuts, *refs), out_shape=blo...  3.56 us
  transfers between devices with their start and end apart: 53, of which 38 were waited for; matrix products, arithmetic and copies ran while one was open for 0% of the time, Pallas kernels for 0%

profile of v2, /device:TPU:0, one launch (start us, length us, event | category | flops | bytes accessed | tf_op | source)
XLA Modules:
  0.0 165.5 jit_solution(6194445431037926842)
XLA Ops:
  0.0 1.2 fusion.7
  3.5 4.0 %collective-permute-start.1 = (bf16[16,2336]{1,0:T(8,128)(2,1)S(1)}, bf16[16,2336]{1,0:T(8,128)(2,1)S(1)}, u32[]{:S(2)}, u32[]{:S(2)}) collective-permute-start(bf16[16,2336]{1,0:T(8,128)(2,1)S(1)} %fusion.9), channel_id=1, source_target_pairs={{0,8},{2,10},{4,12},{6,14},{8,0},{10,2},{12,4},{14,6},{1,9},{3,11}... | collective-permute-start | bytes 224264 | tf_op jit(solution)/shard_map/ppermute | solution.py:19
  7.4 1.6 collective-permute-start.6
  9.0 1.5 collective-permute-start.5
  11.7 1.8 %collective-permute-start.2 = (bf16[16,2336]{1,0:T(8,128)(2,1)S(1)}, bf16[16,2336]{1,0:T(8,128)(2,1)S(1)}, u32[]{:S(2)}, u32[]{:S(2)}) collective-permute-start(bf16[16,2336]{1,0:T(8,128)(2,1)S(1)} %collective-permute-done.1), channel_id=1, source_target_pairs={{0,2},{2,0},{4,6},{6,4},{8,10},{10,8},{12,14},{14,12},{1,3},{3,1},... | collective-permute-start | bytes 224264 | tf_op jit(solution)/shard_map/ppermute | solution.py:19
  13.8 2.9 %collective-permute-done.3 = bf16[16,2336]{1,0:T(8,128)(2,1)S(1)} collective-permute-done((bf16[16,2336]{1,0:T(8,128)(2,1)S(1)}, bf16[16,2336]{1,0:T(8,128)(2,1)S(1)}, u32[]{:S(2)}, u32[]{:S(2)}) %collective-permute-start.3) | collective-permute-done | bytes 74784 | tf_op jit(solution)/shard_map/ppermute | solution.py:19
  17.3 3.8 %collective-permute-done.4 = bf16[16,2336]{1,0:T(8,128)(2,1)S(1)} collective-permute-done((bf16[16,2336]{1,0:T(8,128)(2,1)S(1)}, bf16[16,2336]{1,0:T(8,128)(2,1)S(1)}, u32[]{:S(2)}, u32[]{:S(2)}) %collective-permute-start.4) | collective-permute-done | bytes 74784 | tf_op jit(solution)/shard_map/ppermute | solution.py:19
  24.6 3.4 %copy-done.2 = bf16[8,64,64,128]{3,2,1,0:T(8,128)(2,1)S(1)} copy-done((bf16[8,64,64,128]{3,2,1,0:T(8,128)(2,1)S(1)}, bf16[8,64,64,128]{3,2,1,0:T(8,128)(2,1)}, u32[]{:S(2)}) %copy-start.2) | copy-done | bytes 8388632
  27.9 3.4 %copy-done.3 = bf16[8,64,64,128]{3,2,1,0:T(8,128)(2,1)S(1)} copy-done((bf16[8,64,64,128]{3,2,1,0:T(8,128)(2,1)S(1)}, bf16[8,64,64,128]{3,2,1,0:T(8,128)(2,1)}, u32[]{:S(2)}) %copy-start.3) | copy-done | bytes 8388632
  31.3 7.8 %self_attend.1.refs_1_ = bf16[64,512]{1,0:T(8,128)(2,1)S(1)} custom-call(s32[1]{0:T(128)} %bitcast.1.refs_0_, s32[64,128]{1,0:T(8,128)S(1)} %broadcast_in_dim.10.refs_1_, f32[64,512]{1,0:T(8,128)S(1)} %get-tuple-element.76.refs_2_, f32[64,512]{1,0:T(8,128)S(1)} %collective-permute-done.8.refs_3_, f32[64,1024]{1,0:T(8,128)S(1)} %get-tuple-element.74.refs_4_, ...), custom_call_target="tpu_custom_call" | custom-call | tf_op jit(solution)/shard_map/self_attend/pallas_call | solution.py:323
  40.5 1.8 %heads_out.2 = (f32[16,2336]{1,0:T(8,128)S(1)}, f32[16,2336]{1,0:T(8,128)S(1)}, f32[16,2336]{1,0:T(8,128)S(1)}, f32[16,2336]{1,0:T(8,128)S(1)}, bf16[16,2336]{1,...) custom-call(s32[1]{0:T(128)} %bitcast.refs_0_, ...), custom_call_target="tpu_custom_call" | custom-call | tf_op jit(solution)/shard_map/heads_out/pallas_call | solution.py:95
  42.9 1.5 collective-permute-start.11
  44.9 1.5 collective-permute-start.16
  46.4 1.1 collective-permute-done.12
  47.6 2.8 %collective-permute-start.13 = (bf16[16,2336]{1,0:T(8,128)(2,1)S(1)}, bf16[16,2336]{1,0:T(8,128)(2,1)S(1)}, u32[]{:S(2)}, u32[]{:S(2)}) collective-permute-start(bf16[16,2336]{1,0:T(8,128)(2,1)S(1)} %add_convert_fusion.8), channel_id=1, source_target_pairs={{0,12},{2,14},{4,8},{6,10},{8,4},{10,6},{12,0},{14,2},{1,13},{3,15... | collective-permute-start | bytes 224264 | tf_op jit(solution)/shard_map/ppermute | solution.py:19
  52.0 2.4 %collective-permute-start.17 = (bf16[16,2336]{1,0:T(8,128)(2,1)S(1)}, bf16[16,2336]{1,0:T(8,128)(2,1)S(1)}, u32[]{:S(2)}, u32[]{:S(2)}) collective-permute-start(bf16[16,2336]{1,0:T(8,128)(2,1)S(1)} %add_convert_fusion.6), channel_id=1, source_target_pairs={{0,4},{2,6},{4,0},{6,2},{8,12},{10,14},{12,8},{14,10},{1,5},{3,7},... | collective-permute-start | bytes 224264 | tf_op jit(solution)/shard_map/ppermute | solution.py:19
  54.5 2.7 %collective-permute-done.15 = bf16[16,2336]{1,0:T(8,128)(2,1)S(1)} collective-permute-done((bf16[16,2336]{1,0:T(8,128)(2,1)S(1)}, bf16[16,2336]{1,0:T(8,128)(2,1)S(1)}, u32[]{:S(2)}, u32[]{:S(2)}) %collective-permute-start.15) | collective-permute-done | bytes 74784 | tf_op jit(solution)/shard_map/ppermute | solution.py:19
  59.0 2.9 %collective-permute-start.24 = (bf16[16,2336]{1,0:T(8,128)(2,1)S(1)}, bf16[16,2336]{1,0:T(8,128)(2,1)S(1)}, u32[]{:S(2)}, u32[]{:S(2)}) collective-permute-start(bf16[16,2336]{1,0:T(8,128)(2,1)S(1)} %fusion.13.refs_1_), channel_id=1, source_target_pairs={{0,12},{2,14},{4,8},{6,10},{8,4},{10,6},{12,0},{14,2},{1,13},{3,15... | collective-permute-start | bytes 224264 | tf_op jit(solution)/shard_map/ppermute | solution.py:19
  61.9 1.6 collective-permute-start.20
  64.2 2.0 %collective-permute-done.24.refs_7_ = bf16[16,2336]{1,0:T(8,128)(2,1)S(1)} collective-permute-done((bf16[16,2336]{1,0:T(8,128)(2,1)S(1)}, bf16[16,2336]{1,0:T(8,128)(2,1)S(1)}, u32[]{:S(2)}, u32[]{:S(2)}) %collective-permute-start.24) | collective-permute-done | bytes 74784 | tf_op jit(solution)/shard_map/ppermute | solution.py:19
  66.9 2.4 %collective-permute-done.22.refs_5_ = bf16[16,2336]{1,0:T(8,128)(2,1)S(1)} collective-permute-done((bf16[16,2336]{1,0:T(8,128)(2,1)S(1)}, bf16[16,2336]{1,0:T(8,128)(2,1)S(1)}, u32[]{:S(2)}, u32[]{:S(2)}) %collective-permute-start.22) | collective-permute-done | bytes 74784 | tf_op jit(solution)/shard_map/ppermute | solution.py:19
  69.2 1.2 collective-permute-start.23
  71.3 2.7 %collective-permute-done.23.refs_6_ = bf16[16,2336]{1,0:T(8,128)(2,1)S(1)} collective-permute-done((bf16[16,2336]{1,0:T(8,128)(2,1)S(1)}, bf16[16,2336]{1,0:T(8,128)(2,1)S(1)}, u32[]{:S(2)}, u32[]{:S(2)}) %collective-permute-start.23) | collective-permute-done | bytes 74784 | tf_op jit(solution)/shard_map/ppermute | solution.py:19
  74.9 1.6 query.1
  76.6 1.3 collective-permute-done.26.refs_2_
  78.0 3.4 %copy-done.4 = bf16[8,64,64,128]{3,2,1,0:T(8,128)(2,1)S(1)} copy-done((bf16[8,64,64,128]{3,2,1,0:T(8,128)(2,1)S(1)}, bf16[8,64,64,128]{3,2,1,0:T(8,128)(2,1)}, u32[]{:S(2)}) %copy-start.4) | copy-done | bytes 8388632
  81.3 3.4 %copy-done.5 = bf16[8,64,64,128]{3,2,1,0:T(8,128)(2,1)S(1)} copy-done((bf16[8,64,64,128]{3,2,1,0:T(8,128)(2,1)S(1)}, bf16[8,64,64,128]{3,2,1,0:T(8,128)(2,1)}, u32[]{:S(2)}) %copy-start.5) | copy-done | bytes 8388632
  84.7 7.4 %cross_attend.1.refs_1_ = bf16[64,512]{1,0:T(8,128)(2,1)S(1)} custom-call(s32[1]{0:T(128)} %bitcast.1.refs_0_, f32[64,512]{1,0:T(8,128)S(1)} %get-tuple-element.43.refs_1_, f32[64,512]{1,0:T(8,128)S(1)} %collective-permute-done.26.refs_2_, bf16[8,64,64,128]{3,2,1,0:T(8,128)(2,1)S(1)} %copy-done.4, bf16[8,64,64,128]{3,2,1,0:T(8,128)(2,1)S(1)} %copy-done.5), custom_call_target="tpu_custom_call" | custom-call | tf_op jit(solution)/shard_map/cross_attend/pallas_call | solution.py:323
  93.4 1.8 %heads_out.3 = (f32[16,2336]{1,0:T(8,128)S(1)}, f32[16,2336]{1,0:T(8,128)S(1)}, f32[16,2336]{1,0:T(8,128)S(1)}, f32[16,2336]{1,0:T(8,128)S(1)}, bf16[16,2336]{1,...) custom-call(s32[1]{0:T(128)} %bitcast.refs_0_, ...), custom_call_target="tpu_custom_call" | custom-call | tf_op jit(solution)/shard_map/heads_out/pallas_call | solution.py:95
  99.3 1.1 collective-permute-done.29
  100.5 2.2 %collective-permute-start.30 = (bf16[16,2336]{1,0:T(8,128)(2,1)S(1)}, bf16[16,2336]{1,0:T(8,128)(2,1)S(1)}, u32[]{:S(2)}, u32[]{:S(2)}) collective-permute-start(bf16[16,2336]{1,0:T(8,128)(2,1)S(1)} %add_convert_fusion.5), channel_id=1, source_target_pairs={{0,12},{2,14},{4,8},{6,10},{8,4},{10,6},{12,0},{14,2},{1,13},{3,15... | collective-permute-start | bytes 224264 | tf_op jit(solution)/shard_map/ppermute | solution.py:19
  104.7 2.0 %collective-permute-start.34 = (bf16[16,2336]{1,0:T(8,128)(2,1)S(1)}, bf16[16,2336]{1,0:T(8,128)(2,1)S(1)}, u32[]{:S(2)}, u32[]{:S(2)}) collective-permute-start(bf16[16,2336]{1,0:T(8,128)(2,1)S(1)} %add_convert_fusion.3), channel_id=1, source_target_pairs={{0,4},{2,6},{4,0},{6,2},{8,12},{10,14},{12,8},{14,10},{1,5},{3,7},... | collective-permute-start | bytes 224264 | tf_op jit(solution)/shard_map/ppermute | solution.py:19
  107.7 2.5 %collective-permute-done.32 = bf16[16,2336]{1,0:T(8,128)(2,1)S(1)} collective-permute-done((bf16[16,2336]{1,0:T(8,128)(2,1)S(1)}, bf16[16,2336]{1,0:T(8,128)(2,1)S(1)}, u32[]{:S(2)}, u32[]{:S(2)}) %collective-permute-start.32) | collective-permute-done | bytes 74784 | tf_op jit(solution)/shard_map/ppermute | solution.py:19
  111.9 2.0 %collective-permute-start.41 = (bf16[16,2336]{1,0:T(8,128)(2,1)S(1)}, bf16[16,2336]{1,0:T(8,128)(2,1)S(1)}, u32[]{:S(2)}, u32[]{:S(2)}) collective-permute-start(bf16[16,2336]{1,0:T(8,128)(2,1)S(1)} %fusion.17.refs_0_), channel_id=1, source_target_pairs={{0,12},{2,14},{4,8},{6,10},{8,4},{10,6},{12,0},{14,2},{1,13},{3,15... | collective-permute-start | bytes 224264 | tf_op jit(solution)/shard_map/ppermute | solution.py:19
  114.1 2.2 %collective-permute-start.37 = (bf16[16,2336]{1,0:T(8,128)(2,1)S(1)}, bf16[16,2336]{1,0:T(8,128)(2,1)S(1)}, u32[]{:S(2)}, u32[]{:S(2)}) collective-permute-start(bf16[16,2336]{1,0:T(8,128)(2,1)S(1)} %fusion.17.refs_0_), channel_id=1, source_target_pairs={{0,4},{2,6},{4,0},{6,2},{8,12},{10,14},{12,8},{14,10},{1,5},{3,7},... | collective-permute-start | bytes 224264 | tf_op jit(solution)/shard_map/ppermute | solution.py:19
  117.4 1.7 %collective-permute-done.41.refs_6_ = bf16[16,2336]{1,0:T(8,128)(2,1)S(1)} collective-permute-done((bf16[16,2336]{1,0:T(8,128)(2,1)S(1)}, bf16[16,2336]{1,0:T(8,128)(2,1)S(1)}, u32[]{:S(2)}, u32[]{:S(2)}) %collective-permute-start.41) | collective-permute-done | bytes 74784 | tf_op jit(solution)/shard_map/ppermute | solution.py:19
  120.1 1.5 collective-permute-done.39.refs_4_
  123.6 3.1 %collective-permute-done.40.refs_5_ = bf16[16,2336]{1,0:T(8,128)(2,1)S(1)} collective-permute-done((bf16[16,2336]{1,0:T(8,128)(2,1)S(1)}, bf16[16,2336]{1,0:T(8,128)(2,1)S(1)}, u32[]{:S(2)}, u32[]{:S(2)}) %collective-permute-start.40) | collective-permute-done | bytes 74784 | tf_op jit(solution)/shard_map/ppermute | solution.py:19
  127.5 3.3 %copy-done.6 = bf16[2336,1544]{0,1:T(8,128)(2,1)S(1)} copy-done((bf16[2336,1544]{0,1:T(8,128)(2,1)S(1)}, bf16[2336,1544]{0,1:T(8,128)(2,1)}, u32[]{:S(2)}) %copy-start.6) | copy-done | bytes 7213592
  130.8 3.2 %copy-done.7 = bf16[2336,1544]{0,1:T(8,128)(2,1)S(1)} copy-done((bf16[2336,1544]{0,1:T(8,128)(2,1)S(1)}, bf16[2336,1544]{0,1:T(8,128)(2,1)}, u32[]{:S(2)}) %copy-start.7) | copy-done | bytes 7213592
  134.1 8.4 %gate_up.1 = (f32[128,1544]{1,0:T(8,128)S(1)}, f32[128,1544]{1,0:T(8,128)S(1)}, bf16[128,1544]{1,0:T(8,128)(2,1)S(1)}, bf16[128,1544]{1,0:T(8,128)(2,1)S(1)}) custom-call(bf16[16,2336]{1,0:T(8,128)(2,1)S(1)} %fusion.17.refs_0_, bf16[16,2336]{1,0:T(8,128)(2,1)S(1)} %collective-permute-done.36.refs_1_, bf16[16,2336]{1,0:T(8,128)(2,1)S(1)} %collective-permute-done.37.refs_2_, ...), custom_call_target="tpu_custom_call" | custom-call | tf_op jit(solution)/shard_map/gate_up/pallas_call | solution.py:182
  143.0 1.3 collective-permute-done.43.refs_2_
  144.9 3.6 %down.1 = (f32[16,2336]{1,0:T(8,128)S(1)}, f32[16,2336]{1,0:T(8,128)S(1)}, f32[16,2336]{1,0:T(8,128)S(1)}, f32[16,2336]{1,0:T(8,128)S(1)}, bf16[16,2336]{1,0:T(8...) custom-call(f32[128,1544]{1,0:T(8,128)S(1)} %get-tuple-element.53.refs_0_, ...), custom_call_target="tpu_custom_call" | custom-call | tf_op jit(solution)/shard_map/down/pallas_call | solution.py:218
  152.6 1.2 collective-permute-done.46
  153.8 2.0 %collective-permute-start.47 = (bf16[16,2336]{1,0:T(8,128)(2,1)S(1)}, bf16[16,2336]{1,0:T(8,128)(2,1)S(1)}, u32[]{:S(2)}, u32[]{:S(2)}) collective-permute-start(bf16[16,2336]{1,0:T(8,128)(2,1)S(1)} %add_convert_fusion.2), channel_id=1, source_target_pairs={{0,12},{2,14},{4,8},{6,10},{8,4},{10,6},{12,0},{14,2},{1,13},{3,15... | collective-permute-start | bytes 224264 | tf_op jit(solution)/shard_map/ppermute | solution.py:19
  155.8 1.4 collective-permute-done.48
  158.0 1.8 %collective-permute-start.51 = (bf16[16,2336]{1,0:T(8,128)(2,1)S(1)}, bf16[16,2336]{1,0:T(8,128)(2,1)S(1)}, u32[]{:S(2)}, u32[]{:S(2)}) collective-permute-start(bf16[16,2336]{1,0:T(8,128)(2,1)S(1)} %add_convert_fusion), channel_id=1, source_target_pairs={{0,4},{2,6},{4,0},{6,2},{8,12},{10,14},{12,8},{14,10},{1,5},{3,7},... | collective-permute-start | bytes 224264 | tf_op jit(solution)/shard_map/ppermute | solution.py:19
  160.2 2.7 %collective-permute-done.49 = bf16[16,2336]{1,0:T(8,128)(2,1)S(1)} collective-permute-done((bf16[16,2336]{1,0:T(8,128)(2,1)S(1)}, bf16[16,2336]{1,0:T(8,128)(2,1)S(1)}, u32[]{:S(2)}, u32[]{:S(2)}) %collective-permute-start.49) | collective-permute-done | bytes 74784 | tf_op jit(solution)/shard_map/ppermute | solution.py:19
  (135 shorter events, 41.4 us)
Async XLA Ops:
  1.2 1.3 collective-permute-start
  3.5 8.2 %collective-permute-start.1 = (bf16[16,2336]{1,0:T(8,128)(2,1)S(1)}, bf16[16,2336]{1,0:T(8,128)(2,1)S(1)}, u32[]{:S(2)}, u32[]{:S(2)}) collective-permute-start(bf16[16,2336]{1,0:T(8,128)(2,1)S(1)} %fusion.9), channel_id=1, source_target_pairs={{0,8},{2,10},{4,12},{6,14},{8,0},{10,2},{12,4},{14,6},{1,9},{3,11}... | collective-permute-start | bytes 224264 | tf_op jit(solution)/shard_map/ppermute | solution.py:19
  7.4 6.1 %collective-permute-start.6 = (bf16[16,2336]{1,0:T(8,128)(2,1)S(1)}, bf16[16,2336]{1,0:T(8,128)(2,1)S(1)}, u32[]{:S(2)}, u32[]{:S(2)}) collective-permute-start(bf16[16,2336]{1,0:T(8,128)(2,1)S(1)} %fusion.9), channel_id=1, source_target_pairs={{0,4},{2,6},{4,0},{6,2},{8,12},{10,14},{12,8},{14,10},{1,5},{3,7},... | collective-permute-start | bytes 224264 | tf_op jit(solution)/shard_map/ppermute | solution.py:19
  9.0 12.1 %collective-permute-start.5 = (bf16[16,2336]{1,0:T(8,128)(2,1)S(1)}, bf16[16,2336]{1,0:T(8,128)(2,1)S(1)}, u32[]{:S(2)}, u32[]{:S(2)}) collective-permute-start(bf16[16,2336]{1,0:T(8,128)(2,1)S(1)} %fusion.9), channel_id=1, source_target_pairs={{0,2},{2,0},{4,6},{6,4},{8,10},{10,8},{12,14},{14,12},{1,3},{3,1},... | collective-permute-start | bytes 224264 | tf_op jit(solution)/shard_map/ppermute | solution.py:19
  10.5 6.2 %collective-permute-start.3 = (bf16[16,2336]{1,0:T(8,128)(2,1)S(1)}, bf16[16,2336]{1,0:T(8,128)(2,1)S(1)}, u32[]{:S(2)}, u32[]{:S(2)}) collective-permute-start(bf16[16,2336]{1,0:T(8,128)(2,1)S(1)} %fusion.9), channel_id=1, source_target_pairs={{0,12},{2,14},{4,8},{6,10},{8,4},{10,6},{12,0},{14,2},{1,13},{3,15... | collective-permute-start | bytes 224264 | tf_op jit(solution)/shard_map/ppermute | solution.py:19
  11.7 5.5 %collective-permute-start.2 = (bf16[16,2336]{1,0:T(8,128)(2,1)S(1)}, bf16[16,2336]{1,0:T(8,128)(2,1)S(1)}, u32[]{:S(2)}, u32[]{:S(2)}) collective-permute-start(bf16[16,2336]{1,0:T(8,128)(2,1)S(1)} %collective-permute-done.1), channel_id=1, source_target_pairs={{0,2},{2,0},{4,6},{6,4},{8,10},{10,8},{12,14},{14,12},{1,3},{3,1},... | collective-permute-start | bytes 224264 | tf_op jit(solution)/shard_map/ppermute | solution.py:19
  13.5 7.6 %collective-permute-start.7 = (bf16[16,2336]{1,0:T(8,128)(2,1)S(1)}, bf16[16,2336]{1,0:T(8,128)(2,1)S(1)}, u32[]{:S(2)}, u32[]{:S(2)}) collective-permute-start(bf16[16,2336]{1,0:T(8,128)(2,1)S(1)} %collective-permute-done.6), channel_id=1, source_target_pairs={{0,2},{2,0},{4,6},{6,4},{8,10},{10,8},{12,14},{14,12},{1,3},{3,1},... | collective-permute-start | bytes 224264 | tf_op jit(solution)/shard_map/ppermute | solution.py:19
  16.7 4.4 %collective-permute-start.4 = (bf16[16,2336]{1,0:T(8,128)(2,1)S(1)}, bf16[16,2336]{1,0:T(8,128)(2,1)S(1)}, u32[]{:S(2)}, u32[]{:S(2)}) collective-permute-start(bf16[16,2336]{1,0:T(8,128)(2,1)S(1)} %collective-permute-done.3), channel_id=1, source_target_pairs={{0,2},{2,0},{4,6},{6,4},{8,10},{10,8},{12,14},{14,12},{1,3},{3,1},... | collective-permute-start | bytes 224264 | tf_op jit(solution)/shard_map/ppermute | solution.py:19
  22.7 1.8 %collective-permute-start.9 = (f32[64,1024]{1,0:T(8,128)S(1)}, f32[64,1024]{1,0:T(8,128)S(1)}, u32[]{:S(2)}, u32[]{:S(2)}) collective-permute-start(f32[64,1024]{1,0:T(8,128)S(1)} %get-tuple-element.73), channel_id=1, source_target_pairs={{0,1},{1,0},{2,3},{3,2},{4,5},{5,4},{6,7},{7,6},{8,9},{9,8},{10,11... | collective-permute-start | bytes 786440 | tf_op jit(solution)/shard_map/ppermute | solution.py:19
  22.8 1.7 %collective-permute-start.8 = (f32[64,512]{1,0:T(8,128)S(1)}, f32[64,512]{1,0:T(8,128)S(1)}, u32[]{:S(2)}, u32[]{:S(2)}) collective-permute-start(f32[64,512]{1,0:T(8,128)S(1)} %get-tuple-element.75), channel_id=1, source_target_pairs={{0,1},{1,0},{2,3},{3,2},{4,5},{5,4},{6,7},{7,6},{8,9},{9,8},{10,11... | collective-permute-start | bytes 393224 | tf_op jit(solution)/shard_map/ppermute | solution.py:19
  42.3 5.3 %collective-permute-start.12 = (bf16[16,2336]{1,0:T(8,128)(2,1)S(1)}, bf16[16,2336]{1,0:T(8,128)(2,1)S(1)}, u32[]{:S(2)}, u32[]{:S(2)}) collective-permute-start(bf16[16,2336]{1,0:T(8,128)(2,1)S(1)} %get-tuple-element.38), channel_id=1, source_target_pairs={{0,2},{2,0},{4,6},{6,4},{8,10},{10,8},{12,14},{14,12},{1,3},{3,1},... | collective-permute-start | bytes 224264 | tf_op jit(solution)/shard_map/ppermute | solution.py:19
  42.9 11.5 %collective-permute-start.11 = (bf16[16,2336]{1,0:T(8,128)(2,1)S(1)}, bf16[16,2336]{1,0:T(8,128)(2,1)S(1)}, u32[]{:S(2)}, u32[]{:S(2)}) collective-permute-start(bf16[16,2336]{1,0:T(8,128)(2,1)S(1)} %get-tuple-element.36), channel_id=1, source_target_pairs={{0,2},{2,0},{4,6},{6,4},{8,10},{10,8},{12,14},{14,12},{1,3},{3,1},... | collective-permute-start | bytes 224264 | tf_op jit(solution)/shard_map/ppermute | solution.py:19
  44.4 6.5 %collective-permute-start.14 = (bf16[16,2336]{1,0:T(8,128)(2,1)S(1)}, bf16[16,2336]{1,0:T(8,128)(2,1)S(1)}, u32[]{:S(2)}, u32[]{:S(2)}) collective-permute-start(bf16[16,2336]{1,0:T(8,128)(2,1)S(1)} %get-tuple-element.40), channel_id=1, source_target_pairs={{0,2},{2,0},{4,6},{6,4},{8,10},{10,8},{12,14},{14,12},{1,3},{3,1},... | collective-permute-start | bytes 224264 | tf_op jit(solution)/shard_map/ppermute | solution.py:19
  44.9 7.0 %collective-permute-start.16 = (bf16[16,2336]{1,0:T(8,128)(2,1)S(1)}, bf16[16,2336]{1,0:T(8,128)(2,1)S(1)}, u32[]{:S(2)}, u32[]{:S(2)}) collective-permute-start(bf16[16,2336]{1,0:T(8,128)(2,1)S(1)} %get-tuple-element.42), channel_id=1, source_target_pairs={{0,2},{2,0},{4,6},{6,4},{8,10},{10,8},{12,14},{14,12},{1,3},{3,1},... | collective-permute-start | bytes 224264 | tf_op jit(solution)/shard_map/ppermute | solution.py:19
  47.6 6.9 %collective-permute-start.13 = (bf16[16,2336]{1,0:T(8,128)(2,1)S(1)}, bf16[16,2336]{1,0:T(8,128)(2,1)S(1)}, u32[]{:S(2)}, u32[]{:S(2)}) collective-permute-start(bf16[16,2336]{1,0:T(8,128)(2,1)S(1)} %add_convert_fusion.8), channel_id=1, source_target_pairs={{0,12},{2,14},{4,8},{6,10},{8,4},{10,6},{12,0},{14,2},{1,13},{3,15... | collective-permute-start | bytes 224264 | tf_op jit(solution)/shard_map/ppermute | solution.py:19
  50.9 6.3 %collective-permute-start.15 = (bf16[16,2336]{1,0:T(8,128)(2,1)S(1)}, bf16[16,2336]{1,0:T(8,128)(2,1)S(1)}, u32[]{:S(2)}, u32[]{:S(2)}) collective-permute-start(bf16[16,2336]{1,0:T(8,128)(2,1)S(1)} %add_convert_fusion.7), channel_id=1, source_target_pairs={{0,8},{2,10},{4,12},{6,14},{8,0},{10,2},{12,4},{14,6},{1,9},{3,11}... | collective-permute-start | bytes 224264 | tf_op jit(solution)/shard_map/ppermute | solution.py:19
  52.0 5.5 %collective-permute-start.17 = (bf16[16,2336]{1,0:T(8,128)(2,1)S(1)}, bf16[16,2336]{1,0:T(8,128)(2,1)S(1)}, u32[]{:S(2)}, u32[]{:S(2)}) collective-permute-start(bf16[16,2336]{1,0:T(8,128)(2,1)S(1)} %add_convert_fusion.6), channel_id=1, source_target_pairs={{0,4},{2,6},{4,0},{6,2},{8,12},{10,14},{12,8},{14,10},{1,5},{3,7},... | collective-permute-start | bytes 224264 | tf_op jit(solution)/shard_map/ppermute | solution.py:19
  59.0 7.2 %collective-permute-start.24 = (bf16[16,2336]{1,0:T(8,128)(2,1)S(1)}, bf16[16,2336]{1,0:T(8,128)(2,1)S(1)}, u32[]{:S(2)}, u32[]{:S(2)}) collective-permute-start(bf16[16,2336]{1,0:T(8,128)(2,1)S(1)} %fusion.13.refs_1_), channel_id=1, source_target_pairs={{0,12},{2,14},{4,8},{6,10},{8,4},{10,6},{12,0},{14,2},{1,13},{3,15... | collective-permute-start | bytes 224264 | tf_op jit(solution)/shard_map/ppermute | solution.py:19
  61.9 7.4 %collective-permute-start.22 = (bf16[16,2336]{1,0:T(8,128)(2,1)S(1)}, bf16[16,2336]{1,0:T(8,128)(2,1)S(1)}, u32[]{:S(2)}, u32[]{:S(2)}) collective-permute-start(bf16[16,2336]{1,0:T(8,128)(2,1)S(1)} %fusion.13.refs_1_), channel_id=1, source_target_pairs={{0,8},{2,10},{4,12},{6,14},{8,0},{10,2},{12,4},{14,6},{1,9},{3,11}... | collective-permute-start | bytes 224264 | tf_op jit(solution)/shard_map/ppermute | solution.py:19
  61.9 8.6 %collective-permute-start.20 = (bf16[16,2336]{1,0:T(8,128)(2,1)S(1)}, bf16[16,2336]{1,0:T(8,128)(2,1)S(1)}, u32[]{:S(2)}, u32[]{:S(2)}) collective-permute-start(bf16[16,2336]{1,0:T(8,128)(2,1)S(1)} %fusion.13.refs_1_), channel_id=1, source_target_pairs={{0,4},{2,6},{4,0},{6,2},{8,12},{10,14},{12,8},{14,10},{1,5},{3,7},... | collective-permute-start | bytes 224264 | tf_op jit(solution)/shard_map/ppermute | solution.py:19
  63.4 7.8 %collective-permute-start.19 = (bf16[16,2336]{1,0:T(8,128)(2,1)S(1)}, bf16[16,2336]{1,0:T(8,128)(2,1)S(1)}, u32[]{:S(2)}, u32[]{:S(2)}) collective-permute-start(bf16[16,2336]{1,0:T(8,128)(2,1)S(1)} %fusion.13.refs_1_), channel_id=1, source_target_pairs={{0,2},{2,0},{4,6},{6,4},{8,10},{10,8},{12,14},{14,12},{1,3},{3,1},... | collective-permute-start | bytes 224264 | tf_op jit(solution)/shard_map/ppermute | solution.py:19
  66.1 5.1 %collective-permute-start.25 = (bf16[16,2336]{1,0:T(8,128)(2,1)S(1)}, bf16[16,2336]{1,0:T(8,128)(2,1)S(1)}, u32[]{:S(2)}, u32[]{:S(2)}) collective-permute-start(bf16[16,2336]{1,0:T(8,128)(2,1)S(1)} %collective-permute-done.24.refs_7_), channel_id=1, source_target_pairs={{0,2},{2,0},{4,6},{6,4},{8,10},{10,8},{12,14},{14,12},{1,3},{3,1},... | collective-permute-start | bytes 224264 | tf_op jit(solution)/shard_map/ppermute | solution.py:19
  69.2 4.7 %collective-permute-start.23 = (bf16[16,2336]{1,0:T(8,128)(2,1)S(1)}, bf16[16,2336]{1,0:T(8,128)(2,1)S(1)}, u32[]{:S(2)}, u32[]{:S(2)}) collective-permute-start(bf16[16,2336]{1,0:T(8,128)(2,1)S(1)} %collective-permute-done.22.refs_5_), channel_id=1, source_target_pairs={{0,2},{2,0},{4,6},{6,4},{8,10},{10,8},{12,14},{14,12},{1,3},{3,1},... | collective-permute-start | bytes 224264 | tf_op jit(solution)/shard_map/ppermute | solution.py:19
  70.5 4.4 %collective-permute-start.21 = (bf16[16,2336]{1,0:T(8,128)(2,1)S(1)}, bf16[16,2336]{1,0:T(8,128)(2,1)S(1)}, u32[]{:S(2)}, u32[]{:S(2)}) collective-permute-start(bf16[16,2336]{1,0:T(8,128)(2,1)S(1)} %collective-permute-done.20.refs_3_), channel_id=1, source_target_pairs={{0,2},{2,0},{4,6},{6,4},{8,10},{10,8},{12,14},{14,12},{1,3},{3,1},... | collective-permute-start | bytes 224264 | tf_op jit(solution)/shard_map/ppermute | solution.py:19
  76.5 1.4 collective-permute-start.26
  95.2 5.3 %collective-permute-start.29 = (bf16[16,2336]{1,0:T(8,128)(2,1)S(1)}, bf16[16,2336]{1,0:T(8,128)(2,1)S(1)}, u32[]{:S(2)}, u32[]{:S(2)}) collective-permute-start(bf16[16,2336]{1,0:T(8,128)(2,1)S(1)} %get-tuple-element.48), channel_id=1, source_target_pairs={{0,2},{2,0},{4,6},{6,4},{8,10},{10,8},{12,14},{14,12},{1,3},{3,1},... | collective-permute-start | bytes 224264 | tf_op jit(solution)/shard_map/ppermute | solution.py:19
  96.3 10.4 %collective-permute-start.28 = (bf16[16,2336]{1,0:T(8,128)(2,1)S(1)}, bf16[16,2336]{1,0:T(8,128)(2,1)S(1)}, u32[]{:S(2)}, u32[]{:S(2)}) collective-permute-start(bf16[16,2336]{1,0:T(8,128)(2,1)S(1)} %get-tuple-element.46), channel_id=1, source_target_pairs={{0,2},{2,0},{4,6},{6,4},{8,10},{10,8},{12,14},{14,12},{1,3},{3,1},... | collective-permute-start | bytes 224264 | tf_op jit(solution)/shard_map/ppermute | solution.py:19
  97.3 6.5 %collective-permute-start.31 = (bf16[16,2336]{1,0:T(8,128)(2,1)S(1)}, bf16[16,2336]{1,0:T(8,128)(2,1)S(1)}, u32[]{:S(2)}, u32[]{:S(2)}) collective-permute-start(bf16[16,2336]{1,0:T(8,128)(2,1)S(1)} %get-tuple-element.50), channel_id=1, source_target_pairs={{0,2},{2,0},{4,6},{6,4},{8,10},{10,8},{12,14},{14,12},{1,3},{3,1},... | collective-permute-start | bytes 224264 | tf_op jit(solution)/shard_map/ppermute | solution.py:19
  98.3 6.4 %collective-permute-start.33 = (bf16[16,2336]{1,0:T(8,128)(2,1)S(1)}, bf16[16,2336]{1,0:T(8,128)(2,1)S(1)}, u32[]{:S(2)}, u32[]{:S(2)}) collective-permute-start(bf16[16,2336]{1,0:T(8,128)(2,1)S(1)} %get-tuple-element.52), channel_id=1, source_target_pairs={{0,2},{2,0},{4,6},{6,4},{8,10},{10,8},{12,14},{14,12},{1,3},{3,1},... | collective-permute-start | bytes 224264 | tf_op jit(solution)/shard_map/ppermute | solution.py:19
  100.5 7.1 %collective-permute-start.30 = (bf16[16,2336]{1,0:T(8,128)(2,1)S(1)}, bf16[16,2336]{1,0:T(8,128)(2,1)S(1)}, u32[]{:S(2)}, u32[]{:S(2)}) collective-permute-start(bf16[16,2336]{1,0:T(8,128)(2,1)S(1)} %add_convert_fusion.5), channel_id=1, source_target_pairs={{0,12},{2,14},{4,8},{6,10},{8,4},{10,6},{12,0},{14,2},{1,13},{3,15... | collective-permute-start | bytes 224264 | tf_op jit(solution)/shard_map/ppermute | solution.py:19
  103.9 6.3 %collective-permute-start.32 = (bf16[16,2336]{1,0:T(8,128)(2,1)S(1)}, bf16[16,2336]{1,0:T(8,128)(2,1)S(1)}, u32[]{:S(2)}, u32[]{:S(2)}) collective-permute-start(bf16[16,2336]{1,0:T(8,128)(2,1)S(1)} %add_convert_fusion.4), channel_id=1, source_target_pairs={{0,8},{2,10},{4,12},{6,14},{8,0},{10,2},{12,4},{14,6},{1,9},{3,11}... | collective-permute-start | bytes 224264 | tf_op jit(solution)/shard_map/ppermute | solution.py:19
  104.7 5.7 %collective-permute-start.34 = (bf16[16,2336]{1,0:T(8,128)(2,1)S(1)}, bf16[16,2336]{1,0:T(8,128)(2,1)S(1)}, u32[]{:S(2)}, u32[]{:S(2)}) collective-permute-start(bf16[16,2336]{1,0:T(8,128)(2,1)S(1)} %add_convert_fusion.3), channel_id=1, source_target_pairs={{0,4},{2,6},{4,0},{6,2},{8,12},{10,14},{12,8},{14,10},{1,5},{3,7},... | collective-permute-start | bytes 224264 | tf_op jit(solution)/shard_map/ppermute | solution.py:19
  111.9 7.2 %collective-permute-start.41 = (bf16[16,2336]{1,0:T(8,128)(2,1)S(1)}, bf16[16,2336]{1,0:T(8,128)(2,1)S(1)}, u32[]{:S(2)}, u32[]{:S(2)}) collective-permute-start(bf16[16,2336]{1,0:T(8,128)(2,1)S(1)} %fusion.17.refs_0_), channel_id=1, source_target_pairs={{0,12},{2,14},{4,8},{6,10},{8,4},{10,6},{12,0},{14,2},{1,13},{3,15... | collective-permute-start | bytes 224264 | tf_op jit(solution)/shard_map/ppermute | solution.py:19
  113.9 7.7 %collective-permute-start.39 = (bf16[16,2336]{1,0:T(8,128)(2,1)S(1)}, bf16[16,2336]{1,0:T(8,128)(2,1)S(1)}, u32[]{:S(2)}, u32[]{:S(2)}) collective-permute-start(bf16[16,2336]{1,0:T(8,128)(2,1)S(1)} %fusion.17.refs_0_), channel_id=1, source_target_pairs={{0,8},{2,10},{4,12},{6,14},{8,0},{10,2},{12,4},{14,6},{1,9},{3,11}... | collective-permute-start | bytes 224264 | tf_op jit(solution)/shard_map/ppermute | solution.py:19
  114.1 8.5 %collective-permute-start.37 = (bf16[16,2336]{1,0:T(8,128)(2,1)S(1)}, bf16[16,2336]{1,0:T(8,128)(2,1)S(1)}, u32[]{:S(2)}, u32[]{:S(2)}) collective-permute-start(bf16[16,2336]{1,0:T(8,128)(2,1)S(1)} %fusion.17.refs_0_), channel_id=1, source_target_pairs={{0,4},{2,6},{4,0},{6,2},{8,12},{10,14},{12,8},{14,10},{1,5},{3,7},... | collective-permute-start | bytes 224264 | tf_op jit(solution)/shard_map/ppermute | solution.py:19
  116.4 7.2 %collective-permute-start.36 = (bf16[16,2336]{1,0:T(8,128)(2,1)S(1)}, bf16[16,2336]{1,0:T(8,128)(2,1)S(1)}, u32[]{:S(2)}, u32[]{:S(2)}) collective-permute-start(bf16[16,2336]{1,0:T(8,128)(2,1)S(1)} %fusion.17.refs_0_), channel_id=1, source_target_pairs={{0,2},{2,0},{4,6},{6,4},{8,10},{10,8},{12,14},{14,12},{1,3},{3,1},... | collective-permute-start | bytes 224264 | tf_op jit(solution)/shard_map/ppermute | solution.py:19
  119.1 4.5 %collective-permute-start.42 = (bf16[16,2336]{1,0:T(8,128)(2,1)S(1)}, bf16[16,2336]{1,0:T(8,128)(2,1)S(1)}, u32[]{:S(2)}, u32[]{:S(2)}) collective-permute-start(bf16[16,2336]{1,0:T(8,128)(2,1)S(1)} %collective-permute-done.41.refs_6_), channel_id=1, source_target_pairs={{0,2},{2,0},{4,6},{6,4},{8,10},{10,8},{12,14},{14,12},{1,3},{3,1},... | collective-permute-start | bytes 224264 | tf_op jit(solution)/shard_map/ppermute | solution.py:19
  121.6 5.1 %collective-permute-start.40 = (bf16[16,2336]{1,0:T(8,128)(2,1)S(1)}, bf16[16,2336]{1,0:T(8,128)(2,1)S(1)}, u32[]{:S(2)}, u32[]{:S(2)}) collective-permute-start(bf16[16,2336]{1,0:T(8,128)(2,1)S(1)} %collective-permute-done.39.refs_4_), channel_id=1, source_target_pairs={{0,2},{2,0},{4,6},{6,4},{8,10},{10,8},{12,14},{14,12},{1,3},{3,1},... | collective-permute-start | bytes 224264 | tf_op jit(solution)/shard_map/ppermute | solution.py:19
  122.6 4.9 %collective-permute-start.38 = (bf16[16,2336]{1,0:T(8,128)(2,1)S(1)}, bf16[16,2336]{1,0:T(8,128)(2,1)S(1)}, u32[]{:S(2)}, u32[]{:S(2)}) collective-permute-start(bf16[16,2336]{1,0:T(8,128)(2,1)S(1)} %collective-permute-done.37.refs_2_), channel_id=1, source_target_pairs={{0,2},{2,0},{4,6},{6,4},{8,10},{10,8},{12,14},{14,12},{1,3},{3,1},... | collective-permute-start | bytes 224264 | tf_op jit(solution)/shard_map/ppermute | solution.py:19
  142.5 1.8 %collective-permute-start.43 = (bf16[128,1544]{1,0:T(8,128)(2,1)S(1)}, bf16[128,1544]{1,0:T(8,128)(2,1)S(1)}, u32[]{:S(2)}, u32[]{:S(2)}) collective-permute-start(bf16[128,1544]{1,0:T(8,128)(2,1)S(1)} %get-tuple-element.55), channel_id=1, source_target_pairs={{0,1},{1,0},{2,3},{3,2},{4,5},{5,4},{6,7},{7,6},{8,9},{9,8},{10,11... | collective-permute-start | bytes 1185800 | tf_op jit(solution)/shard_map/ppermute | solution.py:19
  142.6 2.4 %collective-permute-start.44 = (bf16[128,1544]{1,0:T(8,128)(2,1)S(1)}, bf16[128,1544]{1,0:T(8,128)(2,1)S(1)}, u32[]{:S(2)}, u32[]{:S(2)}) collective-permute-start(bf16[128,1544]{1,0:T(8,128)(2,1)S(1)} %get-tuple-element.56), channel_id=1, source_target_pairs={{0,1},{1,0},{2,3},{3,2},{4,5},{5,4},{6,7},{7,6},{8,9},{9,8},{10,11... | collective-permute-start | bytes 1185800 | tf_op jit(solution)/shard_map/ppermute | solution.py:19
  148.5 5.3 %collective-permute-start.46 = (bf16[16,2336]{1,0:T(8,128)(2,1)S(1)}, bf16[16,2336]{1,0:T(8,128)(2,1)S(1)}, u32[]{:S(2)}, u32[]{:S(2)}) collective-permute-start(bf16[16,2336]{1,0:T(8,128)(2,1)S(1)} %get-tuple-element.60), channel_id=1, source_target_pairs={{0,2},{2,0},{4,6},{6,4},{8,10},{10,8},{12,14},{14,12},{1,3},{3,1},... | collective-permute-start | bytes 224264 | tf_op jit(solution)/shard_map/ppermute | solution.py:19
  149.6 10.2 %collective-permute-start.45 = (bf16[16,2336]{1,0:T(8,128)(2,1)S(1)}, bf16[16,2336]{1,0:T(8,128)(2,1)S(1)}, u32[]{:S(2)}, u32[]{:S(2)}) collective-permute-start(bf16[16,2336]{1,0:T(8,128)(2,1)S(1)} %get-tuple-element.58), channel_id=1, source_target_pairs={{0,2},{2,0},{4,6},{6,4},{8,10},{10,8},{12,14},{14,12},{1,3},{3,1},... | collective-permute-start | bytes 224264 | tf_op jit(solution)/shard_map/ppermute | solution.py:19
  150.6 6.5 %collective-permute-start.48 = (bf16[16,2336]{1,0:T(8,128)(2,1)S(1)}, bf16[16,2336]{1,0:T(8,128)(2,1)S(1)}, u32[]{:S(2)}, u32[]{:S(2)}) collective-permute-start(bf16[16,2336]{1,0:T(8,128)(2,1)S(1)} %get-tuple-element.62), channel_id=1, source_target_pairs={{0,2},{2,0},{4,6},{6,4},{8,10},{10,8},{12,14},{14,12},{1,3},{3,1},... | collective-permute-start | bytes 224264 | tf_op jit(solution)/shard_map/ppermute | solution.py:19
  151.6 6.3 %collective-permute-start.50 = (bf16[16,2336]{1,0:T(8,128)(2,1)S(1)}, bf16[16,2336]{1,0:T(8,128)(2,1)S(1)}, u32[]{:S(2)}, u32[]{:S(2)}) collective-permute-start(bf16[16,2336]{1,0:T(8,128)(2,1)S(1)} %get-tuple-element.64), channel_id=1, source_target_pairs={{0,2},{2,0},{4,6},{6,4},{8,10},{10,8},{12,14},{14,12},{1,3},{3,1},... | collective-permute-start | bytes 224264 | tf_op jit(solution)/shard_map/ppermute | solution.py:19
  153.8 6.4 %collective-permute-start.47 = (bf16[16,2336]{1,0:T(8,128)(2,1)S(1)}, bf16[16,2336]{1,0:T(8,128)(2,1)S(1)}, u32[]{:S(2)}, u32[]{:S(2)}) collective-permute-start(bf16[16,2336]{1,0:T(8,128)(2,1)S(1)} %add_convert_fusion.2), channel_id=1, source_target_pairs={{0,12},{2,14},{4,8},{6,10},{8,4},{10,6},{12,0},{14,2},{1,13},{3,15... | collective-permute-start | bytes 224264 | tf_op jit(solution)/shard_map/ppermute | solution.py:19
  157.1 5.7 %collective-permute-start.49 = (bf16[16,2336]{1,0:T(8,128)(2,1)S(1)}, bf16[16,2336]{1,0:T(8,128)(2,1)S(1)}, u32[]{:S(2)}, u32[]{:S(2)}) collective-permute-start(bf16[16,2336]{1,0:T(8,128)(2,1)S(1)} %add_convert_fusion.1), channel_id=1, source_target_pairs={{0,8},{2,10},{4,12},{6,14},{8,0},{10,2},{12,4},{14,6},{1,9},{3,11}... | collective-permute-start | bytes 224264 | tf_op jit(solution)/shard_map/ppermute | solution.py:19
  158.0 5.4 %collective-permute-start.51 = (bf16[16,2336]{1,0:T(8,128)(2,1)S(1)}, bf16[16,2336]{1,0:T(8,128)(2,1)S(1)}, u32[]{:S(2)}, u32[]{:S(2)}) collective-permute-start(bf16[16,2336]{1,0:T(8,128)(2,1)S(1)} %add_convert_fusion), channel_id=1, source_target_pairs={{0,4},{2,6},{4,0},{6,2},{8,12},{10,14},{12,8},{14,10},{1,5},{3,7},... | collective-permute-start | bytes 224264 | tf_op jit(solution)/shard_map/ppermute | solution.py:19
  (24 other events, 234.8 us)

commit v3 on v2

v3 whole, which is shorter than its diff:
```python
import jax
import jax.numpy as jnp
from jax import lax
from jax.experimental import pallas as pl
from jax.experimental.pallas import tpu as pltpu
from jax.sharding import PartitionSpec as P

D = 4672
DK = 64
F32 = jnp.float32
BF16 = jnp.bfloat16
VMEM = pl.BlockSpec(memory_space=pltpu.VMEM)
NT = (((1,), (1,)), ((), ()))


def swap(value, axis, mask, size):
    return lax.ppermute(value, axis, [(i, i ^ mask) for i in range(size)])


def dot(left, right):
    return jnp.dot(left, right, preferred_element_type=F32)


def pieces(total, step):
    starts = list(range(0, total, step))
    if total - starts[-1] < step // 8 and len(starts) > 1:
        starts.pop()
    return [(s, e - s) for s, e in zip(starts, starts[1:] + [total])]


def norm_kernel(stream, mine, other, gain, out):
    inverse = lax.rsqrt((mine[...] + other[...]) / D + 1e-06)
    out[...] = (stream[...].astype(F32) * inverse * gain[...]).astype(BF16)


def norm_ahead(stream, gain):
    stream_f = stream.astype(F32)
    squares = jnp.sum(stream_f * stream_f, axis=1, keepdims=True)
    return pl.pallas_call(
        norm_kernel,
        out_shape=jax.ShapeDtypeStruct(stream.shape, BF16),
        in_specs=[VMEM] * 4,
        out_specs=VMEM,
        compiler_params=pltpu.CompilerParams(vmem_limit_bytes=2 << 20),
        cost_estimate=pl.CostEstimate(flops=30_000_000_000, bytes_accessed=60 << 20, transcendentals=0),
        name="norm",
    )(stream, squares, swap(squares, "gy", 1, 2), gain[None, :])


def normalize(stream, gain):
    stream_f = stream.astype(F32)
    squares = jnp.sum(stream_f * stream_f, axis=1, keepdims=True)
    squares = squares + swap(squares, "gy", 1, 2)
    inverse = lax.rsqrt(squares / D + 1e-06)
    return (stream_f * inverse * gain[None, :]).astype(BF16)


def gather_blocks(block):
    blocks = {0: block}
    for mask in (4, 6, 2):
        blocks[mask] = swap(block, "gx", mask, 8)
    blocks[1] = swap(block, "gx", 1, 8)
    for mask in (4, 2, 6):
        blocks[mask ^ 1] = swap(blocks[mask], "gx", 1, 8)
    return [blocks[p] for p in range(8)]


def scatter_sum(kept, sent):
    pairs = {}
    for k in (3, 2, 1, 0):
        pairs[k] = kept[k] + swap(sent[k], "gx", 1, 8).astype(F32)
    total = pairs[0]
    for k in (3, 2, 1):
        total = total + swap(pairs[k].astype(BF16), "gx", 2 * k, 8).astype(F32)
    return total


def store_blocks(result, kept, sent, start, length):
    rows = kept[0].shape[0]
    for k in range(4):
        low = 2 * k * rows
        kept[k][:, start : start + length] = result[low : low + rows]
        sent[k][:, start : start + length] = result[low + rows : low + 2 * rows].astype(BF16)


def block_shapes(rows, width):
    return [jax.ShapeDtypeStruct((rows, width), F32)] * 4 + [
        jax.ShapeDtypeStruct((rows, width), BF16)
    ] * 4


def upper_half_mine():
    return (lax.axis_index("gy") ^ (lax.axis_index("gx") // 4)) == 1


def heads_out_kernel(cuts, mine, other, weight, *rest):
    kept, sent = rest[:4], rest[4:8]
    swapped = upper_half_mine()
    a, b = mine[...], other[...]
    left = jnp.concatenate([jnp.where(swapped, b, a), jnp.where(swapped, a, b)], axis=0)
    for s, n in cuts:
        result = lax.dot_general(left, weight[s : s + n, :], NT, preferred_element_type=F32)
        store_blocks(result, kept, sent, s, n)


def heads_out(mine, other, weight_t):
    width = weight_t.shape[0]
    cuts = pieces(width, 512)
    outs = pl.pallas_call(
        lambda *refs: heads_out_kernel(cuts, *refs),
        out_shape=block_shapes(mine.shape[0] // 4, width),
        in_specs=[VMEM] * 3,
        out_specs=[VMEM] * 8,
        compiler_params=pltpu.CompilerParams(vmem_limit_bytes=12 << 20),
        name="heads_out",
    )(mine, other, weight_t)
    return outs[:4], outs[4:]


def arranged(blocks):
    swapped = upper_half_mine()
    low = jnp.concatenate([b[...] for b in blocks[:4]], axis=0)
    high = jnp.concatenate([b[...] for b in blocks[4:]], axis=0)
    return jnp.concatenate([jnp.where(swapped, high, low), jnp.where(swapped, low, high)], axis=0)


def arrange_kernel(*refs):
    refs[8][...] = arranged(refs[:8])


def arrange(blocks):
    rows, width = blocks[0].shape
    return pl.pallas_call(
        arrange_kernel,
        out_shape=jax.ShapeDtypeStruct((8 * rows, width), BF16),
        in_specs=[VMEM] * 8,
        out_specs=VMEM,
        compiler_params=pltpu.CompilerParams(vmem_limit_bytes=4 << 20),
        name="arrange",
    )(*blocks)


def query_kernel(*refs):
    weight, mine, other = refs[8:]
    total = dot(arranged(refs[:8]), weight[...])
    half = mine.shape[0]
    mine[...] = total[:half]
    other[...] = total[half:]


def query_halves(blocks, weight):
    half = 4 * blocks[0].shape[0]
    return pl.pallas_call(
        query_kernel,
        out_shape=[jax.ShapeDtypeStruct((half, weight.shape[1]), F32)] * 2,
        in_specs=[VMEM] * 9,
        out_specs=[VMEM] * 2,
        compiler_params=pltpu.CompilerParams(vmem_limit_bytes=12 << 20),
        name="query",
    )(*blocks, weight)


def gate_up_kernel(cuts, *refs):
    blocks, (gate_w, up_w, gate, up, gate_s, up_s) = refs[:8], refs[8:]
    left = jnp.concatenate([b[...] for b in blocks], axis=0)
    for weight, full, short in ((gate_w, gate, gate_s), (up_w, up, up_s)):
        for s, n in cuts:
            result = lax.dot_general(left, weight[s : s + n, :], NT, preferred_element_type=F32)
            full[:, s : s + n] = result
            short[:, s : s + n] = result.astype(BF16)


def gate_up(blocks, gate_t, up_t):
    units = gate_t.shape[0]
    rows = 8 * blocks[0].shape[0]
    cuts = pieces(units, 256)
    return pl.pallas_call(
        lambda *refs: gate_up_kernel(cuts, *refs),
        out_shape=[jax.ShapeDtypeStruct((rows, units), F32)] * 2
        + [jax.ShapeDtypeStruct((rows, units), BF16)] * 2,
        in_specs=[VMEM] * 10,
        out_specs=[VMEM] * 4,
        compiler_params=pltpu.CompilerParams(vmem_limit_bytes=24 << 20),
        name="gate_up",
    )(*blocks, gate_t, up_t)


def down_kernel(cuts, gate, up, gate_r, up_r, weight, *rest):
    kept, sent = rest[:4], rest[4:8]
    g = gate[...] + gate_r[...].astype(F32)
    u = up[...] + up_r[...].astype(F32)
    left = (jax.nn.gelu(g, approximate=True) * u).astype(BF16)
    for s, n in cuts:
        store_blocks(dot(left, weight[:, s : s + n]), kept, sent, s, n)


def down(gate, up, gate_r, up_r, weight):
    width = weight.shape[1]
    cuts = pieces(width, 512)
    outs = pl.pallas_call(
        lambda *refs: down_kernel(cuts, *refs),
        out_shape=block_shapes(gate.shape[0] // 8, width),
        in_specs=[VMEM] * 5,
        out_specs=[VMEM] * 8,
        compiler_params=pltpu.CompilerParams(vmem_limit_bytes=20 << 20),
        name="down",
    )(gate, up, gate_r, up_r, weight)
    return outs[:4], outs[4:]


def attend_kernel(own, block, *refs):
    if own:
        lengths, query_a, query_b, pair_a, pair_b, held_k, held_v, out = refs
    else:
        query_a, query_b, held_k, held_v, out = refs
    heads, rows, width, slots = held_k.shape
    low = lax.axis_index("gx") & 3
    pairs = heads // 2

    spread = block * width
    row = lax.broadcasted_iota(jnp.int32, (block, spread), 0)
    lane = lax.broadcasted_iota(jnp.int32, (block, spread), 1)
    diagonal = lane // width == row
    places = [pl.multiple_of((b ^ low) * block, block) for b in range(rows // block)]
    if own:
        lens = jnp.concatenate([lengths[pl.ds(p, block), :] for p in places], axis=0)
        valid = lax.broadcasted_iota(jnp.int32, (rows, slots), 1) < lens

    def softmax(scores, own_score):
        if own:
            scores = jnp.where(valid, scores, -1e30)
        top = jnp.max(scores, axis=1, keepdims=True)
        if own:
            top = jnp.maximum(top, own_score)
        expo = jnp.exp(scores - top)
        if own:
            expo = jnp.where(valid, expo, 0.0)
        total = jnp.sum(expo, axis=1, keepdims=True)
        if not own:
            return (expo / total).astype(BF16), None
        own_expo = jnp.exp(own_score - top)
        total = total + own_expo
        return (expo / total).astype(BF16), (own_expo / total).astype(BF16).astype(F32)

    def paired(held, i, place):
        return jnp.concatenate(
            [held[2 * i + e, pl.ds(place, block)].reshape(spread, slots) for e in range(2)], axis=1
        )

    def step(i, carry):
        cols = pl.ds(pl.multiple_of(i * 2 * width, 2 * width), 2 * width)
        both = (query_a[:, cols] + query_b[:, cols]).astype(BF16)
        queries = [both[:, e * width : (e + 1) * width] for e in range(2)]
        news, own_scores = [None, None], [None, None]
        if own:
            for e in range(2):
                hcols = pl.ds(pl.multiple_of((2 * i + e) * 2 * width, 2 * width), 2 * width)
                news[e] = (pair_a[:, hcols] + pair_b[:, hcols]).astype(BF16).astype(F32)
                own_scores[e] = jnp.sum(
                    queries[e].astype(F32) * news[e][:, :width], axis=1, keepdims=True
                )
        scores = [[], []]
        for b, place in enumerate(places):
            wides = []
            for e in range(2):
                wide = jnp.concatenate([queries[e][b * block : (b + 1) * block]] * block, axis=1)
                wides.append(jnp.where(diagonal, wide, jnp.zeros_like(wide)))
            result = dot(jnp.concatenate(wides, axis=0), paired(held_k, i, place))
            scores[0].append(result[:block, :slots])
            scores[1].append(result[block:, slots:])
        probs, own_probs = [None, None], [None, None]
        for e in range(2):
            probs[e], own_probs[e] = softmax(jnp.concatenate(scores[e], axis=0), own_scores[e])
        mixes = [[], []]
        for b, place in enumerate(places):
            parts = [p[b * block : (b + 1) * block] for p in probs]
            none = jnp.zeros_like(parts[0])
            left = jnp.concatenate(
                [
                    jnp.concatenate([parts[0], none], axis=1),
                    jnp.concatenate([none, parts[1]], axis=1),
                ],
                axis=0,
            )
            result = lax.dot_general(
                left, paired(held_v, i, place), NT, preferred_element_type=F32
            )
            for e in range(2):
                wide = jnp.where(diagonal, result[e * block : (e + 1) * block], 0.0)
                tiles = [wide[:, j * 2 * width : (j + 1) * 2 * width] for j in range(block // 2)]
                while len(tiles) > 1:
                    tiles = [a + c for a, c in zip(tiles[::2], tiles[1::2])]
                mixes[e].append(tiles[0][:, :width] + tiles[0][:, width:])
        mixes = [jnp.concatenate(m, axis=0) for m in mixes]
        if own:
            mixes = [m + p * n[:, width:] for m, p, n in zip(mixes, own_probs, news)]
        out[:, cols] = jnp.concatenate(mixes, axis=1).astype(BF16)
        return carry

    lax.fori_loop(0, pairs, step, 0)


def attend(lengths, query, pair, keys, values):
    own = pair is not None
    operands = ([lengths] if own else []) + list(query) + (list(pair) if own else [])
    operands += [keys, values]
    heads, rows, width, slots = keys.shape
    return pl.pallas_call(
        lambda *refs: attend_kernel(own, rows // 4, *refs),
        out_shape=jax.ShapeDtypeStruct((rows, heads * width), BF16),
        in_specs=[VMEM] * len(operands),
        out_specs=VMEM,
        compiler_params=pltpu.CompilerParams(vmem_limit_bytes=24 << 20),
        name="self_attend" if own else "cross_attend",
    )(*operands)


def per_device_eight(
    x_in,
    lengths,
    self_gain,
    cross_gain,
    ffn_gain,
    final_gain,
    self_query,
    self_kv,
    self_out,
    cross_query,
    cross_out,
    ffn_gate,
    ffn_up,
    ffn_down,
    self_keys,
    self_values,
    cross_keys,
    cross_values,
):
    half = self_keys.shape[1]
    lengths = jnp.broadcast_to(lengths[:, None], (half, self_keys.shape[3]))

    def other_core(value):
        return swap(value, "gy", 1, 2)

    def update(stream, outs):
        return (stream.astype(F32) + scatter_sum(*outs)).astype(BF16)

    def project_heads(stream, heads, weight):
        return update(stream, heads_out(heads, other_core(heads), weight.T))

    stream = x_in
    normed = arrange(gather_blocks(norm_ahead(stream, self_gain)))
    query_part = dot(normed, self_query)
    pair_part = dot(normed, self_kv.reshape(self_kv.shape[0], -1))
    query = query_part[:half], other_core(query_part[half:])
    pair = pair_part[:half], other_core(pair_part[half:])
    heads = attend(lengths, query, pair, self_keys, self_values)
    stream = project_heads(stream, heads, self_out)

    blocks = gather_blocks(norm_ahead(stream, cross_gain))
    mine, other = query_halves(blocks, cross_query)
    heads = attend(None, (mine, other_core(other)), None, cross_keys, cross_values)
    stream = project_heads(stream, heads, cross_out)

    blocks = gather_blocks(norm_ahead(stream, ffn_gain))
    gate, up, gate_s, up_s = gate_up(blocks, ffn_gate.T, ffn_up.T)
    stream = update(stream, down(gate, up, other_core(gate_s), other_core(up_s), ffn_down))
    return normalize(stream, final_gain)


def softmax_mix(scores, own_score, cache_values, own_value):
    top = jnp.max(scores, axis=2)
    if own_score is not None:
        top = jnp.maximum(top, own_score)
    expo = jnp.exp(scores - top[:, :, None])
    totals = jnp.sum(expo, axis=2)
    if own_score is not None:
        own_expo = jnp.exp(own_score - top)
        totals = totals + own_expo
    probs = (expo / totals[:, :, None]).astype(BF16)
    mixed = jnp.einsum("hbs,hbds->bhd", probs, cache_values, preferred_element_type=F32)
    if own_score is not None:
        own_prob = (own_expo / totals).astype(BF16).T.astype(F32)
        mixed = mixed + own_prob[:, :, None] * own_value.astype(F32)
    return mixed.astype(BF16).reshape(mixed.shape[0], -1)


def per_device_any(
    x_in,
    lengths,
    self_gain,
    cross_gain,
    ffn_gain,
    final_gain,
    self_query,
    self_kv,
    self_out,
    cross_query,
    cross_out,
    ffn_gate,
    ffn_up,
    ffn_down,
    self_keys,
    self_values,
    cross_keys,
    cross_values,
):
    heads_here = self_query.shape[1] // DK
    rows_here = self_keys.shape[1]

    def half_sum(partial):
        total = lax.psum_scatter(partial, "gy", scatter_dimension=0, tiled=True).astype(BF16)
        return total.reshape(rows_here, heads_here, -1)

    def gather(stream, gain):
        return lax.all_gather(normalize(stream, gain), "gx", axis=0, tiled=True)

    def update(stream, left, weight):
        summed = lax.psum_scatter(dot(left, weight), "gx", scatter_dimension=0, tiled=True)
        return (stream.astype(F32) + summed).astype(BF16)

    def both_halves(heads):
        return lax.all_gather(heads, "gy", axis=0, tiled=True)

    def score(query, keys):
        return jnp.einsum("bhd,hbds->hbs", query, keys, preferred_element_type=F32)

    stream = x_in
    normed = gather(stream, self_gain)
    query = half_sum(dot(normed, self_query))
    pair = half_sum(dot(normed, self_kv.reshape(self_kv.shape[0], -1)))
    scores = score(query, self_keys)
    slots = lax.broadcasted_iota(jnp.int32, (1,) + scores.shape[1:], 2)
    scores = jnp.where(slots < lengths[None, :, None], scores, -jnp.inf)
    own_score = jnp.einsum("bhd,bhd->hb", query, pair[:, :, :DK], preferred_element_type=F32)
    heads = softmax_mix(scores, own_score, self_values, pair[:, :, DK:])
    stream = update(stream, both_halves(heads), self_out)

    query = half_sum(dot(gather(stream, cross_gain), cross_query))
    heads = softmax_mix(score(query, cross_keys), None, cross_values, None)
    stream = update(stream, both_halves(heads), cross_out)

    normed = gather(stream, ffn_gain)
    gate, up = dot(normed, ffn_gate), dot(normed, ffn_up)
    gate = gate + swap(gate.astype(BF16), "gy", 1, 2).astype(F32)
    up = up + swap(up.astype(BF16), "gy", 1, 2).astype(F32)
    hidden = (jax.nn.gelu(gate, approximate=True) * up).astype(BF16)
    return normalize(update(stream, hidden, ffn_down), final_gain)


def solution(mesh):
    eight = mesh.shape["gx"] == 8 and mesh.shape["gy"] == 2
    return jax.shard_map(
        per_device_eight if eight else per_device_any,
        mesh=mesh,
        in_specs=(
            P(("groups", "gx"), "gy"),
            P(("groups", "gy")),
            P("gy"),
            P("gy"),
            P("gy"),
            P("gy"),
            P("gy", "gx"),
            P("gy", "gx", None),
            P("gx", "gy"),
            P("gy", "gx"),
            P("gx", "gy"),
            P("gy", "gx"),
            P("gy", "gx"),
            P("gx", "gy"),
            P("gx", ("groups", "gy"), None, None),
            P("gx", ("groups", "gy"), None, None),
            P("gx", ("groups", "gy"), None, None),
            P("gx", ("groups", "gy"), None, None),
        ),
        out_specs=P(("groups", "gx"), "gy"),
        check_vma=False,
    )
```

time: 166 us -> 135 us (0.81)
  local copies, waits for them, and re-layouts: 20.3 us -> 2.69 us
  Pallas kernels: 32.3 us -> 21.4 us
    unnamed x41 -> x48, local copies, waits for them, and re-layouts: 20.2 us -> 1.57 us
    pallas_call x1, Pallas kernels: 8.39 us -> 4.97 us  [gate_up(): pl.pallas_call(lambda *refs: gate_up_kernel(cuts, *refs), out_shape=[jax....]
    pallas_call x2, Pallas kernels: 15.2 us -> 12.1 us  [attend(): pl.pallas_call(lambda *refs: attend_kernel(own, rows // 4, *refs), out_sh...]
    pallas_call x1, Pallas kernels: 3.57 us -> 1.51 us  [down(): pl.pallas_call(lambda *refs: down_kernel(cuts, *refs), out_shape=block_sh...]
    pallas_call x2, Pallas kernels: 3.56 us -> 1.89 us  [heads_out(): pl.pallas_call(lambda *refs: heads_out_kernel(cuts, *refs), out_shape=blo...]
  transfers between devices with their start and end apart: 53 -> 53, of which waited for: 38 -> 39; matrix products, arithmetic and copies ran while one was open for 0% -> 1% of each run, Pallas kernels for 0% -> 0%
where the time goes in v3:
time: 135 us
  starting transfers between devices  55.4 us (41%)
  waiting for transfers between devices  50.9 us (38%)
  Pallas kernels  21.4 us (16%)
  local copies, waits for them, and re-layouts  2.69 us (2%)
  other arithmetic  2.63 us (2%)
  matrix products  1.36 us (1%)
    ppermute x53, starting transfers between devices, swap(): return lax.ppermute(value, axis, [(i, i ^ mask) for i in range(size)])  55.4 us
    ppermute x53, waiting for transfers between devices, swap(): return lax.ppermute(value, axis, [(i, i ^ mask) for i in range(size)])  50.9 us
    pallas_call x2, Pallas kernels, attend(): pl.pallas_call(lambda *refs: attend_kernel(own, rows // 4, *refs), out_sh...  12.1 us
    pallas_call x1, Pallas kernels, gate_up(): pl.pallas_call(lambda *refs: gate_up_kernel(cuts, *refs), out_shape=[jax....  4.97 us
  transfers between devices with their start and end apart: 53, of which 39 were waited for; matrix products, arithmetic and copies ran while one was open for 1% of the time, Pallas kernels for 0%

profile of v3, /device:TPU:0, one launch (start us, length us, event | category | flops | bytes accessed | tf_op | source)
XLA Modules:
  0.0 134.8 jit_solution(3040268446589788258)
XLA Ops:
  0.0 1.2 fusion.3
  3.5 5.0 %collective-permute-start.6 = (bf16[16,2336]{1,0:T(8,128)(2,1)S(1)}, bf16[16,2336]{1,0:T(8,128)(2,1)S(1)}, u32[]{:S(2)}, u32[]{:S(2)}) collective-permute-start(bf16[16,2336]{1,0:T(8,128)(2,1)S(1)} %norm.3.refs_0_), channel_id=1, source_target_pairs={{0,12},{2,14},{4,8},{6,10},{8,4},{10,6},{12,0},{14,2},{1,13},{3,15... | collective-permute-start | bytes 224264 | tf_op jit(solution)/shard_map/ppermute | solution.py:17
  9.2 1.6 %collective-permute-start.1 = (bf16[16,2336]{1,0:T(8,128)(2,1)S(1)}, bf16[16,2336]{1,0:T(8,128)(2,1)S(1)}, u32[]{:S(2)}, u32[]{:S(2)}) collective-permute-start(bf16[16,2336]{1,0:T(8,128)(2,1)S(1)} %norm.3.refs_0_), channel_id=1, source_target_pairs={{0,2},{2,0},{4,6},{6,4},{8,10},{10,8},{12,14},{14,12},{1,3},{3,1},... | collective-permute-start | bytes 224264 | tf_op jit(solution)/shard_map/ppermute | solution.py:17
  11.7 1.5 %collective-permute-start.7 = (bf16[16,2336]{1,0:T(8,128)(2,1)S(1)}, bf16[16,2336]{1,0:T(8,128)(2,1)S(1)}, u32[]{:S(2)}, u32[]{:S(2)}) collective-permute-start(bf16[16,2336]{1,0:T(8,128)(2,1)S(1)} %collective-permute-done.6.refs_6_), channel_id=1, source_target_pairs={{0,2},{2,0},{4,6},{6,4},{8,10},{10,8},{12,14},{14,12},{1,3},{3,1},... | collective-permute-start | bytes 224264 | tf_op jit(solution)/shard_map/ppermute | solution.py:17
  13.2 2.1 %collective-permute-done.4.refs_4_ = bf16[16,2336]{1,0:T(8,128)(2,1)S(1)} collective-permute-done((bf16[16,2336]{1,0:T(8,128)(2,1)S(1)}, bf16[16,2336]{1,0:T(8,128)(2,1)S(1)}, u32[]{:S(2)}, u32[]{:S(2)}) %collective-permute-start.4) | collective-permute-done | bytes 74784 | tf_op jit(solution)/shard_map/ppermute | solution.py:17
  15.4 1.5 %collective-permute-start.5 = (bf16[16,2336]{1,0:T(8,128)(2,1)S(1)}, bf16[16,2336]{1,0:T(8,128)(2,1)S(1)}, u32[]{:S(2)}, u32[]{:S(2)}) collective-permute-start(bf16[16,2336]{1,0:T(8,128)(2,1)S(1)} %collective-permute-done.4.refs_4_), channel_id=1, source_target_pairs={{0,2},{2,0},{4,6},{6,4},{8,10},{10,8},{12,14},{14,12},{1,3},{3,1},... | collective-permute-start | bytes 224264 | tf_op jit(solution)/shard_map/ppermute | solution.py:17
  17.4 2.8 %collective-permute-done.5.refs_5_ = bf16[16,2336]{1,0:T(8,128)(2,1)S(1)} collective-permute-done((bf16[16,2336]{1,0:T(8,128)(2,1)S(1)}, bf16[16,2336]{1,0:T(8,128)(2,1)S(1)}, u32[]{:S(2)}, u32[]{:S(2)}) %collective-permute-start.5) | collective-permute-done | bytes 74784 | tf_op jit(solution)/shard_map/ppermute | solution.py:17
  23.5 1.1 collective-permute-done.8.refs_2_
  25.3 6.5 %self_attend.1.refs_0_ = bf16[64,512]{1,0:T(8,128)(2,1)S(1)} custom-call(s32[64,128]{1,0:T(8,128)S(1)} %broadcast_in_dim.28.refs_0_, f32[64,512]{1,0:T(8,128)S(1)} %get-tuple-element.74.refs_1_, f32[64,512]{1,0:T(8,128)S(1)} %collective-permute-done.8.refs_2_, f32[64,1024]{1,0:T(8,128)S(1)} %get-tuple-element.72.refs_3_, ...), custom_call_target="tpu_custom_call" | custom-call | tf_op jit(solution)/shard_map/self_attend/pallas_call | solution.py:308
  31.9 1.2 collective-permute-done.10.refs_1_
  35.0 1.1 collective-permute-start.11
  37.1 1.1 collective-permute-start.16
  38.2 1.1 collective-permute-done.12
  39.3 2.5 %collective-permute-start.13 = (bf16[16,2336]{1,0:T(8,128)(2,1)S(1)}, bf16[16,2336]{1,0:T(8,128)(2,1)S(1)}, u32[]{:S(2)}, u32[]{:S(2)}) collective-permute-start(bf16[16,2336]{1,0:T(8,128)(2,1)S(1)} %add_convert_fusion.8), channel_id=1, source_target_pairs={{0,12},{2,14},{4,8},{6,10},{8,4},{10,6},{12,0},{14,2},{1,13},{3,15... | collective-permute-start | bytes 224264 | tf_op jit(solution)/shard_map/ppermute | solution.py:17
  43.8 2.1 %collective-permute-start.17 = (bf16[16,2336]{1,0:T(8,128)(2,1)S(1)}, bf16[16,2336]{1,0:T(8,128)(2,1)S(1)}, u32[]{:S(2)}, u32[]{:S(2)}) collective-permute-start(bf16[16,2336]{1,0:T(8,128)(2,1)S(1)} %add_convert_fusion.6), channel_id=1, source_target_pairs={{0,4},{2,6},{4,0},{6,2},{8,12},{10,14},{12,8},{14,10},{1,5},{3,7},... | collective-permute-start | bytes 224264 | tf_op jit(solution)/shard_map/ppermute | solution.py:17
  46.4 2.6 %collective-permute-done.15 = bf16[16,2336]{1,0:T(8,128)(2,1)S(1)} collective-permute-done((bf16[16,2336]{1,0:T(8,128)(2,1)S(1)}, bf16[16,2336]{1,0:T(8,128)(2,1)S(1)}, u32[]{:S(2)}, u32[]{:S(2)}) %collective-permute-start.15) | collective-permute-done | bytes 74784 | tf_op jit(solution)/shard_map/ppermute | solution.py:17
  49.5 1.1 collective-permute-done.18.other
  50.8 2.5 %collective-permute-start.24 = (bf16[16,2336]{1,0:T(8,128)(2,1)S(1)}, bf16[16,2336]{1,0:T(8,128)(2,1)S(1)}, u32[]{:S(2)}, u32[]{:S(2)}) collective-permute-start(bf16[16,2336]{1,0:T(8,128)(2,1)S(1)} %norm.4.refs_0_), channel_id=1, source_target_pairs={{0,12},{2,14},{4,8},{6,10},{8,4},{10,6},{12,0},{14,2},{1,13},{3,15... | collective-permute-start | bytes 224264 | tf_op jit(solution)/shard_map/ppermute | solution.py:17
  53.4 1.9 %collective-permute-start.20 = (bf16[16,2336]{1,0:T(8,128)(2,1)S(1)}, bf16[16,2336]{1,0:T(8,128)(2,1)S(1)}, u32[]{:S(2)}, u32[]{:S(2)}) collective-permute-start(bf16[16,2336]{1,0:T(8,128)(2,1)S(1)} %norm.4.refs_0_), channel_id=1, source_target_pairs={{0,4},{2,6},{4,0},{6,2},{8,12},{10,14},{12,8},{14,10},{1,5},{3,7},... | collective-permute-start | bytes 224264 | tf_op jit(solution)/shard_map/ppermute | solution.py:17
  56.1 1.9 %collective-permute-done.24.refs_6_ = bf16[16,2336]{1,0:T(8,128)(2,1)S(1)} collective-permute-done((bf16[16,2336]{1,0:T(8,128)(2,1)S(1)}, bf16[16,2336]{1,0:T(8,128)(2,1)S(1)}, u32[]{:S(2)}, u32[]{:S(2)}) %collective-permute-start.24) | collective-permute-done | bytes 74784 | tf_op jit(solution)/shard_map/ppermute | solution.py:17
  58.8 2.0 %collective-permute-done.22.refs_4_ = bf16[16,2336]{1,0:T(8,128)(2,1)S(1)} collective-permute-done((bf16[16,2336]{1,0:T(8,128)(2,1)S(1)}, bf16[16,2336]{1,0:T(8,128)(2,1)S(1)}, u32[]{:S(2)}, u32[]{:S(2)}) %collective-permute-start.22) | collective-permute-done | bytes 74784 | tf_op jit(solution)/shard_map/ppermute | solution.py:17
  60.8 1.1 collective-permute-start.23
  62.8 3.0 %collective-permute-done.23.refs_5_ = bf16[16,2336]{1,0:T(8,128)(2,1)S(1)} collective-permute-done((bf16[16,2336]{1,0:T(8,128)(2,1)S(1)}, bf16[16,2336]{1,0:T(8,128)(2,1)S(1)}, u32[]{:S(2)}, u32[]{:S(2)}) %collective-permute-start.23) | collective-permute-done | bytes 74784 | tf_op jit(solution)/shard_map/ppermute | solution.py:17
  67.2 1.3 collective-permute-done.26.refs_1_
  68.6 5.6 %cross_attend.1.refs_0_ = bf16[64,512]{1,0:T(8,128)(2,1)S(1)} custom-call(f32[64,512]{1,0:T(8,128)S(1)} %get-tuple-element.43.refs_0_, f32[64,512]{1,0:T(8,128)S(1)} %collective-permute-done.26.refs_1_, bf16[8,64,64,128]{3,2,1,0:T(8,128)(2,1)S(1)} %bitcast.19, bf16[8,64,64,128]{3,2,1,0:T(8,128)(2,1)S(1)} %bitcast.21), custom_call_target="tpu_custom_call" | custom-call | tf_op jit(solution)/shard_map/cross_attend/pallas_call | solution.py:308
  74.4 1.1 collective-permute-done.27.refs_1_
  77.4 1.1 collective-permute-start.28
  79.5 1.1 collective-permute-start.33
  80.6 1.1 collective-permute-done.29
  81.8 2.2 %collective-permute-start.30 = (bf16[16,2336]{1,0:T(8,128)(2,1)S(1)}, bf16[16,2336]{1,0:T(8,128)(2,1)S(1)}, u32[]{:S(2)}, u32[]{:S(2)}) collective-permute-start(bf16[16,2336]{1,0:T(8,128)(2,1)S(1)} %add_convert_fusion.5), channel_id=1, source_target_pairs={{0,12},{2,14},{4,8},{6,10},{8,4},{10,6},{12,0},{14,2},{1,13},{3,15... | collective-permute-start | bytes 224264 | tf_op jit(solution)/shard_map/ppermute | solution.py:17
  86.0 2.0 %collective-permute-start.34 = (bf16[16,2336]{1,0:T(8,128)(2,1)S(1)}, bf16[16,2336]{1,0:T(8,128)(2,1)S(1)}, u32[]{:S(2)}, u32[]{:S(2)}) collective-permute-start(bf16[16,2336]{1,0:T(8,128)(2,1)S(1)} %add_convert_fusion.3), channel_id=1, source_target_pairs={{0,4},{2,6},{4,0},{6,2},{8,12},{10,14},{12,8},{14,10},{1,5},{3,7},... | collective-permute-start | bytes 224264 | tf_op jit(solution)/shard_map/ppermute | solution.py:17
  88.5 2.5 %collective-permute-done.32 = bf16[16,2336]{1,0:T(8,128)(2,1)S(1)} collective-permute-done((bf16[16,2336]{1,0:T(8,128)(2,1)S(1)}, bf16[16,2336]{1,0:T(8,128)(2,1)S(1)}, u32[]{:S(2)}, u32[]{:S(2)}) %collective-permute-start.32) | collective-permute-done | bytes 74784 | tf_op jit(solution)/shard_map/ppermute | solution.py:17
  92.0 1.1 collective-permute-done.35.other
  93.2 1.9 %collective-permute-start.41 = (bf16[16,2336]{1,0:T(8,128)(2,1)S(1)}, bf16[16,2336]{1,0:T(8,128)(2,1)S(1)}, u32[]{:S(2)}, u32[]{:S(2)}) collective-permute-start(bf16[16,2336]{1,0:T(8,128)(2,1)S(1)} %norm.5.refs_0_), channel_id=1, source_target_pairs={{0,12},{2,14},{4,8},{6,10},{8,4},{10,6},{12,0},{14,2},{1,13},{3,15... | collective-permute-start | bytes 224264 | tf_op jit(solution)/shard_map/ppermute | solution.py:17
  95.5 2.2 %collective-permute-start.37 = (bf16[16,2336]{1,0:T(8,128)(2,1)S(1)}, bf16[16,2336]{1,0:T(8,128)(2,1)S(1)}, u32[]{:S(2)}, u32[]{:S(2)}) collective-permute-start(bf16[16,2336]{1,0:T(8,128)(2,1)S(1)} %norm.5.refs_0_), channel_id=1, source_target_pairs={{0,4},{2,6},{4,0},{6,2},{8,12},{10,14},{12,8},{14,10},{1,5},{3,7},... | collective-permute-start | bytes 224264 | tf_op jit(solution)/shard_map/ppermute | solution.py:17
  98.6 1.8 %collective-permute-done.41.refs_6_ = bf16[16,2336]{1,0:T(8,128)(2,1)S(1)} collective-permute-done((bf16[16,2336]{1,0:T(8,128)(2,1)S(1)}, bf16[16,2336]{1,0:T(8,128)(2,1)S(1)}, u32[]{:S(2)}, u32[]{:S(2)}) %collective-permute-start.41) | collective-permute-done | bytes 74784 | tf_op jit(solution)/shard_map/ppermute | solution.py:17
  101.3 1.5 %collective-permute-done.39.refs_4_ = bf16[16,2336]{1,0:T(8,128)(2,1)S(1)} collective-permute-done((bf16[16,2336]{1,0:T(8,128)(2,1)S(1)}, bf16[16,2336]{1,0:T(8,128)(2,1)S(1)}, u32[]{:S(2)}, u32[]{:S(2)}) %collective-permute-start.39) | collective-permute-done | bytes 74784 | tf_op jit(solution)/shard_map/ppermute | solution.py:17
  104.9 3.1 %collective-permute-done.40.refs_5_ = bf16[16,2336]{1,0:T(8,128)(2,1)S(1)} collective-permute-done((bf16[16,2336]{1,0:T(8,128)(2,1)S(1)}, bf16[16,2336]{1,0:T(8,128)(2,1)S(1)}, u32[]{:S(2)}, u32[]{:S(2)}) %collective-permute-start.40) | collective-permute-done | bytes 74784 | tf_op jit(solution)/shard_map/ppermute | solution.py:17
  108.9 5.0 %gate_up.1 = (f32[128,1544]{1,0:T(8,128)S(1)}, f32[128,1544]{1,0:T(8,128)S(1)}, bf16[128,1544]{1,0:T(8,128)(2,1)S(1)}, bf16[128,1544]{1,0:T(8,128)(2,1)S(1)}) custom-call(bf16[16,2336]{1,0:T(8,128)(2,1)S(1)} %norm.5.refs_0_, bf16[16,2336]{1,0:T(8,128)(2,1)S(1)} %collective-permute-done.36.refs_1_, bf16[16,2336]{1,0:T(8,128)(2,1)S(1)} %collective-permute-done.37.refs_2_, ...), custom_call_target="tpu_custom_call" | custom-call | tf_op jit(solution)/shard_map/gate_up/pallas_call | solution.py:177
  114.4 1.3 collective-permute-done.43.refs_2_
  116.3 1.5 %down.1 = (f32[16,2336]{1,0:T(8,128)S(1)}, f32[16,2336]{1,0:T(8,128)S(1)}, f32[16,2336]{1,0:T(8,128)S(1)}, f32[16,2336]{1,0:T(8,128)S(1)}, bf16[16,2336]{1,0:T(8...) custom-call(f32[128,1544]{1,0:T(8,128)S(1)} %get-tuple-element.53.refs_0_, ...), custom_call_target="tpu_custom_call" | custom-call | tf_op jit(solution)/shard_map/down/pallas_call | solution.py:200
  117.8 1.1 collective-permute-start.46
  122.0 1.1 collective-permute-done.46
  123.1 1.9 %collective-permute-start.47 = (bf16[16,2336]{1,0:T(8,128)(2,1)S(1)}, bf16[16,2336]{1,0:T(8,128)(2,1)S(1)}, u32[]{:S(2)}, u32[]{:S(2)}) collective-permute-start(bf16[16,2336]{1,0:T(8,128)(2,1)S(1)} %add_convert_fusion.2), channel_id=1, source_target_pairs={{0,12},{2,14},{4,8},{6,10},{8,4},{10,6},{12,0},{14,2},{1,13},{3,15... | collective-permute-start | bytes 224264 | tf_op jit(solution)/shard_map/ppermute | solution.py:17
  125.0 1.4 %collective-permute-done.48 = bf16[16,2336]{1,0:T(8,128)(2,1)S(1)} collective-permute-done((bf16[16,2336]{1,0:T(8,128)(2,1)S(1)}, bf16[16,2336]{1,0:T(8,128)(2,1)S(1)}, u32[]{:S(2)}, u32[]{:S(2)}) %collective-permute-start.48) | collective-permute-done | bytes 74784 | tf_op jit(solution)/shard_map/ppermute | solution.py:17
  127.3 1.7 %collective-permute-start.51 = (bf16[16,2336]{1,0:T(8,128)(2,1)S(1)}, bf16[16,2336]{1,0:T(8,128)(2,1)S(1)}, u32[]{:S(2)}, u32[]{:S(2)}) collective-permute-start(bf16[16,2336]{1,0:T(8,128)(2,1)S(1)} %add_convert_fusion), channel_id=1, source_target_pairs={{0,4},{2,6},{4,0},{6,2},{8,12},{10,14},{12,8},{14,10},{1,5},{3,7},... | collective-permute-start | bytes 224264 | tf_op jit(solution)/shard_map/ppermute | solution.py:17
  129.5 2.7 %collective-permute-done.49 = bf16[16,2336]{1,0:T(8,128)(2,1)S(1)} collective-permute-done((bf16[16,2336]{1,0:T(8,128)(2,1)S(1)}, bf16[16,2336]{1,0:T(8,128)(2,1)S(1)}, u32[]{:S(2)}, u32[]{:S(2)}) %collective-permute-start.49) | collective-permute-done | bytes 74784 | tf_op jit(solution)/shard_map/ppermute | solution.py:17
  132.9 1.1 collective-permute-done.52
  (148 shorter events, 36.9 us)
Async XLA Ops:
  1.3 1.3 collective-permute-start
  3.5 8.2 %collective-permute-start.6 = (bf16[16,2336]{1,0:T(8,128)(2,1)S(1)}, bf16[16,2336]{1,0:T(8,128)(2,1)S(1)}, u32[]{:S(2)}, u32[]{:S(2)}) collective-permute-start(bf16[16,2336]{1,0:T(8,128)(2,1)S(1)} %norm.3.refs_0_), channel_id=1, source_target_pairs={{0,12},{2,14},{4,8},{6,10},{8,4},{10,6},{12,0},{14,2},{1,13},{3,15... | collective-permute-start | bytes 224264 | tf_op jit(solution)/shard_map/ppermute | solution.py:17
  8.5 6.8 %collective-permute-start.4 = (bf16[16,2336]{1,0:T(8,128)(2,1)S(1)}, bf16[16,2336]{1,0:T(8,128)(2,1)S(1)}, u32[]{:S(2)}, u32[]{:S(2)}) collective-permute-start(bf16[16,2336]{1,0:T(8,128)(2,1)S(1)} %norm.3.refs_0_), channel_id=1, source_target_pairs={{0,8},{2,10},{4,12},{6,14},{8,0},{10,2},{12,4},{14,6},{1,9},{3,11}... | collective-permute-start | bytes 224264 | tf_op jit(solution)/shard_map/ppermute | solution.py:17
  8.5 8.3 %collective-permute-start.2 = (bf16[16,2336]{1,0:T(8,128)(2,1)S(1)}, bf16[16,2336]{1,0:T(8,128)(2,1)S(1)}, u32[]{:S(2)}, u32[]{:S(2)}) collective-permute-start(bf16[16,2336]{1,0:T(8,128)(2,1)S(1)} %norm.3.refs_0_), channel_id=1, source_target_pairs={{0,4},{2,6},{4,0},{6,2},{8,12},{10,14},{12,8},{14,10},{1,5},{3,7},... | collective-permute-start | bytes 224264 | tf_op jit(solution)/shard_map/ppermute | solution.py:17
  9.2 8.2 %collective-permute-start.1 = (bf16[16,2336]{1,0:T(8,128)(2,1)S(1)}, bf16[16,2336]{1,0:T(8,128)(2,1)S(1)}, u32[]{:S(2)}, u32[]{:S(2)}) collective-permute-start(bf16[16,2336]{1,0:T(8,128)(2,1)S(1)} %norm.3.refs_0_), channel_id=1, source_target_pairs={{0,2},{2,0},{4,6},{6,4},{8,10},{10,8},{12,14},{14,12},{1,3},{3,1},... | collective-permute-start | bytes 224264 | tf_op jit(solution)/shard_map/ppermute | solution.py:17
  11.7 5.7 %collective-permute-start.7 = (bf16[16,2336]{1,0:T(8,128)(2,1)S(1)}, bf16[16,2336]{1,0:T(8,128)(2,1)S(1)}, u32[]{:S(2)}, u32[]{:S(2)}) collective-permute-start(bf16[16,2336]{1,0:T(8,128)(2,1)S(1)} %collective-permute-done.6.refs_6_), channel_id=1, source_target_pairs={{0,2},{2,0},{4,6},{6,4},{8,10},{10,8},{12,14},{14,12},{1,3},{3,1},... | collective-permute-start | bytes 224264 | tf_op jit(solution)/shard_map/ppermute | solution.py:17
  15.4 4.9 %collective-permute-start.5 = (bf16[16,2336]{1,0:T(8,128)(2,1)S(1)}, bf16[16,2336]{1,0:T(8,128)(2,1)S(1)}, u32[]{:S(2)}, u32[]{:S(2)}) collective-permute-start(bf16[16,2336]{1,0:T(8,128)(2,1)S(1)} %collective-permute-done.4.refs_4_), channel_id=1, source_target_pairs={{0,2},{2,0},{4,6},{6,4},{8,10},{10,8},{12,14},{14,12},{1,3},{3,1},... | collective-permute-start | bytes 224264 | tf_op jit(solution)/shard_map/ppermute | solution.py:17
  16.9 4.4 %collective-permute-start.3 = (bf16[16,2336]{1,0:T(8,128)(2,1)S(1)}, bf16[16,2336]{1,0:T(8,128)(2,1)S(1)}, u32[]{:S(2)}, u32[]{:S(2)}) collective-permute-start(bf16[16,2336]{1,0:T(8,128)(2,1)S(1)} %collective-permute-done.2.refs_2_), channel_id=1, source_target_pairs={{0,2},{2,0},{4,6},{6,4},{8,10},{10,8},{12,14},{14,12},{1,3},{3,1},... | collective-permute-start | bytes 224264 | tf_op jit(solution)/shard_map/ppermute | solution.py:17
  22.8 1.8 %collective-permute-start.9 = (f32[64,1024]{1,0:T(8,128)S(1)}, f32[64,1024]{1,0:T(8,128)S(1)}, u32[]{:S(2)}, u32[]{:S(2)}) collective-permute-start(f32[64,1024]{1,0:T(8,128)S(1)} %get-tuple-element.71), channel_id=1, source_target_pairs={{0,1},{1,0},{2,3},{3,2},{4,5},{5,4},{6,7},{7,6},{8,9},{9,8},{10,11... | collective-permute-start | bytes 786440 | tf_op jit(solution)/shard_map/ppermute | solution.py:17
  22.9 1.7 %collective-permute-start.8 = (f32[64,512]{1,0:T(8,128)S(1)}, f32[64,512]{1,0:T(8,128)S(1)}, u32[]{:S(2)}, u32[]{:S(2)}) collective-permute-start(f32[64,512]{1,0:T(8,128)S(1)} %get-tuple-element.73), channel_id=1, source_target_pairs={{0,1},{1,0},{2,3},{3,2},{4,5},{5,4},{6,7},{7,6},{8,9},{9,8},{10,11... | collective-permute-start | bytes 393224 | tf_op jit(solution)/shard_map/ppermute | solution.py:17
  34.1 5.3 %collective-permute-start.12 = (bf16[16,2336]{1,0:T(8,128)(2,1)S(1)}, bf16[16,2336]{1,0:T(8,128)(2,1)S(1)}, u32[]{:S(2)}, u32[]{:S(2)}) collective-permute-start(bf16[16,2336]{1,0:T(8,128)(2,1)S(1)} %get-tuple-element.38), channel_id=1, source_target_pairs={{0,2},{2,0},{4,6},{6,4},{8,10},{10,8},{12,14},{14,12},{1,3},{3,1},... | collective-permute-start | bytes 224264 | tf_op jit(solution)/shard_map/ppermute | solution.py:17
  35.0 10.8 %collective-permute-start.11 = (bf16[16,2336]{1,0:T(8,128)(2,1)S(1)}, bf16[16,2336]{1,0:T(8,128)(2,1)S(1)}, u32[]{:S(2)}, u32[]{:S(2)}) collective-permute-start(bf16[16,2336]{1,0:T(8,128)(2,1)S(1)} %get-tuple-element.36), channel_id=1, source_target_pairs={{0,2},{2,0},{4,6},{6,4},{8,10},{10,8},{12,14},{14,12},{1,3},{3,1},... | collective-permute-start | bytes 224264 | tf_op jit(solution)/shard_map/ppermute | solution.py:17
  36.1 6.5 %collective-permute-start.14 = (bf16[16,2336]{1,0:T(8,128)(2,1)S(1)}, bf16[16,2336]{1,0:T(8,128)(2,1)S(1)}, u32[]{:S(2)}, u32[]{:S(2)}) collective-permute-start(bf16[16,2336]{1,0:T(8,128)(2,1)S(1)} %get-tuple-element.40), channel_id=1, source_target_pairs={{0,2},{2,0},{4,6},{6,4},{8,10},{10,8},{12,14},{14,12},{1,3},{3,1},... | collective-permute-start | bytes 224264 | tf_op jit(solution)/shard_map/ppermute | solution.py:17
  37.1 6.7 %collective-permute-start.16 = (bf16[16,2336]{1,0:T(8,128)(2,1)S(1)}, bf16[16,2336]{1,0:T(8,128)(2,1)S(1)}, u32[]{:S(2)}, u32[]{:S(2)}) collective-permute-start(bf16[16,2336]{1,0:T(8,128)(2,1)S(1)} %get-tuple-element.42), channel_id=1, source_target_pairs={{0,2},{2,0},{4,6},{6,4},{8,10},{10,8},{12,14},{14,12},{1,3},{3,1},... | collective-permute-start | bytes 224264 | tf_op jit(solution)/shard_map/ppermute | solution.py:17
  39.3 7.1 %collective-permute-start.13 = (bf16[16,2336]{1,0:T(8,128)(2,1)S(1)}, bf16[16,2336]{1,0:T(8,128)(2,1)S(1)}, u32[]{:S(2)}, u32[]{:S(2)}) collective-permute-start(bf16[16,2336]{1,0:T(8,128)(2,1)S(1)} %add_convert_fusion.8), channel_id=1, source_target_pairs={{0,12},{2,14},{4,8},{6,10},{8,4},{10,6},{12,0},{14,2},{1,13},{3,15... | collective-permute-start | bytes 224264 | tf_op jit(solution)/shard_map/ppermute | solution.py:17
  42.7 6.4 %collective-permute-start.15 = (bf16[16,2336]{1,0:T(8,128)(2,1)S(1)}, bf16[16,2336]{1,0:T(8,128)(2,1)S(1)}, u32[]{:S(2)}, u32[]{:S(2)}) collective-permute-start(bf16[16,2336]{1,0:T(8,128)(2,1)S(1)} %add_convert_fusion.7), channel_id=1, source_target_pairs={{0,8},{2,10},{4,12},{6,14},{8,0},{10,2},{12,4},{14,6},{1,9},{3,11}... | collective-permute-start | bytes 224264 | tf_op jit(solution)/shard_map/ppermute | solution.py:17
  43.8 5.5 %collective-permute-start.17 = (bf16[16,2336]{1,0:T(8,128)(2,1)S(1)}, bf16[16,2336]{1,0:T(8,128)(2,1)S(1)}, u32[]{:S(2)}, u32[]{:S(2)}) collective-permute-start(bf16[16,2336]{1,0:T(8,128)(2,1)S(1)} %add_convert_fusion.6), channel_id=1, source_target_pairs={{0,4},{2,6},{4,0},{6,2},{8,12},{10,14},{12,8},{14,10},{1,5},{3,7},... | collective-permute-start | bytes 224264 | tf_op jit(solution)/shard_map/ppermute | solution.py:17
  50.8 7.2 %collective-permute-start.24 = (bf16[16,2336]{1,0:T(8,128)(2,1)S(1)}, bf16[16,2336]{1,0:T(8,128)(2,1)S(1)}, u32[]{:S(2)}, u32[]{:S(2)}) collective-permute-start(bf16[16,2336]{1,0:T(8,128)(2,1)S(1)} %norm.4.refs_0_), channel_id=1, source_target_pairs={{0,12},{2,14},{4,8},{6,10},{8,4},{10,6},{12,0},{14,2},{1,13},{3,15... | collective-permute-start | bytes 224264 | tf_op jit(solution)/shard_map/ppermute | solution.py:17
  53.3 7.5 %collective-permute-start.22 = (bf16[16,2336]{1,0:T(8,128)(2,1)S(1)}, bf16[16,2336]{1,0:T(8,128)(2,1)S(1)}, u32[]{:S(2)}, u32[]{:S(2)}) collective-permute-start(bf16[16,2336]{1,0:T(8,128)(2,1)S(1)} %norm.4.refs_0_), channel_id=1, source_target_pairs={{0,8},{2,10},{4,12},{6,14},{8,0},{10,2},{12,4},{14,6},{1,9},{3,11}... | collective-permute-start | bytes 224264 | tf_op jit(solution)/shard_map/ppermute | solution.py:17
  53.4 8.5 %collective-permute-start.20 = (bf16[16,2336]{1,0:T(8,128)(2,1)S(1)}, bf16[16,2336]{1,0:T(8,128)(2,1)S(1)}, u32[]{:S(2)}, u32[]{:S(2)}) collective-permute-start(bf16[16,2336]{1,0:T(8,128)(2,1)S(1)} %norm.4.refs_0_), channel_id=1, source_target_pairs={{0,4},{2,6},{4,0},{6,2},{8,12},{10,14},{12,8},{14,10},{1,5},{3,7},... | collective-permute-start | bytes 224264 | tf_op jit(solution)/shard_map/ppermute | solution.py:17
  55.3 7.5 %collective-permute-start.19 = (bf16[16,2336]{1,0:T(8,128)(2,1)S(1)}, bf16[16,2336]{1,0:T(8,128)(2,1)S(1)}, u32[]{:S(2)}, u32[]{:S(2)}) collective-permute-start(bf16[16,2336]{1,0:T(8,128)(2,1)S(1)} %norm.4.refs_0_), channel_id=1, source_target_pairs={{0,2},{2,0},{4,6},{6,4},{8,10},{10,8},{12,14},{14,12},{1,3},{3,1},... | collective-permute-start | bytes 224264 | tf_op jit(solution)/shard_map/ppermute | solution.py:17
  58.0 4.8 %collective-permute-start.25 = (bf16[16,2336]{1,0:T(8,128)(2,1)S(1)}, bf16[16,2336]{1,0:T(8,128)(2,1)S(1)}, u32[]{:S(2)}, u32[]{:S(2)}) collective-permute-start(bf16[16,2336]{1,0:T(8,128)(2,1)S(1)} %collective-permute-done.24.refs_6_), channel_id=1, source_target_pairs={{0,2},{2,0},{4,6},{6,4},{8,10},{10,8},{12,14},{14,12},{1,3},{3,1},... | collective-permute-start | bytes 224264 | tf_op jit(solution)/shard_map/ppermute | solution.py:17
  60.8 5.0 %collective-permute-start.23 = (bf16[16,2336]{1,0:T(8,128)(2,1)S(1)}, bf16[16,2336]{1,0:T(8,128)(2,1)S(1)}, u32[]{:S(2)}, u32[]{:S(2)}) collective-permute-start(bf16[16,2336]{1,0:T(8,128)(2,1)S(1)} %collective-permute-done.22.refs_4_), channel_id=1, source_target_pairs={{0,2},{2,0},{4,6},{6,4},{8,10},{10,8},{12,14},{14,12},{1,3},{3,1},... | collective-permute-start | bytes 224264 | tf_op jit(solution)/shard_map/ppermute | solution.py:17
  61.9 4.7 %collective-permute-start.21 = (bf16[16,2336]{1,0:T(8,128)(2,1)S(1)}, bf16[16,2336]{1,0:T(8,128)(2,1)S(1)}, u32[]{:S(2)}, u32[]{:S(2)}) collective-permute-start(bf16[16,2336]{1,0:T(8,128)(2,1)S(1)} %collective-permute-done.20.refs_2_), channel_id=1, source_target_pairs={{0,2},{2,0},{4,6},{6,4},{8,10},{10,8},{12,14},{14,12},{1,3},{3,1},... | collective-permute-start | bytes 224264 | tf_op jit(solution)/shard_map/ppermute | solution.py:17
  67.2 1.4 %collective-permute-start.26 = (f32[64,512]{1,0:T(8,128)S(1)}, f32[64,512]{1,0:T(8,128)S(1)}, u32[]{:S(2)}, u32[]{:S(2)}) collective-permute-start(f32[64,512]{1,0:T(8,128)S(1)} %get-tuple-element.44), channel_id=1, source_target_pairs={{0,1},{1,0},{2,3},{3,2},{4,5},{5,4},{6,7},{7,6},{8,9},{9,8},{10,11... | collective-permute-start | bytes 393224 | tf_op jit(solution)/shard_map/ppermute | solution.py:17
  76.5 5.3 %collective-permute-start.29 = (bf16[16,2336]{1,0:T(8,128)(2,1)S(1)}, bf16[16,2336]{1,0:T(8,128)(2,1)S(1)}, u32[]{:S(2)}, u32[]{:S(2)}) collective-permute-start(bf16[16,2336]{1,0:T(8,128)(2,1)S(1)} %get-tuple-element.48), channel_id=1, source_target_pairs={{0,2},{2,0},{4,6},{6,4},{8,10},{10,8},{12,14},{14,12},{1,3},{3,1},... | collective-permute-start | bytes 224264 | tf_op jit(solution)/shard_map/ppermute | solution.py:17
  77.4 10.5 %collective-permute-start.28 = (bf16[16,2336]{1,0:T(8,128)(2,1)S(1)}, bf16[16,2336]{1,0:T(8,128)(2,1)S(1)}, u32[]{:S(2)}, u32[]{:S(2)}) collective-permute-start(bf16[16,2336]{1,0:T(8,128)(2,1)S(1)} %get-tuple-element.46), channel_id=1, source_target_pairs={{0,2},{2,0},{4,6},{6,4},{8,10},{10,8},{12,14},{14,12},{1,3},{3,1},... | collective-permute-start | bytes 224264 | tf_op jit(solution)/shard_map/ppermute | solution.py:17
  78.6 6.5 %collective-permute-start.31 = (bf16[16,2336]{1,0:T(8,128)(2,1)S(1)}, bf16[16,2336]{1,0:T(8,128)(2,1)S(1)}, u32[]{:S(2)}, u32[]{:S(2)}) collective-permute-start(bf16[16,2336]{1,0:T(8,128)(2,1)S(1)} %get-tuple-element.50), channel_id=1, source_target_pairs={{0,2},{2,0},{4,6},{6,4},{8,10},{10,8},{12,14},{14,12},{1,3},{3,1},... | collective-permute-start | bytes 224264 | tf_op jit(solution)/shard_map/ppermute | solution.py:17
  79.5 6.5 %collective-permute-start.33 = (bf16[16,2336]{1,0:T(8,128)(2,1)S(1)}, bf16[16,2336]{1,0:T(8,128)(2,1)S(1)}, u32[]{:S(2)}, u32[]{:S(2)}) collective-permute-start(bf16[16,2336]{1,0:T(8,128)(2,1)S(1)} %get-tuple-element.52), channel_id=1, source_target_pairs={{0,2},{2,0},{4,6},{6,4},{8,10},{10,8},{12,14},{14,12},{1,3},{3,1},... | collective-permute-start | bytes 224264 | tf_op jit(solution)/shard_map/ppermute | solution.py:17
  81.8 6.8 %collective-permute-start.30 = (bf16[16,2336]{1,0:T(8,128)(2,1)S(1)}, bf16[16,2336]{1,0:T(8,128)(2,1)S(1)}, u32[]{:S(2)}, u32[]{:S(2)}) collective-permute-start(bf16[16,2336]{1,0:T(8,128)(2,1)S(1)} %add_convert_fusion.5), channel_id=1, source_target_pairs={{0,12},{2,14},{4,8},{6,10},{8,4},{10,6},{12,0},{14,2},{1,13},{3,15... | collective-permute-start | bytes 224264 | tf_op jit(solution)/shard_map/ppermute | solution.py:17
  85.1 6.0 %collective-permute-start.32 = (bf16[16,2336]{1,0:T(8,128)(2,1)S(1)}, bf16[16,2336]{1,0:T(8,128)(2,1)S(1)}, u32[]{:S(2)}, u32[]{:S(2)}) collective-permute-start(bf16[16,2336]{1,0:T(8,128)(2,1)S(1)} %add_convert_fusion.4), channel_id=1, source_target_pairs={{0,8},{2,10},{4,12},{6,14},{8,0},{10,2},{12,4},{14,6},{1,9},{3,11}... | collective-permute-start | bytes 224264 | tf_op jit(solution)/shard_map/ppermute | solution.py:17
  86.0 5.7 %collective-permute-start.34 = (bf16[16,2336]{1,0:T(8,128)(2,1)S(1)}, bf16[16,2336]{1,0:T(8,128)(2,1)S(1)}, u32[]{:S(2)}, u32[]{:S(2)}) collective-permute-start(bf16[16,2336]{1,0:T(8,128)(2,1)S(1)} %add_convert_fusion.3), channel_id=1, source_target_pairs={{0,4},{2,6},{4,0},{6,2},{8,12},{10,14},{12,8},{14,10},{1,5},{3,7},... | collective-permute-start | bytes 224264 | tf_op jit(solution)/shard_map/ppermute | solution.py:17
  93.2 7.2 %collective-permute-start.41 = (bf16[16,2336]{1,0:T(8,128)(2,1)S(1)}, bf16[16,2336]{1,0:T(8,128)(2,1)S(1)}, u32[]{:S(2)}, u32[]{:S(2)}) collective-permute-start(bf16[16,2336]{1,0:T(8,128)(2,1)S(1)} %norm.5.refs_0_), channel_id=1, source_target_pairs={{0,12},{2,14},{4,8},{6,10},{8,4},{10,6},{12,0},{14,2},{1,13},{3,15... | collective-permute-start | bytes 224264 | tf_op jit(solution)/shard_map/ppermute | solution.py:17
  95.1 7.7 %collective-permute-start.39 = (bf16[16,2336]{1,0:T(8,128)(2,1)S(1)}, bf16[16,2336]{1,0:T(8,128)(2,1)S(1)}, u32[]{:S(2)}, u32[]{:S(2)}) collective-permute-start(bf16[16,2336]{1,0:T(8,128)(2,1)S(1)} %norm.5.refs_0_), channel_id=1, source_target_pairs={{0,8},{2,10},{4,12},{6,14},{8,0},{10,2},{12,4},{14,6},{1,9},{3,11}... | collective-permute-start | bytes 224264 | tf_op jit(solution)/shard_map/ppermute | solution.py:17
  95.5 8.4 %collective-permute-start.37 = (bf16[16,2336]{1,0:T(8,128)(2,1)S(1)}, bf16[16,2336]{1,0:T(8,128)(2,1)S(1)}, u32[]{:S(2)}, u32[]{:S(2)}) collective-permute-start(bf16[16,2336]{1,0:T(8,128)(2,1)S(1)} %norm.5.refs_0_), channel_id=1, source_target_pairs={{0,4},{2,6},{4,0},{6,2},{8,12},{10,14},{12,8},{14,10},{1,5},{3,7},... | collective-permute-start | bytes 224264 | tf_op jit(solution)/shard_map/ppermute | solution.py:17
  97.7 7.2 %collective-permute-start.36 = (bf16[16,2336]{1,0:T(8,128)(2,1)S(1)}, bf16[16,2336]{1,0:T(8,128)(2,1)S(1)}, u32[]{:S(2)}, u32[]{:S(2)}) collective-permute-start(bf16[16,2336]{1,0:T(8,128)(2,1)S(1)} %norm.5.refs_0_), channel_id=1, source_target_pairs={{0,2},{2,0},{4,6},{6,4},{8,10},{10,8},{12,14},{14,12},{1,3},{3,1},... | collective-permute-start | bytes 224264 | tf_op jit(solution)/shard_map/ppermute | solution.py:17
  100.4 4.5 %collective-permute-start.42 = (bf16[16,2336]{1,0:T(8,128)(2,1)S(1)}, bf16[16,2336]{1,0:T(8,128)(2,1)S(1)}, u32[]{:S(2)}, u32[]{:S(2)}) collective-permute-start(bf16[16,2336]{1,0:T(8,128)(2,1)S(1)} %collective-permute-done.41.refs_6_), channel_id=1, source_target_pairs={{0,2},{2,0},{4,6},{6,4},{8,10},{10,8},{12,14},{14,12},{1,3},{3,1},... | collective-permute-start | bytes 224264 | tf_op jit(solution)/shard_map/ppermute | solution.py:17
  102.9 5.1 %collective-permute-start.40 = (bf16[16,2336]{1,0:T(8,128)(2,1)S(1)}, bf16[16,2336]{1,0:T(8,128)(2,1)S(1)}, u32[]{:S(2)}, u32[]{:S(2)}) collective-permute-start(bf16[16,2336]{1,0:T(8,128)(2,1)S(1)} %collective-permute-done.39.refs_4_), channel_id=1, source_target_pairs={{0,2},{2,0},{4,6},{6,4},{8,10},{10,8},{12,14},{14,12},{1,3},{3,1},... | collective-permute-start | bytes 224264 | tf_op jit(solution)/shard_map/ppermute | solution.py:17
  103.9 5.0 %collective-permute-start.38 = (bf16[16,2336]{1,0:T(8,128)(2,1)S(1)}, bf16[16,2336]{1,0:T(8,128)(2,1)S(1)}, u32[]{:S(2)}, u32[]{:S(2)}) collective-permute-start(bf16[16,2336]{1,0:T(8,128)(2,1)S(1)} %collective-permute-done.37.refs_2_), channel_id=1, source_target_pairs={{0,2},{2,0},{4,6},{6,4},{8,10},{10,8},{12,14},{14,12},{1,3},{3,1},... | collective-permute-start | bytes 224264 | tf_op jit(solution)/shard_map/ppermute | solution.py:17
  113.8 1.8 %collective-permute-start.43 = (bf16[128,1544]{1,0:T(8,128)(2,1)S(1)}, bf16[128,1544]{1,0:T(8,128)(2,1)S(1)}, u32[]{:S(2)}, u32[]{:S(2)}) collective-permute-start(bf16[128,1544]{1,0:T(8,128)(2,1)S(1)} %get-tuple-element.55), channel_id=1, source_target_pairs={{0,1},{1,0},{2,3},{3,2},{4,5},{5,4},{6,7},{7,6},{8,9},{9,8},{10,11... | collective-permute-start | bytes 1185800 | tf_op jit(solution)/shard_map/ppermute | solution.py:17
  113.9 2.4 %collective-permute-start.44 = (bf16[128,1544]{1,0:T(8,128)(2,1)S(1)}, bf16[128,1544]{1,0:T(8,128)(2,1)S(1)}, u32[]{:S(2)}, u32[]{:S(2)}) collective-permute-start(bf16[128,1544]{1,0:T(8,128)(2,1)S(1)} %get-tuple-element.56), channel_id=1, source_target_pairs={{0,1},{1,0},{2,3},{3,2},{4,5},{5,4},{6,7},{7,6},{8,9},{9,8},{10,11... | collective-permute-start | bytes 1185800 | tf_op jit(solution)/shard_map/ppermute | solution.py:17
  117.8 5.3 %collective-permute-start.46 = (bf16[16,2336]{1,0:T(8,128)(2,1)S(1)}, bf16[16,2336]{1,0:T(8,128)(2,1)S(1)}, u32[]{:S(2)}, u32[]{:S(2)}) collective-permute-start(bf16[16,2336]{1,0:T(8,128)(2,1)S(1)} %get-tuple-element.60), channel_id=1, source_target_pairs={{0,2},{2,0},{4,6},{6,4},{8,10},{10,8},{12,14},{14,12},{1,3},{3,1},... | collective-permute-start | bytes 224264 | tf_op jit(solution)/shard_map/ppermute | solution.py:17
  119.0 10.0 %collective-permute-start.45 = (bf16[16,2336]{1,0:T(8,128)(2,1)S(1)}, bf16[16,2336]{1,0:T(8,128)(2,1)S(1)}, u32[]{:S(2)}, u32[]{:S(2)}) collective-permute-start(bf16[16,2336]{1,0:T(8,128)(2,1)S(1)} %get-tuple-element.58), channel_id=1, source_target_pairs={{0,2},{2,0},{4,6},{6,4},{8,10},{10,8},{12,14},{14,12},{1,3},{3,1},... | collective-permute-start | bytes 224264 | tf_op jit(solution)/shard_map/ppermute | solution.py:17
  119.9 6.5 %collective-permute-start.48 = (bf16[16,2336]{1,0:T(8,128)(2,1)S(1)}, bf16[16,2336]{1,0:T(8,128)(2,1)S(1)}, u32[]{:S(2)}, u32[]{:S(2)}) collective-permute-start(bf16[16,2336]{1,0:T(8,128)(2,1)S(1)} %get-tuple-element.62), channel_id=1, source_target_pairs={{0,2},{2,0},{4,6},{6,4},{8,10},{10,8},{12,14},{14,12},{1,3},{3,1},... | collective-permute-start | bytes 224264 | tf_op jit(solution)/shard_map/ppermute | solution.py:17
  121.0 6.3 %collective-permute-start.50 = (bf16[16,2336]{1,0:T(8,128)(2,1)S(1)}, bf16[16,2336]{1,0:T(8,128)(2,1)S(1)}, u32[]{:S(2)}, u32[]{:S(2)}) collective-permute-start(bf16[16,2336]{1,0:T(8,128)(2,1)S(1)} %get-tuple-element.64), channel_id=1, source_target_pairs={{0,2},{2,0},{4,6},{6,4},{8,10},{10,8},{12,14},{14,12},{1,3},{3,1},... | collective-permute-start | bytes 224264 | tf_op jit(solution)/shard_map/ppermute | solution.py:17
  123.1 6.3 %collective-permute-start.47 = (bf16[16,2336]{1,0:T(8,128)(2,1)S(1)}, bf16[16,2336]{1,0:T(8,128)(2,1)S(1)}, u32[]{:S(2)}, u32[]{:S(2)}) collective-permute-start(bf16[16,2336]{1,0:T(8,128)(2,1)S(1)} %add_convert_fusion.2), channel_id=1, source_target_pairs={{0,12},{2,14},{4,8},{6,10},{8,4},{10,6},{12,0},{14,2},{1,13},{3,15... | collective-permute-start | bytes 224264 | tf_op jit(solution)/shard_map/ppermute | solution.py:17
  126.5 5.7 %collective-permute-start.49 = (bf16[16,2336]{1,0:T(8,128)(2,1)S(1)}, bf16[16,2336]{1,0:T(8,128)(2,1)S(1)}, u32[]{:S(2)}, u32[]{:S(2)}) collective-permute-start(bf16[16,2336]{1,0:T(8,128)(2,1)S(1)} %add_convert_fusion.1), channel_id=1, source_target_pairs={{0,8},{2,10},{4,12},{6,14},{8,0},{10,2},{12,4},{14,6},{1,9},{3,11}... | collective-permute-start | bytes 224264 | tf_op jit(solution)/shard_map/ppermute | solution.py:17
  127.3 5.4 %collective-permute-start.51 = (bf16[16,2336]{1,0:T(8,128)(2,1)S(1)}, bf16[16,2336]{1,0:T(8,128)(2,1)S(1)}, u32[]{:S(2)}, u32[]{:S(2)}) collective-permute-start(bf16[16,2336]{1,0:T(8,128)(2,1)S(1)} %add_convert_fusion), channel_id=1, source_target_pairs={{0,4},{2,6},{4,0},{6,2},{8,12},{10,14},{12,8},{14,10},{1,5},{3,7},... | collective-permute-start | bytes 224264 | tf_op jit(solution)/shard_map/ppermute | solution.py:17
  (29 other events, 361.9 us)
